TPU v7x, 32 devices: a whole 2x2x4 slice. The times are simulated.
32 devices in a mesh: depth: 16 (over z, y, x), rows: 2 (over core).
Axes of the slice: x: 2, y: 2, z: 4, core: 2. Of those that a mesh axis runs over, the one named last changes fastest.
Arguments:
- substrate: float32 [64, 32, 1024], P('depth', 'rows'), may hold values from 0.2 to 1
- catalyst: float32 [64, 32, 1024], P('depth', 'rows'), may hold values from 0 to 0.5
- feed_rate: float32 [64, 32, 1024], P('depth', 'rows'), may hold values from 0.01 to 0.1
- kill_rate: float32 [64, 32, 1024], P('depth', 'rows'), may hold values from 0.03 to 0.1
- extinction: float32 [64, 32, 1024], P('depth', 'rows'), may hold values from 0.001 to 0.03
- palette: float32 [3, 3], replicated, may hold values from -2 to 2
Outputs:
- new_substrate: float32 [64, 32, 1024], P('depth', 'rows')
- new_catalyst: float32 [64, 32, 1024], P('depth', 'rows')
- image: float32 [4, 32, 1024], P(None, 'rows', 'depth')
All inputs are finite; a program needn't handle non-finite values.
Results may differ from a plain program's by a relative error of at most 0.000039.
Values sent between devices are 32-bit elements; how exact they have to be, the bound alone decides.
No kernel may reach another device: no remote copies, remote signals or barrier semaphores. Data moves between devices by JAX's collectives and lax.ppermute only.
A program may use at most 64 MiB of HBM per device.

v0:
```python
import jax
import jax.numpy as jnp
from jax import lax
from jax.sharding import PartitionSpec as P

STEPS = 2


diffusion_fast = 0.08
diffusion_slow = 0.04
time_step = 2.0


def with_halo(cells, sides, width):
    for axis, dim in sides:
        count = lax.axis_size(axis)
        ends = count - 1
        head = lax.slice_in_dim(cells, 0, width, axis=dim)
        tail = lax.slice_in_dim(cells, cells.shape[dim] - width, cells.shape[dim], axis=dim)
        cells = jnp.concatenate(
            [
                lax.ppermute(tail, axis, [(i, (i + 1) % count) for i in range(ends)]),
                cells,
                lax.ppermute(head, axis, [((i + 1) % count, i) for i in range(ends)]),
            ],
            axis=dim,
        )
    return cells


def swapped(value, axis, distance):
    mask = 2**distance
    pairs = [(source, source ^ mask) for source in range(lax.axis_size(axis))]
    return lax.ppermute(value, axis, pairs)


def react(padded, feed, kill):
    center = padded[:, 1:-1, 1:-1]
    column_pad = jnp.pad(center, ((0, 0), (0, 0), (0, 0), (1, 1)))
    laplace = (
        padded[:, 2:, 1:-1] + padded[:, :-2, 1:-1] + padded[:, 1:-1, 2:] + padded[:, 1:-1, :-2]
    )
    laplace = laplace + column_pad[..., 2:] + column_pad[..., :-2] - 6.0 * center
    fed = center[0]
    auto = center[1]
    reaction = fed * auto * auto
    fed_change = diffusion_fast * laplace[0] - reaction + feed * (1.0 - fed)
    auto_change = diffusion_slow * laplace[1] + reaction - (feed + kill) * auto
    return jnp.stack([fed + time_step * fed_change, auto + time_step * auto_change])


def advance(fields, feed, kill):
    padded = with_halo(fields, (("depth", 1), ("rows", 2)), 1)
    return react(padded, feed, kill)


def body(substrate, catalyst, feed_rate, kill_rate, extinction, palette):
    row_cells = substrate.shape[1]
    fields = jnp.stack([substrate, catalyst])
    for iteration in range(STEPS):
        fields = advance(fields, feed_rate, kill_rate)
    fed = fields[0]
    auto = fields[1]
    passing = jnp.exp(-extinction * (0.25 + 4.0 * auto * auto))
    opacity = 1.0 - passing
    colors = jax.nn.sigmoid(
        8.0 * palette[:, 0, None, None, None] * (fed - 0.65)[None]
        + 8.0 * palette[:, 1, None, None, None] * (auto - 0.25)[None]
        + palette[:, 2, None, None, None]
    )
    cumul = jnp.cumprod(passing, axis=0)
    before = jnp.concatenate([jnp.ones_like(passing[:1]), cumul[:-1]], axis=0)
    weights = before * opacity
    partial_value = jnp.stack(
        [
            jnp.sum(weights * colors[0], axis=0),
            jnp.sum(weights * colors[1], axis=0),
            jnp.sum(weights * colors[2], axis=0),
            cumul[-1],
        ]
    )
    count = lax.axis_size("depth")
    levels = count.bit_length() - 1
    columns = partial_value.shape[2]
    block = columns // count
    shaped = partial_value.reshape((4, row_cells) + (2,) * levels + (block,))
    order = (0, 1) + tuple(range(levels + 1, 1, -1)) + (levels + 2,)
    partial_value = jnp.transpose(shaped, order).reshape((4, row_cells, columns))
    position = lax.axis_index("depth")
    for level in range(levels):
        half = partial_value.shape[2] // 2
        mine_bit = position >> level & 1
        kept = lax.dynamic_slice_in_dim(partial_value, mine_bit * half, half, 2)
        given = lax.dynamic_slice_in_dim(partial_value, (1 - mine_bit) * half, half, 2)
        other = swapped(given, "depth", level)
        is_front = mine_bit == 0
        nearer = jnp.where(is_front, kept, other)
        farther = jnp.where(is_front, other, kept)
        partial_value = jnp.concatenate(
            [nearer[:3] + nearer[3:] * farther[:3], nearer[3:] * farther[3:]], axis=0
        )
    image = jnp.concatenate([partial_value[:3], 1.0 - partial_value[3:]], axis=0)
    return (fed, auto, image)


def solution(mesh):
    return jax.shard_map(
        body,
        mesh=mesh,
        in_specs=(
            P("depth", "rows", None),
            P("depth", "rows", None),
            P("depth", "rows", None),
            P("depth", "rows", None),
            P("depth", "rows", None),
            P(),
        ),
        out_specs=(P("depth", "rows", None), P("depth", "rows", None), P(None, "rows", "depth")),
        check_vma=False,
    )
```

profile of v0, /device:TPU:0, one launch (start us, length us, event | category | flops | bytes accessed | tf_op | source)
XLA Modules:
  0.0 64.0 jit_solution(6921270508977106941)
XLA Ops:
  0.6 0.0 copy-start
  0.6 0.0 copy-start.1
  0.6 1.0 %fusion.44 = (f32[2,1,16,1024]{3,2,1,0:T(8,128)S(1)}, f32[2,1,16,1024]{3,2,1,0:T(8,128)S(1)}) fusion(f32[1,4,16,1024]{3,2,1,0:T(8,128)} %bitcast.86, f32[1,4,16,1024]{3,2,1,0:T(8,128)} %bitcast.82), kind=kLoop, calls=%fused_computation.99 | loop fusion | flops 65536 | bytes 786432 | tf_op jit(solution)/shard_map/stack | solution.py:59
  1.7 1.3 %collective-permute-start = (f32[2,1,16,1024]{3,2,1,0:T(8,128)S(1)}, f32[2,1,16,1024]{3,2,1,0:T(8,128)S(1)}, u32[]{:S(2)}, u32[]{:S(2)}) collective-permute-start(f32[2,1,16,1024]{3,2,1,0:T(8,128)S(1)} %get-tuple-element.25), channel_id=1, source_target_pairs={{2,0},{4,2},{6,4},{8,6},{10,8},{12,10},{14,12},{16,14},{18,16},{20... | collective-permute-start | bytes 393224 | tf_op jit(solution)/shard_map/ppermute | solution.py:24
  3.0 5.5 %collective-permute-start.1 = (f32[2,1,16,1024]{3,2,1,0:T(8,128)S(1)}, f32[2,1,16,1024]{3,2,1,0:T(8,128)S(1)}, u32[]{:S(2)}, u32[]{:S(2)}) collective-permute-start(f32[2,1,16,1024]{3,2,1,0:T(8,128)S(1)} %get-tuple-element.24), channel_id=1, source_target_pairs={{0,2},{2,4},{4,6},{6,8},{8,10},{10,12},{12,14},{14,16},{16,18},{18... | collective-permute-start | bytes 393224 | tf_op jit(solution)/shard_map/ppermute | solution.py:22
  8.4 1.5 %collective-permute-done = f32[2,1,16,1024]{3,2,1,0:T(8,128)S(1)} collective-permute-done((f32[2,1,16,1024]{3,2,1,0:T(8,128)S(1)}, f32[2,1,16,1024]{3,2,1,0:T(8,128)S(1)}, u32[]{:S(2)}, u32[]{:S(2)}) %collective-permute-start) | collective-permute-done | bytes 131104 | tf_op jit(solution)/shard_map/ppermute | solution.py:24
  10.0 3.9 %collective-permute-done.1 = f32[2,1,16,1024]{3,2,1,0:T(8,128)S(1)} collective-permute-done((f32[2,1,16,1024]{3,2,1,0:T(8,128)S(1)}, f32[2,1,16,1024]{3,2,1,0:T(8,128)S(1)}, u32[]{:S(2)}, u32[]{:S(2)}) %collective-permute-start.1) | collective-permute-done | bytes 131104 | tf_op jit(solution)/shard_map/ppermute | solution.py:22
  13.9 0.0 copy-done
  13.9 0.0 copy-done.1
  13.9 0.1 pad_maximum_fusion.33
  14.0 1.3 %collective-permute-start.2 = (f32[2,6,1,1024]{3,2,1,0:T(1,128)S(1)}, f32[2,6,1,1024]{3,2,1,0:T(1,128)S(1)}, u32[]{:S(2)}, u32[]{:S(2)}) collective-permute-start(f32[2,6,1,1024]{3,2,1,0:T(1,128)S(1)} %get-tuple-element.20), channel_id=1, source_target_pairs={{1,0},{3,2},{5,4},{7,6},{9,8},{11,10},{13,12},{15,14},{17,16},{19,... | collective-permute-start | bytes 147464 | tf_op jit(solution)/shard_map/ppermute | solution.py:24
  15.3 3.0 %collective-permute-start.3 = (f32[2,6,1,1024]{3,2,1,0:T(1,128)S(1)}, f32[2,6,1,1024]{3,2,1,0:T(1,128)S(1)}, u32[]{:S(2)}, u32[]{:S(2)}) collective-permute-start(f32[2,6,1,1024]{3,2,1,0:T(1,128)S(1)} %get-tuple-element.21), channel_id=1, source_target_pairs={{0,1},{2,3},{4,5},{6,7},{8,9},{10,11},{12,13},{14,15},{16,17},{18,... | collective-permute-start | bytes 147464 | tf_op jit(solution)/shard_map/ppermute | solution.py:22
  18.4 0.0 copy-start.3
  18.4 0.0 copy-start.6
  18.4 0.0 collective-permute-done.2
  18.4 0.8 %collective-permute-done.3 = f32[2,6,1,1024]{3,2,1,0:T(1,128)S(1)} collective-permute-done((f32[2,6,1,1024]{3,2,1,0:T(1,128)S(1)}, f32[2,6,1,1024]{3,2,1,0:T(1,128)S(1)}, u32[]{:S(2)}, u32[]{:S(2)}) %collective-permute-start.3) | collective-permute-done | bytes 49184 | tf_op jit(solution)/shard_map/ppermute | solution.py:22
  19.2 0.4 fusion.2
  19.6 0.0 copy-done.3
  19.6 0.0 copy-done.6
  19.6 0.2 fusion.35
  19.8 1.3 %collective-permute-start.4 = (f32[2,1,16,1024]{3,2,1,0:T(8,128)S(1)}, f32[2,1,16,1024]{3,2,1,0:T(8,128)S(1)}, u32[]{:S(2)}, u32[]{:S(2)}) collective-permute-start(f32[2,1,16,1024]{3,2,1,0:T(8,128)S(1)} %get-tuple-element.23), channel_id=1, source_target_pairs={{2,0},{4,2},{6,4},{8,6},{10,8},{12,10},{14,12},{16,14},{18,16},{20... | collective-permute-start | bytes 393224 | tf_op jit(solution)/shard_map/ppermute | solution.py:24
  21.1 5.0 %collective-permute-start.5 = (f32[2,1,16,1024]{3,2,1,0:T(8,128)S(1)}, f32[2,1,16,1024]{3,2,1,0:T(8,128)S(1)}, u32[]{:S(2)}, u32[]{:S(2)}) collective-permute-start(f32[2,1,16,1024]{3,2,1,0:T(8,128)S(1)} %get-tuple-element.22), channel_id=1, source_target_pairs={{0,2},{2,4},{4,6},{6,8},{8,10},{10,12},{12,14},{14,16},{16,18},{18... | collective-permute-start | bytes 393224 | tf_op jit(solution)/shard_map/ppermute | solution.py:22
  26.2 0.0 copy-start.7
  26.2 0.7 %copy-done.7 = f32[3,3]{1,0:T(4,128)S(1)} copy-done((f32[3,3]{1,0:T(4,128)S(1)}, f32[3,3]{1,0:T(4,128)}, u32[]{:S(2)}) %copy-start.7) | copy-done | bytes 60
  26.8 0.2 multiply_reduce_fusion.1
  27.0 1.2 %collective-permute-done.4 = f32[2,1,16,1024]{3,2,1,0:T(8,128)S(1)} collective-permute-done((f32[2,1,16,1024]{3,2,1,0:T(8,128)S(1)}, f32[2,1,16,1024]{3,2,1,0:T(8,128)S(1)}, u32[]{:S(2)}, u32[]{:S(2)}) %collective-permute-start.4) | collective-permute-done | bytes 131104 | tf_op jit(solution)/shard_map/ppermute | solution.py:24
  28.2 3.0 %collective-permute-done.5 = f32[2,1,16,1024]{3,2,1,0:T(8,128)S(1)} collective-permute-done((f32[2,1,16,1024]{3,2,1,0:T(8,128)S(1)}, f32[2,1,16,1024]{3,2,1,0:T(8,128)S(1)}, u32[]{:S(2)}, u32[]{:S(2)}) %collective-permute-start.5) | collective-permute-done | bytes 131104 | tf_op jit(solution)/shard_map/ppermute | solution.py:22
  31.2 0.1 pad_maximum_fusion.29
  31.3 1.3 %collective-permute-start.6 = (f32[2,6,1,1024]{3,2,1,0:T(1,128)S(1)}, f32[2,6,1,1024]{3,2,1,0:T(1,128)S(1)}, u32[]{:S(2)}, u32[]{:S(2)}) collective-permute-start(f32[2,6,1,1024]{3,2,1,0:T(1,128)S(1)} %get-tuple-element.18), channel_id=1, source_target_pairs={{1,0},{3,2},{5,4},{7,6},{9,8},{11,10},{13,12},{15,14},{17,16},{19,... | collective-permute-start | bytes 147464 | tf_op jit(solution)/shard_map/ppermute | solution.py:24
  32.6 3.0 %collective-permute-start.7 = (f32[2,6,1,1024]{3,2,1,0:T(1,128)S(1)}, f32[2,6,1,1024]{3,2,1,0:T(1,128)S(1)}, u32[]{:S(2)}, u32[]{:S(2)}) collective-permute-start(f32[2,6,1,1024]{3,2,1,0:T(1,128)S(1)} %get-tuple-element.19), channel_id=1, source_target_pairs={{0,1},{2,3},{4,5},{6,7},{8,9},{10,11},{12,13},{14,15},{16,17},{18,... | collective-permute-start | bytes 147464 | tf_op jit(solution)/shard_map/ppermute | solution.py:22
  35.7 0.0 collective-permute-done.6
  35.7 0.8 %collective-permute-done.7 = f32[2,6,1,1024]{3,2,1,0:T(1,128)S(1)} collective-permute-done((f32[2,6,1,1024]{3,2,1,0:T(1,128)S(1)}, f32[2,6,1,1024]{3,2,1,0:T(1,128)S(1)}, u32[]{:S(2)}, u32[]{:S(2)}) %collective-permute-start.7) | collective-permute-done | bytes 49184 | tf_op jit(solution)/shard_map/ppermute | solution.py:22
  36.5 0.4 fusion.5
  36.9 0.0 copy-start.5
  37.0 0.9 %broadcast_add_fusion = (f32[4,16,1024]{2,1,0:T(8,128)S(1)}, f32[4,16,1024]{2,1,0:T(8,128)S(1)}, f32[4,16,1024]{2,1,0:T(8,128)S(1)}, f32[4,16,1024]{2,1,0:T(8,128)}) fusion(f32[4,16,1024]{2,1,0:T(8,128)S(1)} %get-tuple-element.13, f32[4,16,1024]{2,1,0:T(8,128)S(1)} %get-tuple-element.14, f32[4,16,1024]{2,1,0:T(8,128)S(1)} %get-tuple-element.15, ...), kind=kLoop, calls=%fused_computation.100 | loop fusion | flops 1114112 | bytes 2621440 | tf_op jit(solution)/shard_map/sub | solution.py:68
  37.8 0.0 copy-start.2
  37.8 0.0 copy-done.5
  37.9 0.3 fusion.49
  38.2 0.0 copy-start.4
  38.2 0.7 %copy-done.4 = f32[4,16,1024]{2,1,0:T(8,128)} copy-done((f32[4,16,1024]{2,1,0:T(8,128)}, f32[4,16,1024]{2,1,0:T(8,128)S(1)}, u32[]{:S(2)}) %copy-start.4) | copy-done | bytes 262168
  38.8 0.3 add_divide_fusion
  39.1 0.0 copy-done.2
  39.1 0.6 slice-done
  39.8 0.1 fusion.20
  39.9 0.1 stack.38
  40.0 0.1 stack.39
  40.2 0.0 slice-start.1
  40.2 0.1 stack.40
  40.3 0.7 %slice-done.1 = f32[1,16,1024]{2,1,0:T(8,128)S(1)} async-done(((f32[4,16,1024]{2,1,0:T(8,128)}), f32[1,16,1024]{2,1,0:T(8,128)S(1)}, s32[]{:S(2)}) %slice-start.1) | async-done | bytes 65560 | tf_op jit(solution)/shard_map/slice | solution.py:79
  41.0 0.1 stack.41
  41.1 0.3 maximum_bitcast_fusion
  41.4 0.3 copy.10
  41.7 0.5 reshape.46
  42.2 2.5 %collective-permute-start.8 = (f32[4,16,512]{2,1,0:T(8,128)S(1)}, f32[4,16,512]{2,1,0:T(8,128)S(1)}, u32[]{:S(2)}, u32[]{:S(2)}) collective-permute-start(f32[4,16,512]{2,1,0:T(8,128)S(1)} %constant_dynamic-slice_fusion), channel_id=1, source_target_pairs={{0,2},{2,0},{4,6},{6,4},{8,10},{10,8},{12,14},{14,12},{16,18},{18,... | collective-permute-start | bytes 393224 | tf_op jit(solution)/shard_map/ppermute | solution.py:34
  44.7 4.0 %collective-permute-done.8 = f32[4,16,512]{2,1,0:T(8,128)S(1)} collective-permute-done((f32[4,16,512]{2,1,0:T(8,128)S(1)}, f32[4,16,512]{2,1,0:T(8,128)S(1)}, u32[]{:S(2)}, u32[]{:S(2)}) %collective-permute-start.8) | collective-permute-done | bytes 131104 | tf_op jit(solution)/shard_map/ppermute | solution.py:34
  48.8 2.1 %collective-permute-start.9 = (f32[4,16,256]{2,1,0:T(8,128)S(1)}, f32[4,16,256]{2,1,0:T(8,128)S(1)}, u32[]{:S(2)}, u32[]{:S(2)}) collective-permute-start(f32[4,16,256]{2,1,0:T(8,128)S(1)} %fusion.46), channel_id=1, source_target_pairs={{0,4},{2,6},{4,0},{6,2},{8,12},{10,14},{12,8},{14,10},{16,20},{18,... | collective-permute-start | bytes 196616 | tf_op jit(solution)/shard_map/ppermute | solution.py:34
  50.9 2.3 %collective-permute-done.9 = f32[4,16,256]{2,1,0:T(8,128)S(1)} collective-permute-done((f32[4,16,256]{2,1,0:T(8,128)S(1)}, f32[4,16,256]{2,1,0:T(8,128)S(1)}, u32[]{:S(2)}, u32[]{:S(2)}) %collective-permute-start.9) | collective-permute-done | bytes 65568 | tf_op jit(solution)/shard_map/ppermute | solution.py:34
  53.2 3.0 %collective-permute-start.10 = (f32[4,16,128]{2,1,0:T(8,128)S(1)}, f32[4,16,128]{2,1,0:T(8,128)S(1)}, u32[]{:S(2)}, u32[]{:S(2)}) collective-permute-start(f32[4,16,128]{2,1,0:T(8,128)S(1)} %fusion.53), channel_id=1, source_target_pairs={{0,8},{2,10},{4,12},{6,14},{8,0},{10,2},{12,4},{14,6},{16,24},{18,... | collective-permute-start | bytes 98312 | tf_op jit(solution)/shard_map/ppermute | solution.py:34
  56.2 1.9 %collective-permute-done.10 = f32[4,16,128]{2,1,0:T(8,128)S(1)} collective-permute-done((f32[4,16,128]{2,1,0:T(8,128)S(1)}, f32[4,16,128]{2,1,0:T(8,128)S(1)}, u32[]{:S(2)}, u32[]{:S(2)}) %collective-permute-start.10) | collective-permute-done | bytes 32800 | tf_op jit(solution)/shard_map/ppermute | solution.py:34
  58.2 0.1 fusion.51
  58.2 3.2 %collective-permute-start.11 = (f32[4,16,64]{2,1,0:T(8,128)S(1)}, f32[4,16,64]{2,1,0:T(8,128)S(1)}, u32[]{:S(2)}, u32[]{:S(2)}) collective-permute-start(f32[4,16,64]{2,1,0:T(8,128)S(1)} %fusion.51), channel_id=1, source_target_pairs={{0,16},{2,18},{4,20},{6,22},{8,24},{10,26},{12,28},{14,30},{16,0},... | collective-permute-start | bytes 49160 | tf_op jit(solution)/shard_map/ppermute | solution.py:34
  61.4 1.9 %collective-permute-done.11 = f32[4,16,64]{2,1,0:T(8,128)S(1)} collective-permute-done((f32[4,16,64]{2,1,0:T(8,128)S(1)}, f32[4,16,64]{2,1,0:T(8,128)S(1)}, u32[]{:S(2)}, u32[]{:S(2)}) %collective-permute-start.11) | collective-permute-done | bytes 16416 | tf_op jit(solution)/shard_map/ppermute | solution.py:34
  63.3 0.1 broadcast_select_fusion.5
  63.4 0.6 pad_maximum_fusion.34
  (18 shorter events, 0.3 us)
Async XLA Ops:
  0.6 13.3 %copy-start = (f32[4,16,1024]{2,1,0:T(8,128)S(1)}, f32[4,16,1024]{2,1,0:T(8,128)}, u32[]{:S(2)}) copy-start(f32[4,16,1024]{2,1,0:T(8,128)} %param.7) | copy-start | bytes 786436
  0.6 13.3 %copy-start.1 = (f32[4,16,1024]{2,1,0:T(8,128)S(1)}, f32[4,16,1024]{2,1,0:T(8,128)}, u32[]{:S(2)}) copy-start(f32[4,16,1024]{2,1,0:T(8,128)} %param.6) | copy-start | bytes 786436
  1.7 8.3 %collective-permute-start = (f32[2,1,16,1024]{3,2,1,0:T(8,128)S(1)}, f32[2,1,16,1024]{3,2,1,0:T(8,128)S(1)}, u32[]{:S(2)}, u32[]{:S(2)}) collective-permute-start(f32[2,1,16,1024]{3,2,1,0:T(8,128)S(1)} %get-tuple-element.25), channel_id=1, source_target_pairs={{2,0},{4,2},{6,4},{8,6},{10,8},{12,10},{14,12},{16,14},{18,16},{20... | collective-permute-start | bytes 393224 | tf_op jit(solution)/shard_map/ppermute | solution.py:24
  3.0 11.0 %collective-permute-start.1 = (f32[2,1,16,1024]{3,2,1,0:T(8,128)S(1)}, f32[2,1,16,1024]{3,2,1,0:T(8,128)S(1)}, u32[]{:S(2)}, u32[]{:S(2)}) collective-permute-start(f32[2,1,16,1024]{3,2,1,0:T(8,128)S(1)} %get-tuple-element.24), channel_id=1, source_target_pairs={{0,2},{2,4},{4,6},{6,8},{8,10},{10,12},{12,14},{14,16},{16,18},{18... | collective-permute-start | bytes 393224 | tf_op jit(solution)/shard_map/ppermute | solution.py:22
  14.0 4.4 %collective-permute-start.2 = (f32[2,6,1,1024]{3,2,1,0:T(1,128)S(1)}, f32[2,6,1,1024]{3,2,1,0:T(1,128)S(1)}, u32[]{:S(2)}, u32[]{:S(2)}) collective-permute-start(f32[2,6,1,1024]{3,2,1,0:T(1,128)S(1)} %get-tuple-element.20), channel_id=1, source_target_pairs={{1,0},{3,2},{5,4},{7,6},{9,8},{11,10},{13,12},{15,14},{17,16},{19,... | collective-permute-start | bytes 147464 | tf_op jit(solution)/shard_map/ppermute | solution.py:24
  15.3 3.9 %collective-permute-start.3 = (f32[2,6,1,1024]{3,2,1,0:T(1,128)S(1)}, f32[2,6,1,1024]{3,2,1,0:T(1,128)S(1)}, u32[]{:S(2)}, u32[]{:S(2)}) collective-permute-start(f32[2,6,1,1024]{3,2,1,0:T(1,128)S(1)} %get-tuple-element.21), channel_id=1, source_target_pairs={{0,1},{2,3},{4,5},{6,7},{8,9},{10,11},{12,13},{14,15},{16,17},{18,... | collective-permute-start | bytes 147464 | tf_op jit(solution)/shard_map/ppermute | solution.py:22
  18.4 1.2 %copy-start.3 = (f32[4,16,1024]{2,1,0:T(8,128)S(1)}, f32[4,16,1024]{2,1,0:T(8,128)}, u32[]{:S(2)}) copy-start(f32[4,16,1024]{2,1,0:T(8,128)} %param.8) | copy-start | bytes 786436
  18.4 1.2 %copy-start.6 = (f32[4,16,1024]{2,1,0:T(8,128)S(1)}, f32[4,16,1024]{2,1,0:T(8,128)}, u32[]{:S(2)}) copy-start(f32[4,16,1024]{2,1,0:T(8,128)} %param.9) | copy-start | bytes 786436
  19.8 8.4 %collective-permute-start.4 = (f32[2,1,16,1024]{3,2,1,0:T(8,128)S(1)}, f32[2,1,16,1024]{3,2,1,0:T(8,128)S(1)}, u32[]{:S(2)}, u32[]{:S(2)}) collective-permute-start(f32[2,1,16,1024]{3,2,1,0:T(8,128)S(1)} %get-tuple-element.23), channel_id=1, source_target_pairs={{2,0},{4,2},{6,4},{8,6},{10,8},{12,10},{14,12},{16,14},{18,16},{20... | collective-permute-start | bytes 393224 | tf_op jit(solution)/shard_map/ppermute | solution.py:24
  21.1 10.1 %collective-permute-start.5 = (f32[2,1,16,1024]{3,2,1,0:T(8,128)S(1)}, f32[2,1,16,1024]{3,2,1,0:T(8,128)S(1)}, u32[]{:S(2)}, u32[]{:S(2)}) collective-permute-start(f32[2,1,16,1024]{3,2,1,0:T(8,128)S(1)} %get-tuple-element.22), channel_id=1, source_target_pairs={{0,2},{2,4},{4,6},{6,8},{8,10},{10,12},{12,14},{14,16},{16,18},{18... | collective-permute-start | bytes 393224 | tf_op jit(solution)/shard_map/ppermute | solution.py:22
  26.2 0.7 %copy-start.7 = (f32[3,3]{1,0:T(4,128)S(1)}, f32[3,3]{1,0:T(4,128)}, u32[]{:S(2)}) copy-start(f32[3,3]{1,0:T(4,128)} %param.11) | copy-start | bytes 112
  31.3 4.4 %collective-permute-start.6 = (f32[2,6,1,1024]{3,2,1,0:T(1,128)S(1)}, f32[2,6,1,1024]{3,2,1,0:T(1,128)S(1)}, u32[]{:S(2)}, u32[]{:S(2)}) collective-permute-start(f32[2,6,1,1024]{3,2,1,0:T(1,128)S(1)} %get-tuple-element.18), channel_id=1, source_target_pairs={{1,0},{3,2},{5,4},{7,6},{9,8},{11,10},{13,12},{15,14},{17,16},{19,... | collective-permute-start | bytes 147464 | tf_op jit(solution)/shard_map/ppermute | solution.py:24
  32.6 3.9 %collective-permute-start.7 = (f32[2,6,1,1024]{3,2,1,0:T(1,128)S(1)}, f32[2,6,1,1024]{3,2,1,0:T(1,128)S(1)}, u32[]{:S(2)}, u32[]{:S(2)}) collective-permute-start(f32[2,6,1,1024]{3,2,1,0:T(1,128)S(1)} %get-tuple-element.19), channel_id=1, source_target_pairs={{0,1},{2,3},{4,5},{6,7},{8,9},{10,11},{12,13},{14,15},{16,17},{18,... | collective-permute-start | bytes 147464 | tf_op jit(solution)/shard_map/ppermute | solution.py:22
  36.9 1.0 %copy-start.5 = (f32[4,16,1024]{2,1,0:T(8,128)S(1)}, f32[4,16,1024]{2,1,0:T(8,128)}, u32[]{:S(2)}) copy-start(f32[4,16,1024]{2,1,0:T(8,128)} %param.10) | copy-start | bytes 786436
  37.8 1.3 %copy-start.2 = (f32[4,16,1024]{2,1,0:T(8,128)}, f32[4,16,1024]{2,1,0:T(8,128)S(1)}, u32[]{:S(2)}) copy-start(f32[4,16,1024]{2,1,0:T(8,128)S(1)} %get-tuple-element.12) | copy-start | bytes 786436
  38.2 0.7 %copy-start.4 = (f32[4,16,1024]{2,1,0:T(8,128)}, f32[4,16,1024]{2,1,0:T(8,128)S(1)}, u32[]{:S(2)}) copy-start(f32[4,16,1024]{2,1,0:T(8,128)S(1)} %fusion.49) | copy-start | bytes 786436
  38.8 0.9 %slice-start = ((f32[4,16,1024]{2,1,0:T(8,128)}), f32[3,16,1024]{2,1,0:T(8,128)S(1)}, s32[]{:S(2)}) async-start(f32[4,16,1024]{2,1,0:T(8,128)} %copy-done.4), calls=%async_computation | async-start | bytes 393216 | tf_op jit(solution)/shard_map/slice | solution.py:72
  40.2 0.8 %slice-start.1 = ((f32[4,16,1024]{2,1,0:T(8,128)}), f32[1,16,1024]{2,1,0:T(8,128)S(1)}, s32[]{:S(2)}) async-start(f32[4,16,1024]{2,1,0:T(8,128)} %copy-done.4), calls=%async_computation.1 | async-start | bytes 131072 | tf_op jit(solution)/shard_map/slice | solution.py:79
  42.2 6.5 %collective-permute-start.8 = (f32[4,16,512]{2,1,0:T(8,128)S(1)}, f32[4,16,512]{2,1,0:T(8,128)S(1)}, u32[]{:S(2)}, u32[]{:S(2)}) collective-permute-start(f32[4,16,512]{2,1,0:T(8,128)S(1)} %constant_dynamic-slice_fusion), channel_id=1, source_target_pairs={{0,2},{2,0},{4,6},{6,4},{8,10},{10,8},{12,14},{14,12},{16,18},{18,... | collective-permute-start | bytes 393224 | tf_op jit(solution)/shard_map/ppermute | solution.py:34
  48.8 4.3 %collective-permute-start.9 = (f32[4,16,256]{2,1,0:T(8,128)S(1)}, f32[4,16,256]{2,1,0:T(8,128)S(1)}, u32[]{:S(2)}, u32[]{:S(2)}) collective-permute-start(f32[4,16,256]{2,1,0:T(8,128)S(1)} %fusion.46), channel_id=1, source_target_pairs={{0,4},{2,6},{4,0},{6,2},{8,12},{10,14},{12,8},{14,10},{16,20},{18,... | collective-permute-start | bytes 196616 | tf_op jit(solution)/shard_map/ppermute | solution.py:34
  53.2 4.9 %collective-permute-start.10 = (f32[4,16,128]{2,1,0:T(8,128)S(1)}, f32[4,16,128]{2,1,0:T(8,128)S(1)}, u32[]{:S(2)}, u32[]{:S(2)}) collective-permute-start(f32[4,16,128]{2,1,0:T(8,128)S(1)} %fusion.53), channel_id=1, source_target_pairs={{0,8},{2,10},{4,12},{6,14},{8,0},{10,2},{12,4},{14,6},{16,24},{18,... | collective-permute-start | bytes 98312 | tf_op jit(solution)/shard_map/ppermute | solution.py:34
  58.2 5.1 %collective-permute-start.11 = (f32[4,16,64]{2,1,0:T(8,128)S(1)}, f32[4,16,64]{2,1,0:T(8,128)S(1)}, u32[]{:S(2)}, u32[]{:S(2)}) collective-permute-start(f32[4,16,64]{2,1,0:T(8,128)S(1)} %fusion.51), channel_id=1, source_target_pairs={{0,16},{2,18},{4,20},{6,22},{8,24},{10,26},{12,28},{14,30},{16,0},... | collective-permute-start | bytes 49160 | tf_op jit(solution)/shard_map/ppermute | solution.py:34
where the time goes:
time: 64.5 us; the launch traced here: 64 us
  starting transfers between devices  32.5 us (50%)
  waiting for transfers between devices  21.3 us (33%)
  other arithmetic  5.19 us (8%)
  local copies, waits for them, and re-layouts  4.03 us (6%)
  between operations  1.01 us (2%)
    ppermute x4, starting transfers between devices, with_halo(): lax.ppermute(tail, axis, [(i, (i + 1) % count) for i in range(ends)])  16.6 us
    ppermute x4, starting transfers between devices, swapped(): return lax.ppermute(value, axis, pairs)  10.8 us
    ppermute x4, waiting for transfers between devices, swapped(): return lax.ppermute(value, axis, pairs)  10.1 us
    ppermute x4, waiting for transfers between devices, with_halo(): lax.ppermute(tail, axis, [(i, (i + 1) % count) for i in range(ends)])  8.51 us
    ppermute x4, starting transfers between devices, with_halo(): lax.ppermute(head, axis, [((i + 1) % count, i) for i in range(ends)])  5.17 us
    ppermute x4, waiting for transfers between devices, with_halo(): lax.ppermute(head, axis, [((i + 1) % count, i) for i in range(ends)])  2.74 us
    unnamed x16, local copies, waits for them, and re-layouts  1.44 us
  transfers between devices with their start and end apart: 12, of which 10 were waited for; matrix products, arithmetic and copies ran while one was open for 0% of the time, Pallas kernels for 0%

commit v1 on v0

v1 whole, which is shorter than its diff:
```python
import functools

import jax
import jax.numpy as jnp
from jax import lax
from jax.experimental import pallas as pl
from jax.experimental.pallas import tpu as pltpu
from jax.sharding import PartitionSpec as P

diffusion_fast = 0.08
diffusion_slow = 0.04
time_step = 2.0
reach_fast = time_step * diffusion_fast
reach_slow = time_step * diffusion_slow
LANES = 128
SUBLANES = 8
VMEM = pl.BlockSpec(memory_space=pltpu.VMEM)
SMEM = pl.BlockSpec(memory_space=pltpu.SMEM)
PARAMS = pltpu.CompilerParams(vmem_limit_bytes=24 * 1024 * 1024)


def pairings(axis, other):
    count, width = lax.axis_size(axis), lax.axis_size(other)
    flat = (lambda i, j: i * width + j) if axis == "depth" else (lambda i, j: j * count + i)
    result = []
    for shift in (0, 1):
        pairs = []
        for i in range(count):
            partner = ((i + shift) ^ 1) - shift
            for j in range(width):
                if 0 <= partner < count:
                    pairs.append((flat(i, j), flat(partner, j)))
                elif j ^ 1 < width:
                    pairs.append((flat(i, j), flat(i, j ^ 1)))
        result.append(pairs if count > 2 or shift == 0 else None)
    return result


def paired(value, pairs):
    return lax.ppermute(value, ("depth", "rows"), pairs)


def is_even(axis):
    return lax.rem(lax.axis_index(axis), 2) == 0


def shifted_columns(value):
    width = value.shape[-1]
    column = lax.broadcasted_iota(jnp.int32, value.shape, value.ndim - 1)
    left = jnp.where(column == 0, 0.0, pltpu.roll(value, 1, value.ndim - 1))
    right = jnp.where(column == width - 1, 0.0, pltpu.roll(value, width - 1, value.ndim - 1))
    return left + right


def shifted_rows(value, above, below):
    rows = value.shape[0]
    row = lax.broadcasted_iota(jnp.int32, value.shape, 0)
    upper = jnp.where(row == 0, above, pltpu.roll(value, 1, 0))
    lower = jnp.where(row == rows - 1, below, pltpu.roll(value, rows - 1, 0))
    return upper + lower


def react(fed, auto, fed_near, auto_near, feed, kill):
    reaction = fed * auto * auto
    fed_change = diffusion_fast * (fed_near - 6.0 * fed) - reaction + feed * (1.0 - fed)
    auto_change = diffusion_slow * (auto_near - 6.0 * auto) + reaction - (feed + kill) * auto
    return fed + time_step * fed_change, auto + time_step * auto_change


def first_kernel(s_ref, c_ref, f_ref, k_ref, ps_ref, pc_ref, a_ref, b_ref, *row_refs):
    depth, rows, _ = s_ref.shape
    for layer in range(depth):
        near = []
        for ref in (s_ref, c_ref):
            value = ref[layer]
            total = shifted_rows(value, 0.0, 0.0) + shifted_columns(value)
            if layer > 0:
                total = total + ref[layer - 1]
            if layer < depth - 1:
                total = total + ref[layer + 1]
            near.append(total)
        ps_ref[layer], pc_ref[layer] = react(
            s_ref[layer], c_ref[layer], near[0], near[1], f_ref[layer], k_ref[layer]
        )
    fields = (s_ref, c_ref, ps_ref, pc_ref)
    even = is_even("depth")
    for out, towards_next in ((a_ref, even), (b_ref, jnp.logical_not(even))):
        layer = jnp.where(towards_next, depth - 1, 0)
        for n, ref in enumerate(fields):
            out[n] = ref[layer]
    even = is_even("rows")
    for out, towards_next in zip(row_refs, (even, jnp.logical_not(even))):
        for n, ref in enumerate(fields):
            for layer in range(depth):
                head, tail = ref[layer, 0:1], ref[layer, rows - 1 : rows]
                out[n * depth + layer : n * depth + layer + 1] = jnp.where(towards_next, tail, head)


def sides(axis, refs, read):
    index, count = lax.axis_index(axis), lax.axis_size(axis)
    even = is_even(axis)
    first = read(refs[0])
    second = read(refs[1]) if len(refs) == 2 else 0.0
    before = jnp.where(even, second, first)
    after = jnp.where(even, first, second)
    return jnp.where(index == 0, 0.0, before), jnp.where(index == count - 1, 0.0, after)


def corner_kernel(depth, *refs):
    half = len(refs) - 2
    a_ref, b_ref = refs[half:]
    even = is_even("depth")
    for out, towards_next in ((a_ref, even), (b_ref, jnp.logical_not(even))):
        for n in range(2):
            ends = []
            for layer in (0, depth - 1):
                at = n * depth + layer
                ends.append(sides("rows", refs[:half], lambda ref: ref[at : at + 1]))
            for side in range(2):
                at = 2 * n + side
                out[at : at + 1] = jnp.where(towards_next, ends[1][side], ends[0][side])


def second_kernel(depth_count, row_pairings, *refs):
    s_ref, c_ref, f_ref, k_ref, e_ref, palette, ps_ref, pc_ref = refs[:8]
    far = refs[8:10]
    corners = refs[10:12]
    beside = refs[12 : 12 + row_pairings]
    fed_out, auto_out, part_ref = refs[12 + row_pairings : 15 + row_pairings]
    depth, rows, columns = s_ref.shape
    row = lax.broadcasted_iota(jnp.int32, (rows, columns), 0)

    def with_rows(value, above, below):
        return value + jnp.where(row == 0, above, 0.0) + jnp.where(row == rows - 1, below, 0.0)

    steps = []
    for n, (old, partial, reach) in enumerate(
        ((s_ref, ps_ref, reach_fast), (c_ref, pc_ref, reach_slow))
    ):
        old_far = sides("depth", far, lambda ref: ref[n])
        new_far = sides("depth", far, lambda ref: ref[2 + n])
        corner_rows = [sides("depth", corners, lambda ref: ref[2 * n + side : 2 * n + side + 1]) for side in range(2)]
        corner = [[corner_rows[side][end] for side in range(2)] for end in range(2)]
        old_rows, new_rows = [], []
        for layer in range(depth):
            at = n * depth + layer
            old_rows.append(sides("rows", beside, lambda ref: ref[at : at + 1]))
            at = (2 + n) * depth + layer
            new_rows.append(sides("rows", beside, lambda ref: ref[at : at + 1]))
        edge = (lax.axis_index("depth") > 0, lax.axis_index("depth") < depth_count - 1)
        row_edge = (
            lax.axis_index("rows") > 0,
            lax.axis_index("rows") < lax.axis_size("rows") - 1,
        )
        fields = []
        for layer in range(-1, depth + 1):
            if layer in (-1, depth):
                end = 0 if layer < 0 else 1
                own = old[0 if layer < 0 else depth - 1]
                near = with_rows(own, corner[end][0], corner[end][1])
                fields.append(jnp.where(edge[end], new_far[end] + reach * near, 0.0))
                continue
            near = jnp.where(row == 0, old_rows[layer][0], 0.0) + jnp.where(
                row == rows - 1, old_rows[layer][1], 0.0
            )
            if layer == 0:
                near = near + old_far[0]
            if layer == depth - 1:
                near = near + old_far[1]
            fields.append(partial[layer] + reach * near)
        outside = []
        for layer in range(depth):
            ends = []
            for side in range(2):
                near = old[layer, 0:1] if side == 0 else old[layer, rows - 1 : rows]
                if layer == 0:
                    near = near + corner[0][side]
                if layer == depth - 1:
                    near = near + corner[1][side]
                ends.append(jnp.where(row_edge[side], new_rows[layer][side] + reach * near, 0.0))
            outside.append(ends)
        steps.append((fields, outside))

    gather = [0.0, 0.0, 0.0, 0.0]
    before = None
    for layer in range(depth):
        near = []
        for fields, outside in steps:
            value = fields[layer + 1]
            near.append(
                shifted_rows(value, outside[layer][0], outside[layer][1])
                + shifted_columns(value)
                + (fields[layer] + fields[layer + 2])
            )
        fed, auto = react(
            steps[0][0][layer + 1], steps[1][0][layer + 1], near[0], near[1], f_ref[layer], k_ref[layer]
        )
        fed_out[layer] = fed
        auto_out[layer] = auto
        passing = jnp.exp(-e_ref[layer] * (0.25 + 4.0 * auto * auto))
        opacity = 1.0 - passing
        weight = opacity if before is None else before * opacity
        before = passing if before is None else before * passing
        for channel in range(3):
            level = (
                (8.0 * palette[channel, 0]) * (fed - 0.65)
                + (8.0 * palette[channel, 1]) * (auto - 0.25)
                + palette[channel, 2]
            )
            gather[channel] = gather[channel] + weight / (1.0 + jnp.exp(-level))
        gather[3] = gather[3] + weight

    block = columns // depth_count
    group = packing(rows, block)
    if not group:
        for channel in range(4):
            part_ref[channel] = gather[channel]
        return
    high = rows // group
    lane = lax.broadcasted_iota(jnp.int32, (high, LANES), 1) // block
    for channel in range(4):
        for tile in range(columns // LANES):
            pieces = [
                gather[channel][q * high : (q + 1) * high, tile * LANES : (tile + 1) * LANES]
                for q in range(group)
            ]
            for p in range(group):
                packed = None
                for q in range(group):
                    turn = (q - p) * block % LANES
                    piece = pltpu.roll(pieces[q], turn, 1) if turn else pieces[q]
                    packed = piece if packed is None else jnp.where(lane == q, piece, packed)
                part_ref[tile * group + p, channel * high : (channel + 1) * high] = packed


def packing(rows, block):
    if block >= LANES or LANES % block:
        return 0
    group = LANES // block
    return group if rows % (group * SUBLANES) == 0 else 0


def last_kernel(group, part_ref, image_ref):
    _, rows, block = image_ref.shape
    high = rows // group
    count = part_ref.shape[0]
    total = [part_ref[0, channel * high : (channel + 1) * high] for channel in range(4)]
    before = 1.0 - total[3]
    for n in range(1, count):
        for channel in range(4):
            piece = part_ref[n, channel * high : (channel + 1) * high]
            total[channel] = total[channel] + before * piece
        if n < count - 1:
            before = before * (1.0 - piece)
    for channel in range(4):
        for q in range(group):
            image_ref[channel, q * high : (q + 1) * high] = total[channel][:, q * block : (q + 1) * block]


def body(substrate, catalyst, feed_rate, kill_rate, extinction, palette):
    depth, rows, columns = substrate.shape
    count = lax.axis_size("depth")
    f32 = functools.partial(jax.ShapeDtypeStruct, dtype=jnp.float32)
    whole = f32(substrate.shape)
    along_depth = pairings("depth", "rows")
    if along_depth[1] is None:
        along_depth[1] = along_depth[0]
    along_rows = [pairs for pairs in pairings("rows", "depth") if pairs is not None]

    beam = f32((4, rows, columns))
    strip = f32((4 * depth, columns))
    outs = pl.pallas_call(
        first_kernel,
        out_shape=(whole, whole, beam, beam) + (strip,) * len(along_rows),
        in_specs=[VMEM] * 4,
        out_specs=(VMEM,) * (4 + len(along_rows)),
        compiler_params=PARAMS,
        name="first_step",
    )(substrate, catalyst, feed_rate, kill_rate)
    step_fed, step_auto, *beams = outs[:4]
    far = [paired(value, pairs) for value, pairs in zip(beams, along_depth)]
    beside = [paired(value, pairs) for value, pairs in zip(outs[4:], along_rows)]
    corner = f32((SUBLANES, columns))
    corners = pl.pallas_call(
        functools.partial(corner_kernel, depth),
        out_shape=(corner, corner),
        in_specs=[VMEM] * len(beside),
        out_specs=(VMEM, VMEM),
        compiler_params=PARAMS,
        name="corner_rows",
    )(*beside)
    corners = [paired(value, pairs) for value, pairs in zip(corners, along_depth)]

    block = columns // count
    group = packing(rows, block)
    part = f32((count, 4 * rows // group, LANES) if group else (4, rows, columns))
    fed, auto, part = pl.pallas_call(
        functools.partial(second_kernel, count, len(beside)),
        out_shape=(whole, whole, part),
        in_specs=[VMEM] * 5 + [SMEM] + [VMEM] * (6 + len(beside)),
        out_specs=(VMEM,) * 3,
        compiler_params=PARAMS,
        name="second_step",
    )(substrate, catalyst, feed_rate, kill_rate, extinction, palette, step_fed, step_auto, *far, *corners, *beside)
    if not group:
        part = jnp.transpose(part.reshape(4 * rows, count, block), (1, 0, 2))
    part = lax.all_to_all(part, "depth", 0, 0)
    image = pl.pallas_call(
        functools.partial(last_kernel, group or 1),
        out_shape=f32((4, rows, block)),
        in_specs=[VMEM],
        out_specs=VMEM,
        compiler_params=PARAMS,
        name="front_to_back",
    )(part)
    return fed, auto, image


def solution(mesh):
    cells = P("depth", "rows", None)
    return jax.shard_map(
        body,
        mesh=mesh,
        in_specs=(cells,) * 5 + (P(),),
        out_specs=(cells, cells, P(None, "rows", "depth")),
        check_vma=False,
    )
```

time: 64.5 us -> 40.3 us (0.62)
  starting transfers between devices: 32.5 us -> 6.19 us
  blocking collectives: 0 us -> 16.2 us
  waiting for transfers between devices: 21.3 us -> 9.78 us
  other arithmetic: 5.19 us -> 0 us
  Pallas kernels: 0 us -> 3.37 us
    ppermute x12 -> x5, starting transfers between devices: 32.5 us -> 6.19 us  [paired(): return lax.ppermute(value, ('depth', 'rows'), pairs)]
    all_to_all x0 -> x1, blocking collectives: none -> 16.2 us  [body(): part = lax.all_to_all(part, 'depth', 0, 0)]
    ppermute x12 -> x5, waiting for transfers between devices: 21.3 us -> 9.78 us  [paired(): return lax.ppermute(value, ('depth', 'rows'), pairs)]
    pallas_call x0 -> x4, Pallas kernels: none -> 3.37 us  [the longest x1 2.14 us: body(): pl.pallas_call(functools.partial(second_kernel, count, len(beside)), out_...]
    unnamed x16 -> x14, local copies, waits for them, and re-layouts: 1.44 us -> 3.8 us
    sub x3 -> x0, other arithmetic: 1.74 us -> none  [the longest x1 0.89 us: body(): auto - 0.25]
    another operation x5 -> x0, other arithmetic: 1.36 us -> none  [the longest x2 1.05 us: body(): fields = jnp.stack([substrate, catalyst])]
    slice x4 -> x0, local copies, waits for them, and re-layouts: 1.33 us -> none  [the longest x2 0.7 us: body(): cumul[-1]]
  transfers between devices with their start and end apart: 12 -> 5, of which waited for: 10 -> 2; matrix products, arithmetic and copies ran while one was open for 0% -> 0% of each run, Pallas kernels for 0% -> 0%
where the time goes in v1:
time: 40.3 us; the launch traced here: 40.1 us
  blocking collectives  16.2 us (40%)
  waiting for transfers between devices  9.78 us (24%)
  starting transfers between devices  6.19 us (15%)
  local copies, waits for them, and re-layouts  3.8 us (9%)
  Pallas kernels  3.37 us (8%)
  between operations  0.68 us (2%)
    all_to_all x1, blocking collectives, body(): part = lax.all_to_all(part, 'depth', 0, 0)  16.2 us
    ppermute x5, waiting for transfers between devices, paired(): return lax.ppermute(value, ('depth', 'rows'), pairs)  9.78 us
    ppermute x5, starting transfers between devices, paired(): return lax.ppermute(value, ('depth', 'rows'), pairs)  6.19 us
    unnamed x14, local copies, waits for them, and re-layouts  3.8 us
    pallas_call x1, Pallas kernels, body(): pl.pallas_call(functools.partial(second_kernel, count, len(beside)), out_...  2.14 us
  transfers between devices with their start and end apart: 5, of which 2 were waited for; matrix products, arithmetic and copies ran while one was open for 0% of the time, Pallas kernels for 0%

profile of v1, /device:TPU:0, one launch (start us, length us, event | category | flops | bytes accessed | tf_op | source)
XLA Modules:
  0.0 40.1 jit_solution(9489207934515058218)
XLA Ops:
  0.6 0.0 copy-start
  0.6 0.9 %copy-done = f32[4,16,1024]{2,1,0:T(8,128)S(1)} copy-done((f32[4,16,1024]{2,1,0:T(8,128)S(1)}, f32[4,16,1024]{2,1,0:T(8,128)}, u32[]{:S(2)}) %copy-start) | copy-done | bytes 262168
  1.6 0.0 copy-start.2
  1.6 0.9 %copy-done.2 = f32[4,16,1024]{2,1,0:T(8,128)S(1)} copy-done((f32[4,16,1024]{2,1,0:T(8,128)S(1)}, f32[4,16,1024]{2,1,0:T(8,128)}, u32[]{:S(2)}) %copy-start.2) | copy-done | bytes 262168
  2.5 0.0 copy-start.3
  2.5 0.9 %copy-done.3 = f32[4,16,1024]{2,1,0:T(8,128)S(1)} copy-done((f32[4,16,1024]{2,1,0:T(8,128)S(1)}, f32[4,16,1024]{2,1,0:T(8,128)}, u32[]{:S(2)}) %copy-start.3) | copy-done | bytes 262168
  3.5 0.0 copy-start.4
  3.5 0.9 %copy-done.4 = f32[4,16,1024]{2,1,0:T(8,128)S(1)} copy-done((f32[4,16,1024]{2,1,0:T(8,128)S(1)}, f32[4,16,1024]{2,1,0:T(8,128)}, u32[]{:S(2)}) %copy-start.4) | copy-done | bytes 262168
  4.4 0.0 copy-start.1
  4.4 0.0 copy-start.5
  4.4 0.5 %first_step.1 = (f32[4,16,1024]{2,1,0:T(8,128)S(1)}, f32[4,16,1024]{2,1,0:T(8,128)S(1)}, f32[4,16,1024]{2,1,0:T(8,128)S(1)}, f32[4,16,1024]{2,1,0:T(8,128)S(1)}, f32[16,1024]{1,0:T(8,128)S(1)}) custom-call(f32[4,16,1024]{2,1,0:T(8,128)S(1)} %copy-done, f32[4,16,1024]{2,1,0:T(8,128)S(1)} %copy-done.2, f32[4,16,1024]{2,1,0:T(8,128)S(1)} %copy-done.3, ...), custom_call_target="tpu_custom_call" | custom-call | tf_op jit(solution)/shard_map/first_step/pallas_call | solution.py:272
  4.9 3.0 %collective-permute-start = (f32[4,16,1024]{2,1,0:T(8,128)S(1)}, f32[4,16,1024]{2,1,0:T(8,128)S(1)}, u32[]{:S(2)}, u32[]{:S(2)}) collective-permute-start(f32[4,16,1024]{2,1,0:T(8,128)S(1)} %get-tuple-element.15), channel_id=1, source_target_pairs={{0,2},{1,3},{2,0},{3,1},{4,6},{5,7},{6,4},{7,5},{8,10},{9,11},{10,... | collective-permute-start | bytes 786440 | tf_op jit(solution)/shard_map/ppermute | solution.py:40
  7.9 0.0 collective-permute-start.1
  7.9 0.5 %collective-permute-start.2 = (f32[16,1024]{1,0:T(8,128)S(1)}, f32[16,1024]{1,0:T(8,128)S(1)}, u32[]{:S(2)}, u32[]{:S(2)}) collective-permute-start(f32[16,1024]{1,0:T(8,128)S(1)} %get-tuple-element.17), channel_id=1, source_target_pairs={{0,1},{2,3},{4,5},{6,7},{8,9},{10,11},{12,13},{14,15},{16,17},{18,... | collective-permute-start | bytes 196616 | tf_op jit(solution)/shard_map/ppermute | solution.py:40
  8.5 1.1 %collective-permute-done.2.refs_0_.refs_12_ = f32[16,1024]{1,0:T(8,128)S(1)} collective-permute-done((f32[16,1024]{1,0:T(8,128)S(1)}, f32[16,1024]{1,0:T(8,128)S(1)}, u32[]{:S(2)}, u32[]{:S(2)}) %collective-permute-start.2) | collective-permute-done | bytes 65568 | tf_op jit(solution)/shard_map/ppermute | solution.py:40
  9.6 2.7 %collective-permute-start.3 = (f32[8,1024]{1,0:T(8,128)S(1)}, f32[8,1024]{1,0:T(8,128)S(1)}, u32[]{:S(2)}, u32[]{:S(2)}) collective-permute-start(f32[8,1024]{1,0:T(8,128)S(1)} %get-tuple-element.18), channel_id=1, source_target_pairs={{0,2},{1,3},{2,0},{3,1},{4,6},{5,7},{6,4},{7,5},{8,10},{9,11},{10,... | collective-permute-start | bytes 98312 | tf_op jit(solution)/shard_map/ppermute | solution.py:40
  12.3 0.0 copy-start.6
  12.3 0.0 collective-permute-start.4
  12.3 8.7 %collective-permute-done.3.refs_10_ = f32[8,1024]{1,0:T(8,128)S(1)} collective-permute-done((f32[8,1024]{1,0:T(8,128)S(1)}, f32[8,1024]{1,0:T(8,128)S(1)}, u32[]{:S(2)}, u32[]{:S(2)}) %collective-permute-start.3) | collective-permute-done | bytes 32800 | tf_op jit(solution)/shard_map/ppermute | solution.py:40
  20.9 0.0 collective-permute-done.4.refs_11_
  20.9 0.0 collective-permute-done.refs_8_
  20.9 0.0 collective-permute-done.1.refs_9_
  20.9 0.0 copy-done.1
  20.9 0.0 copy-done.5
  21.0 0.0 copy-done.6
  21.0 2.1 %second_step.1 = (f32[4,16,1024]{2,1,0:T(8,128)}, f32[4,16,1024]{2,1,0:T(8,128)}, f32[16,32,128]{2,1,0:T(8,128)S(1)}) custom-call(f32[4,16,1024]{2,1,0:T(8,128)S(1)} %copy-done.1, f32[4,16,1024]{2,1,0:T(8,128)S(1)} %copy-done.2, f32[4,16,1024]{2,1,0:T(8,128)S(1)} %copy-done.3, f32[4,16,1024]{2,1,0:T(8,128)S(1)} %copy-done.4, f32[4,16,1024]{2,1,0:T(8,128)S(1)} %copy-done.5, ...), custom_call_target="tpu_custom_call" | custom-call | tf_op jit(solution)/shard_map/second_step/pallas_call | solution.py:297
  23.1 16.2 %all_to_all.5.part_ref = f32[16,32,128]{2,1,0:T(8,128)S(1)} all-to-all(f32[16,32,128]{2,1,0:T(8,128)S(1)} %get-tuple-element.22), channel_id=1, replica_groups=mesh['depth'=16,'rows'=2] {'depth'}, dimensions={0} | all-to-all | bytes 524288 | tf_op jit(solution)/shard_map/all_to_all | solution.py:307
  39.3 0.7 %front_to_back.1 = f32[4,16,64]{2,1,0:T(8,128)} custom-call(f32[16,32,128]{2,1,0:T(8,128)S(1)} %all_to_all.5.part_ref), custom_call_target="tpu_custom_call" | custom-call | tf_op jit(solution)/shard_map/front_to_back/pallas_call | solution.py:308
  (1 shorter events, 0.0 us)
Async XLA Ops:
  0.6 1.0 %copy-start = (f32[4,16,1024]{2,1,0:T(8,128)S(1)}, f32[4,16,1024]{2,1,0:T(8,128)}, u32[]{:S(2)}) copy-start(f32[4,16,1024]{2,1,0:T(8,128)} %refs_0_.1) | copy-start | bytes 786436
  1.6 0.9 %copy-start.2 = (f32[4,16,1024]{2,1,0:T(8,128)S(1)}, f32[4,16,1024]{2,1,0:T(8,128)}, u32[]{:S(2)}) copy-start(f32[4,16,1024]{2,1,0:T(8,128)} %refs_1_.1) | copy-start | bytes 786436
  2.5 0.9 %copy-start.3 = (f32[4,16,1024]{2,1,0:T(8,128)S(1)}, f32[4,16,1024]{2,1,0:T(8,128)}, u32[]{:S(2)}) copy-start(f32[4,16,1024]{2,1,0:T(8,128)} %refs_2_.1) | copy-start | bytes 786436
  3.5 0.9 %copy-start.4 = (f32[4,16,1024]{2,1,0:T(8,128)S(1)}, f32[4,16,1024]{2,1,0:T(8,128)}, u32[]{:S(2)}) copy-start(f32[4,16,1024]{2,1,0:T(8,128)} %refs_3_.1) | copy-start | bytes 786436
  4.4 16.5 %copy-start.1 = (f32[4,16,1024]{2,1,0:T(8,128)S(1)}, f32[4,16,1024]{2,1,0:T(8,128)}, u32[]{:S(2)}) copy-start(f32[4,16,1024]{2,1,0:T(8,128)} %refs_0_.1) | copy-start | bytes 786436
  4.4 16.5 %copy-start.5 = (f32[4,16,1024]{2,1,0:T(8,128)S(1)}, f32[4,16,1024]{2,1,0:T(8,128)}, u32[]{:S(2)}) copy-start(f32[4,16,1024]{2,1,0:T(8,128)} %refs_4_.1) | copy-start | bytes 786436
  4.9 16.0 %collective-permute-start = (f32[4,16,1024]{2,1,0:T(8,128)S(1)}, f32[4,16,1024]{2,1,0:T(8,128)S(1)}, u32[]{:S(2)}, u32[]{:S(2)}) collective-permute-start(f32[4,16,1024]{2,1,0:T(8,128)S(1)} %get-tuple-element.15), channel_id=1, source_target_pairs={{0,2},{1,3},{2,0},{3,1},{4,6},{5,7},{6,4},{7,5},{8,10},{9,11},{10,... | collective-permute-start | bytes 786440 | tf_op jit(solution)/shard_map/ppermute | solution.py:40
  7.9 13.0 %collective-permute-start.1 = (f32[4,16,1024]{2,1,0:T(8,128)S(1)}, f32[4,16,1024]{2,1,0:T(8,128)S(1)}, u32[]{:S(2)}, u32[]{:S(2)}) collective-permute-start(f32[4,16,1024]{2,1,0:T(8,128)S(1)} %get-tuple-element.16), channel_id=1, source_target_pairs={{0,1},{1,0},{2,4},{3,5},{4,2},{5,3},{6,8},{7,9},{8,6},{9,7},{10,12... | collective-permute-start | bytes 786440 | tf_op jit(solution)/shard_map/ppermute | solution.py:40
  7.9 1.6 %collective-permute-start.2 = (f32[16,1024]{1,0:T(8,128)S(1)}, f32[16,1024]{1,0:T(8,128)S(1)}, u32[]{:S(2)}, u32[]{:S(2)}) collective-permute-start(f32[16,1024]{1,0:T(8,128)S(1)} %get-tuple-element.17), channel_id=1, source_target_pairs={{0,1},{2,3},{4,5},{6,7},{8,9},{10,11},{12,13},{14,15},{16,17},{18,... | collective-permute-start | bytes 196616 | tf_op jit(solution)/shard_map/ppermute | solution.py:40
  9.6 11.3 %collective-permute-start.3 = (f32[8,1024]{1,0:T(8,128)S(1)}, f32[8,1024]{1,0:T(8,128)S(1)}, u32[]{:S(2)}, u32[]{:S(2)}) collective-permute-start(f32[8,1024]{1,0:T(8,128)S(1)} %get-tuple-element.18), channel_id=1, source_target_pairs={{0,2},{1,3},{2,0},{3,1},{4,6},{5,7},{6,4},{7,5},{8,10},{9,11},{10,... | collective-permute-start | bytes 98312 | tf_op jit(solution)/shard_map/ppermute | solution.py:40
  12.3 8.7 %copy-start.6 = (f32[3,3]{1,0:T(4,128)S(1)}, f32[3,3]{1,0:T(4,128)}, u32[]{:S(2)}) copy-start(f32[3,3]{1,0:T(4,128)} %refs_5_.1) | copy-start | bytes 112
  12.3 8.7 %collective-permute-start.4 = (f32[8,1024]{1,0:T(8,128)S(1)}, f32[8,1024]{1,0:T(8,128)S(1)}, u32[]{:S(2)}, u32[]{:S(2)}) collective-permute-start(f32[8,1024]{1,0:T(8,128)S(1)} %get-tuple-element.19), channel_id=1, source_target_pairs={{0,1},{1,0},{2,4},{3,5},{4,2},{5,3},{6,8},{7,9},{8,6},{9,7},{10,12... | collective-permute-start | bytes 98312 | tf_op jit(solution)/shard_map/ppermute | solution.py:40

commit v2 on v1

--- a/solution.py
+++ b/solution.py
@@ -16,6 +16,7 @@
 SUBLANES = 8
 VMEM = pl.BlockSpec(memory_space=pltpu.VMEM)
 SMEM = pl.BlockSpec(memory_space=pltpu.SMEM)
+HBM = pl.BlockSpec(memory_space=pltpu.HBM)
 PARAMS = pltpu.CompilerParams(vmem_limit_bytes=24 * 1024 * 1024)
 
 
@@ -67,7 +68,16 @@
     return fed + time_step * fed_change, auto + time_step * auto_change
 
 
-def first_kernel(s_ref, c_ref, f_ref, k_ref, ps_ref, pc_ref, a_ref, b_ref, *row_refs):
+def first_kernel(row_pairings, *refs):
+    ps_ref, pc_ref, a_ref, b_ref = refs[4:8]
+    row_refs = refs[8 : 8 + row_pairings]
+    *held, arrived = refs[8 + row_pairings :]
+    copies = [pltpu.make_async_copy(refs[n], held[n], arrived.at[n]) for n in range(4)]
+    for copy in copies:
+        copy.start()
+    for copy in copies:
+        copy.wait()
+    s_ref, c_ref, f_ref, k_ref = held
     depth, rows, _ = s_ref.shape
     for layer in range(depth):
         near = []
@@ -270,17 +280,20 @@
     beam = f32((4, rows, columns))
     strip = f32((4 * depth, columns))
     outs = pl.pallas_call(
-        first_kernel,
+        functools.partial(first_kernel, len(along_rows)),
         out_shape=(whole, whole, beam, beam) + (strip,) * len(along_rows),
-        in_specs=[VMEM] * 4,
+        in_specs=[HBM] * 4,
         out_specs=(VMEM,) * (4 + len(along_rows)),
+        scratch_shapes=[pltpu.VMEM(whole.shape, jnp.float32)] * 4 + [pltpu.SemaphoreType.DMA((4,))],
         compiler_params=PARAMS,
         name="first_step",
-    )(substrate, catalyst, feed_rate, kill_rate)
+    )(*(pltpu.with_memory_space_constraint(x, pltpu.HBM) for x in (substrate, catalyst, feed_rate, kill_rate)))
     step_fed, step_auto, *beams = outs[:4]
-    far = [paired(value, pairs) for value, pairs in zip(beams, along_depth)]
+    far_b = paired(beams[1], along_depth[1])
+    far_a = paired(beams[0], along_depth[0])
+    far = [far_a, far_b]
     beside = [paired(value, pairs) for value, pairs in zip(outs[4:], along_rows)]
-    corner = f32((SUBLANES, columns))
+    corner = f32((4, columns))
     corners = pl.pallas_call(
         functools.partial(corner_kernel, depth),
         out_shape=(corner, corner),

time: 40.3 us -> 38.2 us (0.948)
  local copies, waits for them, and re-layouts: 3.8 us -> 0.97 us
  Pallas kernels: 3.37 us -> 4.75 us
  waiting for transfers between devices: 9.78 us -> 9.25 us
    unnamed x14 -> x12, local copies, waits for them, and re-layouts: 3.8 us -> 0.97 us
    pallas_call x1, Pallas kernels: 0.51 us -> 1.81 us  [body(): pl.pallas_call(functools.partial(first_kernel, len(along_rows)), out_shap...]
    ppermute x5, waiting for transfers between devices: 9.78 us -> 9.25 us  [paired(): return lax.ppermute(value, ('depth', 'rows'), pairs)]
where the time goes in v2:
time: 38.2 us; the launch traced here: 38 us
  blocking collectives  16.1 us (42%)
  waiting for transfers between devices  9.25 us (24%)
  starting transfers between devices  6.19 us (16%)
  Pallas kernels  4.75 us (12%)
  local copies, waits for them, and re-layouts  0.97 us (3%)
  between operations  0.73 us (2%)
    all_to_all x1, blocking collectives, body(): part = lax.all_to_all(part, 'depth', 0, 0)  16.1 us
    ppermute x5, waiting for transfers between devices, paired(): return lax.ppermute(value, ('depth', 'rows'), pairs)  9.25 us
    ppermute x5, starting transfers between devices, paired(): return lax.ppermute(value, ('depth', 'rows'), pairs)  6.19 us
    pallas_call x1, Pallas kernels, body(): pl.pallas_call(functools.partial(second_kernel, count, len(beside)), out_...  2.22 us
    pallas_call x1, Pallas kernels, body(): pl.pallas_call(functools.partial(first_kernel, len(along_rows)), out_shap...  1.81 us
    unnamed x12, local copies, waits for them, and re-layouts  0.97 us
  transfers between devices with their start and end apart: 5, of which 2 were waited for; matrix products, arithmetic and copies ran while one was open for 0% of the time, Pallas kernels for 0%

profile of v2, /device:TPU:0, one launch (start us, length us, event | category | flops | bytes accessed | tf_op | source)
XLA Modules:
  0.0 38.0 jit_solution(2474003157306384972)
XLA Ops:
  0.6 0.0 copy-start.3
  0.6 0.0 copy-start.2
  0.7 0.0 copy-start.1
  0.7 0.0 copy-start
  0.7 1.8 %first_step.1 = (f32[4,16,1024]{2,1,0:T(8,128)S(1)}, f32[4,16,1024]{2,1,0:T(8,128)S(1)}, f32[4,16,1024]{2,1,0:T(8,128)S(1)}, f32[4,16,1024]{2,1,0:T(8,128)S(1)}, f32[16,1024]{1,0:T(8,128)S(1)}) custom-call(f32[4,16,1024]{2,1,0:T(8,128)} %refs_0_.3, f32[4,16,1024]{2,1,0:T(8,128)} %refs_1_.3, f32[4,16,1024]{2,1,0:T(8,128)} %refs_2_.3, f32[4,16,1024]{2,1,0:T(8,128)} %refs_3_.3), custom_call_target="tpu_custom_call" | custom-call | tf_op jit(solution)/shard_map/first_step/pallas_call | solution.py:282
  2.5 3.0 %collective-permute-start = (f32[4,16,1024]{2,1,0:T(8,128)S(1)}, f32[4,16,1024]{2,1,0:T(8,128)S(1)}, u32[]{:S(2)}, u32[]{:S(2)}) collective-permute-start(f32[4,16,1024]{2,1,0:T(8,128)S(1)} %get-tuple-element.15), channel_id=1, source_target_pairs={{0,2},{1,3},{2,0},{3,1},{4,6},{5,7},{6,4},{7,5},{8,10},{9,11},{10,... | collective-permute-start | bytes 786440 | tf_op jit(solution)/shard_map/ppermute | solution.py:41
  5.5 0.0 collective-permute-start.1
  5.5 0.5 %collective-permute-start.2 = (f32[16,1024]{1,0:T(8,128)S(1)}, f32[16,1024]{1,0:T(8,128)S(1)}, u32[]{:S(2)}, u32[]{:S(2)}) collective-permute-start(f32[16,1024]{1,0:T(8,128)S(1)} %get-tuple-element.17), channel_id=1, source_target_pairs={{0,1},{2,3},{4,5},{6,7},{8,9},{10,11},{12,13},{14,15},{16,17},{18,... | collective-permute-start | bytes 196616 | tf_op jit(solution)/shard_map/ppermute | solution.py:41
  6.0 1.1 %collective-permute-done.2.refs_0_.refs_12_ = f32[16,1024]{1,0:T(8,128)S(1)} collective-permute-done((f32[16,1024]{1,0:T(8,128)S(1)}, f32[16,1024]{1,0:T(8,128)S(1)}, u32[]{:S(2)}, u32[]{:S(2)}) %collective-permute-start.2) | collective-permute-done | bytes 65568 | tf_op jit(solution)/shard_map/ppermute | solution.py:41
  7.1 2.7 %collective-permute-start.3 = (f32[4,1024]{1,0:T(4,128)S(1)}, f32[4,1024]{1,0:T(4,128)S(1)}, u32[]{:S(2)}, u32[]{:S(2)}) collective-permute-start(f32[4,1024]{1,0:T(4,128)S(1)} %get-tuple-element.18), channel_id=1, source_target_pairs={{0,2},{1,3},{2,0},{3,1},{4,6},{5,7},{6,4},{7,5},{8,10},{9,11},{10,... | collective-permute-start | bytes 49160 | tf_op jit(solution)/shard_map/ppermute | solution.py:41
  9.8 0.0 copy-start.5
  9.8 0.0 collective-permute-start.4
  9.8 8.1 %collective-permute-done.3.refs_10_ = f32[4,1024]{1,0:T(4,128)S(1)} collective-permute-done((f32[4,1024]{1,0:T(4,128)S(1)}, f32[4,1024]{1,0:T(4,128)S(1)}, u32[]{:S(2)}, u32[]{:S(2)}) %collective-permute-start.3) | collective-permute-done | bytes 16416 | tf_op jit(solution)/shard_map/ppermute | solution.py:41
  17.9 0.0 collective-permute-done.4.refs_11_
  17.9 0.0 collective-permute-done.refs_8_
  17.9 0.0 collective-permute-done.1.refs_9_
  18.0 0.0 copy-done.3
  18.0 0.0 copy-done.2
  18.0 0.0 copy-done.1
  18.0 0.0 copy-done
  18.0 0.0 copy-done.5
  18.0 0.0 copy-start.4
  18.0 0.9 %copy-done.4 = f32[4,16,1024]{2,1,0:T(8,128)S(1)} copy-done((f32[4,16,1024]{2,1,0:T(8,128)S(1)}, f32[4,16,1024]{2,1,0:T(8,128)}, u32[]{:S(2)}) %copy-start.4) | copy-done | bytes 262168
  19.0 2.2 %second_step.1 = (f32[4,16,1024]{2,1,0:T(8,128)}, f32[4,16,1024]{2,1,0:T(8,128)}, f32[16,32,128]{2,1,0:T(8,128)S(1)}) custom-call(f32[4,16,1024]{2,1,0:T(8,128)S(1)} %copy-done, f32[4,16,1024]{2,1,0:T(8,128)S(1)} %copy-done.1, f32[4,16,1024]{2,1,0:T(8,128)S(1)} %copy-done.2, f32[4,16,1024]{2,1,0:T(8,128)S(1)} %copy-done.3, f32[4,16,1024]{2,1,0:T(8,128)S(1)} %copy-done.4, ...), custom_call_target="tpu_custom_call" | custom-call | tf_op jit(solution)/shard_map/second_step/pallas_call | solution.py:310
  21.2 16.1 %all_to_all.5.part_ref = f32[16,32,128]{2,1,0:T(8,128)S(1)} all-to-all(f32[16,32,128]{2,1,0:T(8,128)S(1)} %get-tuple-element.22), channel_id=1, replica_groups=mesh['depth'=16,'rows'=2] {'depth'}, dimensions={0} | all-to-all | bytes 524288 | tf_op jit(solution)/shard_map/all_to_all | solution.py:320
  37.2 0.7 %front_to_back.1 = f32[4,16,64]{2,1,0:T(8,128)} custom-call(f32[16,32,128]{2,1,0:T(8,128)S(1)} %all_to_all.5.part_ref), custom_call_target="tpu_custom_call" | custom-call | tf_op jit(solution)/shard_map/front_to_back/pallas_call | solution.py:321
  (1 shorter events, 0.0 us)
Async XLA Ops:
  0.6 17.3 %copy-start.3 = (f32[4,16,1024]{2,1,0:T(8,128)S(1)}, f32[4,16,1024]{2,1,0:T(8,128)}, u32[]{:S(2)}) copy-start(f32[4,16,1024]{2,1,0:T(8,128)} %refs_3_.3) | copy-start | bytes 786436
  0.6 17.3 %copy-start.2 = (f32[4,16,1024]{2,1,0:T(8,128)S(1)}, f32[4,16,1024]{2,1,0:T(8,128)}, u32[]{:S(2)}) copy-start(f32[4,16,1024]{2,1,0:T(8,128)} %refs_2_.3) | copy-start | bytes 786436
  0.7 17.3 %copy-start.1 = (f32[4,16,1024]{2,1,0:T(8,128)S(1)}, f32[4,16,1024]{2,1,0:T(8,128)}, u32[]{:S(2)}) copy-start(f32[4,16,1024]{2,1,0:T(8,128)} %refs_1_.3) | copy-start | bytes 786436
  0.7 17.3 %copy-start = (f32[4,16,1024]{2,1,0:T(8,128)S(1)}, f32[4,16,1024]{2,1,0:T(8,128)}, u32[]{:S(2)}) copy-start(f32[4,16,1024]{2,1,0:T(8,128)} %refs_0_.3) | copy-start | bytes 786436
  2.5 15.5 %collective-permute-start = (f32[4,16,1024]{2,1,0:T(8,128)S(1)}, f32[4,16,1024]{2,1,0:T(8,128)S(1)}, u32[]{:S(2)}, u32[]{:S(2)}) collective-permute-start(f32[4,16,1024]{2,1,0:T(8,128)S(1)} %get-tuple-element.15), channel_id=1, source_target_pairs={{0,2},{1,3},{2,0},{3,1},{4,6},{5,7},{6,4},{7,5},{8,10},{9,11},{10,... | collective-permute-start | bytes 786440 | tf_op jit(solution)/shard_map/ppermute | solution.py:41
  5.5 12.5 %collective-permute-start.1 = (f32[4,16,1024]{2,1,0:T(8,128)S(1)}, f32[4,16,1024]{2,1,0:T(8,128)S(1)}, u32[]{:S(2)}, u32[]{:S(2)}) collective-permute-start(f32[4,16,1024]{2,1,0:T(8,128)S(1)} %get-tuple-element.16), channel_id=1, source_target_pairs={{0,1},{1,0},{2,4},{3,5},{4,2},{5,3},{6,8},{7,9},{8,6},{9,7},{10,12... | collective-permute-start | bytes 786440 | tf_op jit(solution)/shard_map/ppermute | solution.py:41
  5.5 1.6 %collective-permute-start.2 = (f32[16,1024]{1,0:T(8,128)S(1)}, f32[16,1024]{1,0:T(8,128)S(1)}, u32[]{:S(2)}, u32[]{:S(2)}) collective-permute-start(f32[16,1024]{1,0:T(8,128)S(1)} %get-tuple-element.17), channel_id=1, source_target_pairs={{0,1},{2,3},{4,5},{6,7},{8,9},{10,11},{12,13},{14,15},{16,17},{18,... | collective-permute-start | bytes 196616 | tf_op jit(solution)/shard_map/ppermute | solution.py:41
  7.1 10.8 %collective-permute-start.3 = (f32[4,1024]{1,0:T(4,128)S(1)}, f32[4,1024]{1,0:T(4,128)S(1)}, u32[]{:S(2)}, u32[]{:S(2)}) collective-permute-start(f32[4,1024]{1,0:T(4,128)S(1)} %get-tuple-element.18), channel_id=1, source_target_pairs={{0,2},{1,3},{2,0},{3,1},{4,6},{5,7},{6,4},{7,5},{8,10},{9,11},{10,... | collective-permute-start | bytes 49160 | tf_op jit(solution)/shard_map/ppermute | solution.py:41
  9.8 8.2 %copy-start.5 = (f32[3,3]{1,0:T(4,128)S(1)}, f32[3,3]{1,0:T(4,128)}, u32[]{:S(2)}) copy-start(f32[3,3]{1,0:T(4,128)} %refs_5_.1) | copy-start | bytes 112
  9.8 8.1 %collective-permute-start.4 = (f32[4,1024]{1,0:T(4,128)S(1)}, f32[4,1024]{1,0:T(4,128)S(1)}, u32[]{:S(2)}, u32[]{:S(2)}) collective-permute-start(f32[4,1024]{1,0:T(4,128)S(1)} %get-tuple-element.19), channel_id=1, source_target_pairs={{0,1},{1,0},{2,4},{3,5},{4,2},{5,3},{6,8},{7,9},{8,6},{9,7},{10,12... | collective-permute-start | bytes 49160 | tf_op jit(solution)/shard_map/ppermute | solution.py:41
  18.0 1.0 %copy-start.4 = (f32[4,16,1024]{2,1,0:T(8,128)S(1)}, f32[4,16,1024]{2,1,0:T(8,128)}, u32[]{:S(2)}) copy-start(f32[4,16,1024]{2,1,0:T(8,128)} %refs_4_.1) | copy-start | bytes 786436

commit v3 on v1

v3 whole, which is shorter than its diff:
```python
import functools

import jax
import jax.numpy as jnp
from jax import lax
from jax.experimental import pallas as pl
from jax.experimental.pallas import tpu as pltpu
from jax.sharding import PartitionSpec as P

diffusion_fast = 0.08
diffusion_slow = 0.04
time_step = 2.0
reach_fast = time_step * diffusion_fast
reach_slow = time_step * diffusion_slow
LANES = 128
SUBLANES = 8
VMEM = pl.BlockSpec(memory_space=pltpu.VMEM)
SMEM = pl.BlockSpec(memory_space=pltpu.SMEM)
HBM = pl.BlockSpec(memory_space=pltpu.HBM)
WORK = pl.CostEstimate(flops=20_000_000, bytes_accessed=4_000_000, transcendentals=0)
PARAMS = pltpu.CompilerParams(vmem_limit_bytes=24 * 1024 * 1024)


def pairings(axis, other):
    count, width = lax.axis_size(axis), lax.axis_size(other)
    flat = (lambda i, j: i * width + j) if axis == "depth" else (lambda i, j: j * count + i)
    result = []
    for shift in (0, 1):
        pairs = []
        for i in range(count):
            partner = ((i + shift) ^ 1) - shift
            for j in range(width):
                if 0 <= partner < count:
                    pairs.append((flat(i, j), flat(partner, j)))
                elif j ^ 1 < width:
                    pairs.append((flat(i, j), flat(i, j ^ 1)))
        result.append(pairs if count > 2 or shift == 0 else None)
    return result


def paired(value, pairs):
    return lax.ppermute(value, ("depth", "rows"), pairs)


def is_even(axis):
    return lax.rem(lax.axis_index(axis), 2) == 0


def shifted_columns(value):
    width = value.shape[-1]
    column = lax.broadcasted_iota(jnp.int32, value.shape, value.ndim - 1)
    left = jnp.where(column == 0, 0.0, pltpu.roll(value, 1, value.ndim - 1))
    right = jnp.where(column == width - 1, 0.0, pltpu.roll(value, width - 1, value.ndim - 1))
    return left + right


def shifted_rows(value, above, below):
    rows = value.shape[0]
    row = lax.broadcasted_iota(jnp.int32, value.shape, 0)
    upper = jnp.where(row == 0, above, pltpu.roll(value, 1, 0))
    lower = jnp.where(row == rows - 1, below, pltpu.roll(value, rows - 1, 0))
    return upper + lower


def react(fed, auto, fed_near, auto_near, feed, kill):
    reaction = fed * auto * auto
    fed_change = diffusion_fast * (fed_near - 6.0 * fed) - reaction + feed * (1.0 - fed)
    auto_change = diffusion_slow * (auto_near - 6.0 * auto) + reaction - (feed + kill) * auto
    return fed + time_step * fed_change, auto + time_step * auto_change


def partial_step(s_ref, c_ref, feed, kill, layer, inner):
    near = []
    for ref in (s_ref, c_ref):
        value = ref[layer]
        total = shifted_rows(value, 0.0, 0.0) + shifted_columns(value)
        for other in inner:
            total = total + ref[other]
        near.append(total)
    return react(s_ref[layer], c_ref[layer], near[0], near[1], feed, kill)


def beam_kernel(s_hbm, c_hbm, f_hbm, k_hbm, a_ref, b_ref, s_ref, c_ref, f_ref, k_ref, arrived):
    depth = s_hbm.shape[0]
    even = is_even("depth")
    ends = []
    for n, towards_next in enumerate((even, jnp.logical_not(even))):
        layer = jnp.where(towards_next, depth - 1, 0)
        places = [layer]
        if depth > 1:
            places.append(jnp.where(towards_next, depth - 2, 1))
        copies = []
        for m, place in enumerate(places):
            for i, (hbm, ref) in enumerate(((s_hbm, s_ref), (c_hbm, c_ref))):
                copies.append(pltpu.make_async_copy(hbm.at[place], ref.at[2 * n + m], arrived.at[n, 2 * m + i]))
        for i, (hbm, ref) in enumerate(((f_hbm, f_ref), (k_hbm, k_ref))):
            copies.append(pltpu.make_async_copy(hbm.at[layer], ref.at[n], arrived.at[n, 4 + i]))
        for copy in copies:
            copy.start()
        ends.append(copies)
    for n, out in enumerate((a_ref, b_ref)):
        for copy in ends[n]:
            copy.wait()
        out[0] = s_ref[2 * n]
        out[1] = c_ref[2 * n]
        inner = [2 * n + 1] if depth > 1 else []
        out[2], out[3] = partial_step(s_ref, c_ref, f_ref[n], k_ref[n], 2 * n, inner)


def strip_kernel(s_ref, c_ref, f_ref, k_ref, ps_ref, pc_ref, *strips):
    depth, rows, _ = s_ref.shape
    for layer in range(depth):
        inner = [other for other in (layer - 1, layer + 1) if 0 <= other < depth]
        ps_ref[layer], pc_ref[layer] = partial_step(s_ref, c_ref, f_ref[layer], k_ref[layer], layer, inner)
    even = is_even("rows")
    for out, towards_next in zip(strips, (even, jnp.logical_not(even))):
        for n, ref in enumerate((s_ref, c_ref, ps_ref, pc_ref)):
            for layer in range(depth):
                head, tail = ref[layer, 0:1], ref[layer, rows - 1 : rows]
                out[n * depth + layer : n * depth + layer + 1] = jnp.where(towards_next, tail, head)


def sides(axis, refs, read):
    index, count = lax.axis_index(axis), lax.axis_size(axis)
    even = is_even(axis)
    first = read(refs[0])
    second = read(refs[1]) if len(refs) == 2 else 0.0
    before = jnp.where(even, second, first)
    after = jnp.where(even, first, second)
    return jnp.where(index == 0, 0.0, before), jnp.where(index == count - 1, 0.0, after)


def step_two(fields, outside, layer, others, feed, kill):
    near = []
    for n in range(2):
        value = fields[n][layer]
        total = shifted_rows(value, outside[n][layer][0], outside[n][layer][1]) + shifted_columns(value)
        for other in others[n]:
            total = total + other
        near.append(total)
    return react(fields[0][layer], fields[1][layer], near[0], near[1], feed, kill)


def inner_kernel(s_ref, c_ref, f_ref, k_ref, e_ref, ps_ref, pc_ref, *refs):
    *beside, fed_one, auto_one, fed_two, auto_two, outer_ref, fade_ref = refs
    depth, rows, columns = s_ref.shape
    row = lax.broadcasted_iota(jnp.int32, (rows, columns), 0)
    index, last = lax.axis_index("rows"), lax.axis_size("rows") - 1
    inside = (index > 0, index < last)
    fields, outside = [], []
    for n, (old, partial, out, reach) in enumerate(
        ((s_ref, ps_ref, fed_one, reach_fast), (c_ref, pc_ref, auto_one, reach_slow))
    ):
        values, rows_outside = [], []
        for layer in range(depth):
            at = n * depth + layer
            above, below = sides("rows", beside, lambda ref: ref[at : at + 1])
            near = jnp.where(row == 0, above, 0.0) + jnp.where(row == rows - 1, below, 0.0)
            value = partial[layer] + reach * near
            values.append(value)
            out[layer] = value
            at = (2 + n) * depth + layer
            beyond = sides("rows", beside, lambda ref: ref[at : at + 1])
            ends = []
            for side, own in enumerate((old[layer, 0:1], old[layer, rows - 1 : rows])):
                end = jnp.where(inside[side], beyond[side] + reach * own, 0.0)
                ends.append(end)
                at = (n * 2 + side) * depth + layer
                outer_ref[at : at + 1] = end
            rows_outside.append(ends)
        fields.append(values)
        outside.append(rows_outside)
    for layer in range(1, depth - 1):
        others = [(values[layer - 1], values[layer + 1]) for values in fields]
        fed_two[layer], auto_two[layer] = step_two(fields, outside, layer, others, f_ref[layer], k_ref[layer])
    for layer in range(depth):
        fade_ref[layer] = -e_ref[layer]


def corner_kernel(a_ref, b_ref, _, *outs):
    rows = a_ref.shape[1]
    even = is_even("rows")
    for out, towards_next in zip(outs, (even, jnp.logical_not(even))):
        for n in range(2):
            pair = sides(
                "depth",
                (a_ref, b_ref),
                lambda ref: jnp.where(towards_next, ref[n, rows - 1 : rows], ref[n, 0:1]),
            )
            for end in range(2):
                out[2 * n + end : 2 * n + end + 1] = pair[end]


class Shading:
    def __init__(self, palette):
        self.palette = palette
        self.gather = None
        self.before = None

    def put(self, pieces, passing):
        if self.gather is None:
            self.gather, self.before = list(pieces), passing
            return
        self.gather = [total + self.before * piece for total, piece in zip(self.gather, pieces)]
        self.before = self.before * passing

    def add(self, fed, auto, fade):
        passing = jnp.exp(fade * (0.25 + 4.0 * auto * auto))
        opacity = 1.0 - passing
        pieces = []
        for channel in range(3):
            level = (
                (8.0 * self.palette[channel, 0]) * (fed - 0.65)
                + (8.0 * self.palette[channel, 1]) * (auto - 0.25)
                + self.palette[channel, 2]
            )
            pieces.append(opacity / (1.0 + jnp.exp(-level)))
        self.put(pieces + [opacity], passing)


def second_kernel(*refs):
    s_ref, c_ref, f_ref, k_ref, fade_ref, palette = refs[:6]
    fed_one, auto_one, fed_mid, auto_mid, outer_ref = refs[6:11]
    far = refs[11:13]
    fed_two, auto_two, middle_ref = refs[13:]
    depth = s_ref.shape[0]
    index, last = lax.axis_index("depth"), lax.axis_size("depth") - 1
    inside = (index > 0, index < last)
    fields, outside, beyond, far_old = [], [], [], []
    for n, (old, one, reach) in enumerate(((s_ref, fed_one, reach_fast), (c_ref, auto_one, reach_slow))):
        old_far = sides("depth", far, lambda ref: ref[n])
        new_far = sides("depth", far, lambda ref: ref[2 + n])
        far_old.append(old_far)
        beyond.append(
            [
                jnp.where(inside[end], new_far[end] + reach * old[layer], 0.0)
                for end, layer in enumerate((0, depth - 1))
            ]
        )
        values, rows_outside = {}, {}
        for layer in (0, depth - 1):
            near = 0.0
            if layer == 0:
                near = near + old_far[0]
            if layer == depth - 1:
                near = near + old_far[1]
            values[layer] = one[layer] + reach * near
            rows_outside[layer] = [
                outer_ref[(n * 2 + side) * depth + layer : (n * 2 + side) * depth + layer + 1] for side in range(2)
            ]
        fields.append(values)
        outside.append(rows_outside)
    shading = Shading(palette)
    for layer in range(depth):
        if layer in (0, depth - 1):
            others = []
            for n, one in enumerate((fed_one, auto_one)):
                others.append(
                    [
                        beyond[n][0] if layer == 0 else fields[n].get(layer - 1, one[layer - 1]),
                        beyond[n][1] if layer == depth - 1 else fields[n].get(layer + 1, one[layer + 1]),
                    ]
                )
            fed, auto = step_two(fields, outside, layer, others, f_ref[layer], k_ref[layer])
        else:
            fed, auto = fed_mid[layer], auto_mid[layer]
            for end, beside in enumerate((1, depth - 2)):
                if layer == beside:
                    fed = fed + (reach_fast * reach_fast) * far_old[0][end]
                    auto = auto + (reach_slow * reach_slow) * far_old[1][end]
            shading.add(fed, auto, fade_ref[layer])
        fed_two[layer] = fed
        auto_two[layer] = auto
    if shading.gather is not None:
        for n, value in enumerate(shading.gather + [shading.before]):
            middle_ref[n] = value


def shade_kernel(depth_count, fed_two, auto_two, fade_ref, palette, middle_ref, *refs):
    *corners, fed_out, auto_out, part_ref = refs
    depth, rows, columns = fed_two.shape
    row = lax.broadcasted_iota(jnp.int32, (rows, columns), 0)
    shading = Shading(palette)
    for layer in range(depth):
        if layer not in (0, depth - 1):
            if layer == 1:
                shading.put([middle_ref[n] for n in range(4)], middle_ref[4])
            continue
        values = []
        for n, (two, out, reach) in enumerate(
            ((fed_two, fed_out, reach_fast), (auto_two, auto_out, reach_slow))
        ):
            value = two[layer]
            for end, place in enumerate((0, depth - 1)):
                if layer == place:
                    at = 2 * n + end
                    above, below = sides("rows", corners, lambda ref: ref[at : at + 1])
                    near = jnp.where(row == 0, above, 0.0) + jnp.where(row == rows - 1, below, 0.0)
                    value = value + (2.0 * reach * reach) * near
            out[layer] = value
            values.append(value)
        shading.add(values[0], values[1], fade_ref[layer])
    gather = shading.gather

    block = columns // depth_count
    group = packing(rows, block)
    if not group:
        for channel in range(4):
            part_ref[channel] = gather[channel]
        return
    high = rows // group
    lane = lax.broadcasted_iota(jnp.int32, (high, LANES), 1) // block
    for channel in range(4):
        for tile in range(columns // LANES):
            pieces = [
                gather[channel][q * high : (q + 1) * high, tile * LANES : (tile + 1) * LANES]
                for q in range(group)
            ]
            for p in range(group):
                packed = None
                for q in range(group):
                    turn = (q - p) * block % LANES
                    piece = pltpu.roll(pieces[q], turn, 1) if turn else pieces[q]
                    packed = piece if packed is None else jnp.where(lane == q, piece, packed)
                part_ref[tile * group + p, channel * high : (channel + 1) * high] = packed


def packing(rows, block):
    if block >= LANES or LANES % block:
        return 0
    group = LANES // block
    return group if rows % (group * SUBLANES) == 0 else 0


def last_kernel(group, part_ref, fed_ref, auto_ref, image_ref, fed_out, auto_out, written):
    copies = [
        pltpu.make_async_copy(ref, out, written.at[n])
        for n, (ref, out) in enumerate(((fed_ref, fed_out), (auto_ref, auto_out)))
    ]
    for copy in copies:
        copy.start()
    _, rows, block = image_ref.shape
    high = rows // group
    count = part_ref.shape[0]
    total = [part_ref[0, channel * high : (channel + 1) * high] for channel in range(4)]
    before = 1.0 - total[3]
    for n in range(1, count):
        for channel in range(4):
            piece = part_ref[n, channel * high : (channel + 1) * high]
            total[channel] = total[channel] + before * piece
        if n < count - 1:
            before = before * (1.0 - piece)
    for channel in range(4):
        for q in range(group):
            image_ref[channel, q * high : (q + 1) * high] = total[channel][:, q * block : (q + 1) * block]
    for copy in copies:
        copy.wait()


def body(substrate, catalyst, feed_rate, kill_rate, extinction, palette):
    depth, rows, columns = substrate.shape
    count = lax.axis_size("depth")
    f32 = functools.partial(jax.ShapeDtypeStruct, dtype=jnp.float32)
    whole = f32(substrate.shape)
    along_depth = pairings("depth", "rows")
    if along_depth[1] is None:
        along_depth[1] = along_depth[0]
    along_rows = [pairs for pairs in pairings("rows", "depth") if pairs is not None]

    cells = (substrate, catalyst, feed_rate, kill_rate)
    beam = f32((4, rows, columns))
    layers = lambda count: pltpu.VMEM((count, rows, columns), jnp.float32)
    held = layers(depth)
    beams = pl.pallas_call(
        beam_kernel,
        out_shape=(beam, beam),
        in_specs=[HBM] * 4,
        out_specs=(VMEM, VMEM),
        scratch_shapes=[layers(4), layers(4), layers(2), layers(2), pltpu.SemaphoreType.DMA((2, 6))],
        compiler_params=PARAMS,
        name="depth_messages",
    )(*(pltpu.with_memory_space_constraint(x, pltpu.HBM) for x in cells))
    far = [paired(value, pairs) for value, pairs in zip(beams, along_depth)]

    strip = f32((4 * depth, columns))
    step_fed, step_auto, *strips = pl.pallas_call(
        strip_kernel,
        out_shape=(whole, whole) + (strip,) * len(along_rows),
        cost_estimate=WORK,
        in_specs=[VMEM] * 4,
        out_specs=(VMEM,) * (2 + len(along_rows)),
        compiler_params=PARAMS,
        name="row_messages",
    )(*cells)
    beside = [paired(value, pairs) for value, pairs in zip(strips, along_rows)]
    *inner, fade = pl.pallas_call(
        inner_kernel,
        out_shape=(whole,) * 4 + (strip, whole),
        cost_estimate=WORK,
        in_specs=[VMEM] * (7 + len(beside)),
        out_specs=(VMEM,) * 6,
        compiler_params=PARAMS,
        name="inner_cells",
    )(*cells, extinction, step_fed, step_auto, *beside)

    corner = f32((4, columns))
    corners = pl.pallas_call(
        corner_kernel,
        out_shape=(corner,) * len(along_rows),
        in_specs=[VMEM] * 2 + [pl.BlockSpec(memory_space=pl.ANY)],
        out_specs=(VMEM,) * len(along_rows),
        compiler_params=PARAMS,
        name="corner_rows",
    )(*far, inner[4])
    corners = [paired(value, pairs) for value, pairs in zip(corners, along_rows)]
    fed, auto, middle = pl.pallas_call(
        second_kernel,
        out_shape=(held, held, f32((5, rows, columns))),
        in_specs=[VMEM] * 5 + [SMEM] + [VMEM] * 7,
        out_specs=(VMEM,) * 3,
        compiler_params=PARAMS,
        name="second_step",
    )(*cells, fade, palette, *inner, *far)

    block = columns // count
    group = packing(rows, block)
    part = f32((count, 4 * rows // group, LANES) if group else (4, rows, columns))
    fed, auto, part = pl.pallas_call(
        functools.partial(shade_kernel, count),
        out_shape=(held, held, part),
        in_specs=[VMEM] * 3 + [SMEM] + [VMEM] * (1 + len(corners)),
        out_specs=(VMEM,) * 3,
        input_output_aliases={0: 0, 1: 1},
        compiler_params=PARAMS,
        name="shading",
    )(fed, auto, fade, palette, middle, *corners)
    if not group:
        part = jnp.transpose(part.reshape(4 * rows, count, block), (1, 0, 2))
    part = lax.all_to_all(part, "depth", 0, 0)
    image, fed, auto = pl.pallas_call(
        functools.partial(last_kernel, group or 1),
        out_shape=(f32((4, rows, block)), whole, whole),
        in_specs=[VMEM] * 3,
        out_specs=(VMEM, HBM, HBM),
        scratch_shapes=[pltpu.SemaphoreType.DMA((2,))],
        compiler_params=PARAMS,
        name="front_to_back",
    )(part, fed, auto)
    return fed, auto, image


def solution(mesh):
    cells = P("depth", "rows", None)
    return jax.shard_map(
        body,
        mesh=mesh,
        in_specs=(cells,) * 5 + (P(),),
        out_specs=(cells, cells, P(None, "rows", "depth")),
        check_vma=False,
    )
```

time: 40.3 us -> 39.1 us (0.970)
  local copies, waits for them, and re-layouts: 3.8 us -> 0.7 us
  starting transfers between devices: 6.19 us -> 3.64 us
  Pallas kernels: 3.37 us -> 5.85 us
  blocking collectives: 16.2 us -> 18.2 us
    unnamed x14 -> x12, local copies, waits for them, and re-layouts: 3.8 us -> 0.7 us
    ppermute x5 -> x4, starting transfers between devices: 6.19 us -> 3.64 us  [paired(): return lax.ppermute(value, ('depth', 'rows'), pairs)]
    pallas_call x4 -> x7, Pallas kernels: 3.37 us -> 5.85 us  [the longest x1 1.52 us: body(): pl.pallas_call(beam_kernel, out_shape=(beam, beam), in_specs=[HBM] * 4, o...]
    all_to_all x1, blocking collectives: 16.2 us -> 18.2 us  [body(): part = lax.all_to_all(part, 'depth', 0, 0)]
    ppermute x5 -> x4, waiting for transfers between devices: 9.78 us -> 9.77 us  [paired(): return lax.ppermute(value, ('depth', 'rows'), pairs)]
  transfers between devices with their start and end apart: 5 -> 4, of which waited for: 2 -> 2; matrix products, arithmetic and copies ran while one was open for 0% -> 0% of each run, Pallas kernels for 0% -> 5%
where the time goes in v3:
time: 39.1 us; the launch traced here: 38.9 us
  blocking collectives  18.2 us (47%)
  waiting for transfers between devices  9.77 us (25%)
  Pallas kernels  5.85 us (15%)
  starting transfers between devices  3.64 us (9%)
  between operations  0.74 us (2%)
  local copies, waits for them, and re-layouts  0.7 us (2%)
    all_to_all x1, blocking collectives, body(): part = lax.all_to_all(part, 'depth', 0, 0)  18.2 us
    ppermute x4, waiting for transfers between devices, paired(): return lax.ppermute(value, ('depth', 'rows'), pairs)  9.77 us
    ppermute x4, starting transfers between devices, paired(): return lax.ppermute(value, ('depth', 'rows'), pairs)  3.64 us
    pallas_call x1, Pallas kernels, body(): pl.pallas_call(beam_kernel, out_shape=(beam, beam), in_specs=[HBM] * 4, o...  1.52 us
    pallas_call x1, Pallas kernels, body(): pl.pallas_call(functools.partial(last_kernel, group or 1), out_shape=(f32...  1.43 us
    pallas_call x1, Pallas kernels, body(): pl.pallas_call(second_kernel, out_shape=(held, held, f32((5, rows, column...  1.11 us
    pallas_call x1, Pallas kernels, body(): pl.pallas_call(functools.partial(shade_kernel, count), out_shape=(held, h...  0.96 us
  transfers between devices with their start and end apart: 4, of which 2 were waited for; matrix products, arithmetic and copies ran while one was open for 0% of the time, Pallas kernels for 5%

profile of v3, /device:TPU:0, one launch (start us, length us, event | category | flops | bytes accessed | tf_op | source)
XLA Modules:
  0.0 38.9 jit_solution(566132594943019896)
XLA Ops:
  0.6 0.0 copy-start.3
  0.6 0.0 copy-start.2
  0.7 0.0 copy-start.1
  0.7 0.0 copy-start
  0.7 1.5 %depth_messages.1 = (f32[4,16,1024]{2,1,0:T(8,128)S(1)}, f32[4,16,1024]{2,1,0:T(8,128)S(1)}) custom-call(f32[4,16,1024]{2,1,0:T(8,128)} %refs_0_.1, f32[4,16,1024]{2,1,0:T(8,128)} %refs_1_.1, f32[4,16,1024]{2,1,0:T(8,128)} %refs_2_.1, f32[4,16,1024]{2,1,0:T(8,128)} %refs_3_.1), custom_call_target="tpu_custom_call" | custom-call | tf_op jit(solution)/shard_map/depth_messages/pallas_call | solution.py:374
  2.2 3.0 %collective-permute-start.1 = (f32[4,16,1024]{2,1,0:T(8,128)S(1)}, f32[4,16,1024]{2,1,0:T(8,128)S(1)}, u32[]{:S(2)}, u32[]{:S(2)}) collective-permute-start(f32[4,16,1024]{2,1,0:T(8,128)S(1)} %get-tuple-element.32), channel_id=1, source_target_pairs={{0,2},{1,3},{2,0},{3,1},{4,6},{5,7},{6,4},{7,5},{8,10},{9,11},{10,... | collective-permute-start | bytes 786440 | tf_op jit(solution)/shard_map/ppermute | solution.py:42
  5.2 0.0 copy-start.4
  5.2 0.0 collective-permute-start.2
  5.2 0.0 copy-done.3
  5.2 0.0 copy-done.2
  5.2 0.0 copy-done.1
  5.2 0.0 copy-done
  5.2 0.5 %row_messages.1 = (f32[4,16,1024]{2,1,0:T(8,128)S(1)}, f32[4,16,1024]{2,1,0:T(8,128)S(1)}, f32[16,1024]{1,0:T(8,128)S(1)}) custom-call(f32[4,16,1024]{2,1,0:T(8,128)S(1)} %copy-done, f32[4,16,1024]{2,1,0:T(8,128)S(1)} %copy-done.1, f32[4,16,1024]{2,1,0:T(8,128)S(1)} %copy-done.2, f32[4,16,1024]{2,1,0:T(8,128)S(1)} %copy-done.3), custom_call_target="tpu_custom_call" | custom-call | flops 20000000 | bytes 4000000 | tf_op jit(solution)/shard_map/row_messages/pallas_call | solution.py:386
  5.7 0.6 %collective-permute-start = (f32[16,1024]{1,0:T(8,128)S(1)}, f32[16,1024]{1,0:T(8,128)S(1)}, u32[]{:S(2)}, u32[]{:S(2)}) collective-permute-start(f32[16,1024]{1,0:T(8,128)S(1)} %get-tuple-element.25), channel_id=1, source_target_pairs={{0,1},{2,3},{4,5},{6,7},{8,9},{10,11},{12,13},{14,15},{16,17},{18,... | collective-permute-start | bytes 196616 | tf_op jit(solution)/shard_map/ppermute | solution.py:42
  6.3 0.9 %collective-permute-done.refs_0_ = f32[16,1024]{1,0:T(8,128)S(1)} collective-permute-done((f32[16,1024]{1,0:T(8,128)S(1)}, f32[16,1024]{1,0:T(8,128)S(1)}, u32[]{:S(2)}, u32[]{:S(2)}) %collective-permute-start) | collective-permute-done | bytes 65568 | tf_op jit(solution)/shard_map/ppermute | solution.py:42
  7.2 0.0 copy-done.4
  7.2 0.3 inner_cells.1
  7.5 8.9 %collective-permute-done.1.refs_11_.a_ref = f32[4,16,1024]{2,1,0:T(8,128)S(1)} collective-permute-done((f32[4,16,1024]{2,1,0:T(8,128)S(1)}, f32[4,16,1024]{2,1,0:T(8,128)S(1)}, u32[]{:S(2)}, u32[]{:S(2)}) %collective-permute-start.1) | collective-permute-done | bytes 262176 | tf_op jit(solution)/shard_map/ppermute | solution.py:42
  16.4 0.0 collective-permute-done.2.refs_12_.b_ref
  16.4 0.1 collective-permute-start.3
  16.5 0.0 copy-start.5
  16.5 0.7 %copy-done.5 = f32[3,3]{1,0:T(4,128)S(1)} copy-done((f32[3,3]{1,0:T(4,128)S(1)}, f32[3,3]{1,0:T(4,128)}, u32[]{:S(2)}) %copy-start.5) | copy-done | bytes 60
  17.2 1.1 %second_step.1 = (f32[4,16,1024]{2,1,0:T(8,128)S(1)}, f32[4,16,1024]{2,1,0:T(8,128)S(1)}, f32[5,16,1024]{2,1,0:T(8,128)S(1)}) custom-call(f32[4,16,1024]{2,1,0:T(8,128)S(1)} %copy-done, f32[4,16,1024]{2,1,0:T(8,128)S(1)} %copy-done.1, f32[4,16,1024]{2,1,0:T(8,128)S(1)} %copy-done.2, f32[4,16,1024]{2,1,0:T(8,128)S(1)} %copy-done.3, ...), custom_call_target="tpu_custom_call" | custom-call | tf_op jit(solution)/shard_map/second_step/pallas_call | solution.py:416
  18.3 0.0 collective-permute-done.3.refs_0_
  18.3 1.0 %shading.1 = (f32[4,16,1024]{2,1,0:T(8,128)S(1)}, f32[4,16,1024]{2,1,0:T(8,128)S(1)}, f32[16,32,128]{2,1,0:T(8,128)S(1)}) custom-call(f32[4,16,1024]{2,1,0:T(8,128)S(1)} %get-tuple-element.34.fed_two, f32[4,16,1024]{2,1,0:T(8,128)S(1)} %get-tuple-element.35.auto_two, ...), custom_call_target="tpu_custom_call", output_to_operand_aliasing={{0}: (0, {}), {1}: (1, {})} | custom-call | tf_op jit(solution)/shard_map/shading/pallas_call | solution.py:428
  19.3 18.2 %all_to_all.5.part_ref = f32[16,32,128]{2,1,0:T(8,128)S(1)} all-to-all(f32[16,32,128]{2,1,0:T(8,128)S(1)} %get-tuple-element.37), channel_id=1, replica_groups=mesh['depth'=16,'rows'=2] {'depth'}, dimensions={0} | all-to-all | bytes 524288 | tf_op jit(solution)/shard_map/all_to_all | solution.py:439
  37.4 1.4 %front_to_back.1 = (f32[4,16,64]{2,1,0:T(8,128)}, f32[4,16,1024]{2,1,0:T(8,128)}, f32[4,16,1024]{2,1,0:T(8,128)}) custom-call(f32[16,32,128]{2,1,0:T(8,128)S(1)} %all_to_all.5.part_ref, f32[4,16,1024]{2,1,0:T(8,128)S(1)} %get-tuple-element.38.fed_ref, f32[4,16,1024]{2,1,0:T(8,128)S(1)} %get-tuple-element.39.auto_ref), custom_call_target="tpu_custom_call" | custom-call | tf_op jit(solution)/shard_map/front_to_back/pallas_call | solution.py:440
  (1 shorter events, 0.0 us)
Async XLA Ops:
  0.6 4.6 %copy-start.3 = (f32[4,16,1024]{2,1,0:T(8,128)S(1)}, f32[4,16,1024]{2,1,0:T(8,128)}, u32[]{:S(2)}) copy-start(f32[4,16,1024]{2,1,0:T(8,128)} %refs_3_.1) | copy-start | bytes 786436
  0.6 4.6 %copy-start.2 = (f32[4,16,1024]{2,1,0:T(8,128)S(1)}, f32[4,16,1024]{2,1,0:T(8,128)}, u32[]{:S(2)}) copy-start(f32[4,16,1024]{2,1,0:T(8,128)} %refs_2_.1) | copy-start | bytes 786436
  0.7 4.6 %copy-start.1 = (f32[4,16,1024]{2,1,0:T(8,128)S(1)}, f32[4,16,1024]{2,1,0:T(8,128)}, u32[]{:S(2)}) copy-start(f32[4,16,1024]{2,1,0:T(8,128)} %refs_1_.1) | copy-start | bytes 786436
  0.7 4.6 %copy-start = (f32[4,16,1024]{2,1,0:T(8,128)S(1)}, f32[4,16,1024]{2,1,0:T(8,128)}, u32[]{:S(2)}) copy-start(f32[4,16,1024]{2,1,0:T(8,128)} %refs_0_.1) | copy-start | bytes 786436
  2.2 14.2 %collective-permute-start.1 = (f32[4,16,1024]{2,1,0:T(8,128)S(1)}, f32[4,16,1024]{2,1,0:T(8,128)S(1)}, u32[]{:S(2)}, u32[]{:S(2)}) collective-permute-start(f32[4,16,1024]{2,1,0:T(8,128)S(1)} %get-tuple-element.32), channel_id=1, source_target_pairs={{0,2},{1,3},{2,0},{3,1},{4,6},{5,7},{6,4},{7,5},{8,10},{9,11},{10,... | collective-permute-start | bytes 786440 | tf_op jit(solution)/shard_map/ppermute | solution.py:42
  5.2 2.0 %copy-start.4 = (f32[4,16,1024]{2,1,0:T(8,128)S(1)}, f32[4,16,1024]{2,1,0:T(8,128)}, u32[]{:S(2)}) copy-start(f32[4,16,1024]{2,1,0:T(8,128)} %e_ref.1) | copy-start | bytes 786436
  5.2 11.2 %collective-permute-start.2 = (f32[4,16,1024]{2,1,0:T(8,128)S(1)}, f32[4,16,1024]{2,1,0:T(8,128)S(1)}, u32[]{:S(2)}, u32[]{:S(2)}) collective-permute-start(f32[4,16,1024]{2,1,0:T(8,128)S(1)} %get-tuple-element.33), channel_id=1, source_target_pairs={{0,1},{1,0},{2,4},{3,5},{4,2},{5,3},{6,8},{7,9},{8,6},{9,7},{10,12... | collective-permute-start | bytes 786440 | tf_op jit(solution)/shard_map/ppermute | solution.py:42
  5.7 1.5 %collective-permute-start = (f32[16,1024]{1,0:T(8,128)S(1)}, f32[16,1024]{1,0:T(8,128)S(1)}, u32[]{:S(2)}, u32[]{:S(2)}) collective-permute-start(f32[16,1024]{1,0:T(8,128)S(1)} %get-tuple-element.25), channel_id=1, source_target_pairs={{0,1},{2,3},{4,5},{6,7},{8,9},{10,11},{12,13},{14,15},{16,17},{18,... | collective-permute-start | bytes 196616 | tf_op jit(solution)/shard_map/ppermute | solution.py:42
  16.4 1.9 %collective-permute-start.3 = (f32[4,1024]{1,0:T(4,128)S(1)}, f32[4,1024]{1,0:T(4,128)S(1)}, u32[]{:S(2)}, u32[]{:S(2)}) collective-permute-start(f32[4,1024]{1,0:T(4,128)S(1)} %corner_rows.1), channel_id=1, source_target_pairs={{0,1},{2,3},{4,5},{6,7},{8,9},{10,11},{12,13},{14,15},{16,17},{18,... | collective-permute-start | bytes 49160 | tf_op jit(solution)/shard_map/ppermute | solution.py:42
  16.5 0.7 %copy-start.5 = (f32[3,3]{1,0:T(4,128)S(1)}, f32[3,3]{1,0:T(4,128)}, u32[]{:S(2)}) copy-start(f32[3,3]{1,0:T(4,128)} %palette.1) | copy-start | bytes 112

commit v4 on v3

--- a/solution.py
+++ b/solution.py
@@ -17,6 +17,7 @@
 VMEM = pl.BlockSpec(memory_space=pltpu.VMEM)
 SMEM = pl.BlockSpec(memory_space=pltpu.SMEM)
 HBM = pl.BlockSpec(memory_space=pltpu.HBM)
+ANY = pl.BlockSpec(memory_space=pl.ANY)
 WORK = pl.CostEstimate(flops=20_000_000, bytes_accessed=4_000_000, transcendentals=0)
 PARAMS = pltpu.CompilerParams(vmem_limit_bytes=24 * 1024 * 1024)
 
@@ -80,44 +81,45 @@
     return react(s_ref[layer], c_ref[layer], near[0], near[1], feed, kill)
 
 
-def beam_kernel(s_hbm, c_hbm, f_hbm, k_hbm, a_ref, b_ref, s_ref, c_ref, f_ref, k_ref, arrived):
+def old_kernel(s_hbm, c_hbm, a_ref, b_ref, arrived):
     depth = s_hbm.shape[0]
     even = is_even("depth")
-    ends = []
-    for n, towards_next in enumerate((even, jnp.logical_not(even))):
+    copies = []
+    for n, (out, towards_next) in enumerate(((a_ref, even), (b_ref, jnp.logical_not(even)))):
         layer = jnp.where(towards_next, depth - 1, 0)
-        places = [layer]
-        if depth > 1:
-            places.append(jnp.where(towards_next, depth - 2, 1))
-        copies = []
-        for m, place in enumerate(places):
-            for i, (hbm, ref) in enumerate(((s_hbm, s_ref), (c_hbm, c_ref))):
-                copies.append(pltpu.make_async_copy(hbm.at[place], ref.at[2 * n + m], arrived.at[n, 2 * m + i]))
-        for i, (hbm, ref) in enumerate(((f_hbm, f_ref), (k_hbm, k_ref))):
-            copies.append(pltpu.make_async_copy(hbm.at[layer], ref.at[n], arrived.at[n, 4 + i]))
-        for copy in copies:
-            copy.start()
-        ends.append(copies)
-    for n, out in enumerate((a_ref, b_ref)):
-        for copy in ends[n]:
-            copy.wait()
-        out[0] = s_ref[2 * n]
-        out[1] = c_ref[2 * n]
-        inner = [2 * n + 1] if depth > 1 else []
-        out[2], out[3] = partial_step(s_ref, c_ref, f_ref[n], k_ref[n], 2 * n, inner)
-
-
-def strip_kernel(s_ref, c_ref, f_ref, k_ref, ps_ref, pc_ref, *strips):
+        for i, hbm in enumerate((s_hbm, c_hbm)):
+            copies.append(pltpu.make_async_copy(hbm.at[layer], out.at[i], arrived.at[n, i]))
+    for copy in copies:
+        copy.start()
+    for copy in copies:
+        copy.wait()
+
+
+def partial_kernel(*refs):
+    held = refs[6:11]
+    s_ref, c_ref, f_ref, k_ref, _ = held
+    ps_ref, pc_ref, a_ref, b_ref, *strips, arrived = refs[11:]
+    copies = [pltpu.make_async_copy(refs[n], held[n], arrived.at[n]) for n in range(5)]
+    for copy in copies:
+        copy.start()
+    for copy in copies[:4]:
+        copy.wait()
     depth, rows, _ = s_ref.shape
     for layer in range(depth):
         inner = [other for other in (layer - 1, layer + 1) if 0 <= other < depth]
         ps_ref[layer], pc_ref[layer] = partial_step(s_ref, c_ref, f_ref[layer], k_ref[layer], layer, inner)
+    even = is_even("depth")
+    for out, towards_next in ((a_ref, even), (b_ref, jnp.logical_not(even))):
+        layer = jnp.where(towards_next, depth - 1, 0)
+        out[0] = ps_ref[layer]
+        out[1] = pc_ref[layer]
     even = is_even("rows")
     for out, towards_next in zip(strips, (even, jnp.logical_not(even))):
         for n, ref in enumerate((s_ref, c_ref, ps_ref, pc_ref)):
             for layer in range(depth):
                 head, tail = ref[layer, 0:1], ref[layer, rows - 1 : rows]
                 out[n * depth + layer : n * depth + layer + 1] = jnp.where(towards_next, tail, head)
+    copies[4].wait()
 
 
 def sides(axis, refs, read):
@@ -141,8 +143,8 @@
     return react(fields[0][layer], fields[1][layer], near[0], near[1], feed, kill)
 
 
-def inner_kernel(s_ref, c_ref, f_ref, k_ref, e_ref, ps_ref, pc_ref, *refs):
-    *beside, fed_one, auto_one, fed_two, auto_two, outer_ref, fade_ref = refs
+def inner_kernel(s_ref, c_ref, f_ref, k_ref, ps_ref, pc_ref, palette, *refs):
+    *beside, fed_one, auto_one, fed_two, auto_two, outer_ref, mix_ref = refs
     depth, rows, columns = s_ref.shape
     row = lax.broadcasted_iota(jnp.int32, (rows, columns), 0)
     index, last = lax.axis_index("rows"), lax.axis_size("rows") - 1
@@ -173,8 +175,10 @@
     for layer in range(1, depth - 1):
         others = [(values[layer - 1], values[layer + 1]) for values in fields]
         fed_two[layer], auto_two[layer] = step_two(fields, outside, layer, others, f_ref[layer], k_ref[layer])
-    for layer in range(depth):
-        fade_ref[layer] = -e_ref[layer]
+    for channel in range(3):
+        for n, scale in enumerate((8.0, 8.0, 1.0)):
+            at = 3 * channel + n
+            mix_ref[at : at + 1] = jnp.full((1, columns), scale * palette[channel, n], jnp.float32)
 
 
 def corner_kernel(a_ref, b_ref, _, *outs):
@@ -192,8 +196,8 @@
 
 
 class Shading:
-    def __init__(self, palette):
-        self.palette = palette
+    def __init__(self, mix_ref):
+        self.mix = [[mix_ref[3 * k + n : 3 * k + n + 1] for n in range(3)] for k in range(3)]
         self.gather = None
         self.before = None
 
@@ -204,55 +208,52 @@
         self.gather = [total + self.before * piece for total, piece in zip(self.gather, pieces)]
         self.before = self.before * passing
 
-    def add(self, fed, auto, fade):
-        passing = jnp.exp(fade * (0.25 + 4.0 * auto * auto))
+    def add(self, fed, auto, extinction):
+        passing = jnp.exp(-extinction * (0.25 + 4.0 * auto * auto))
         opacity = 1.0 - passing
         pieces = []
-        for channel in range(3):
-            level = (
-                (8.0 * self.palette[channel, 0]) * (fed - 0.65)
-                + (8.0 * self.palette[channel, 1]) * (auto - 0.25)
-                + self.palette[channel, 2]
-            )
+        for fed_mix, auto_mix, offset in self.mix:
+            level = fed_mix * (fed - 0.65) + auto_mix * (auto - 0.25) + offset
             pieces.append(opacity / (1.0 + jnp.exp(-level)))
         self.put(pieces + [opacity], passing)
 
 
-def second_kernel(*refs):
-    s_ref, c_ref, f_ref, k_ref, fade_ref, palette = refs[:6]
+def second_kernel(row_pairings, *refs):
+    s_ref, c_ref, f_ref, k_ref, e_ref, mix_ref = refs[:6]
     fed_one, auto_one, fed_mid, auto_mid, outer_ref = refs[6:11]
     far = refs[11:13]
-    fed_two, auto_two, middle_ref = refs[13:]
-    depth = s_ref.shape[0]
+    corners = refs[13 : 13 + row_pairings]
+    fed_two, auto_two, middle_ref = refs[13 + row_pairings :]
+    depth, rows, columns = s_ref.shape
+    row = lax.broadcasted_iota(jnp.int32, (rows, columns), 0)
     index, last = lax.axis_index("depth"), lax.axis_size("depth") - 1
     inside = (index > 0, index < last)
+    ends = (0, depth - 1)
     fields, outside, beyond, far_old = [], [], [], []
     for n, (old, one, reach) in enumerate(((s_ref, fed_one, reach_fast), (c_ref, auto_one, reach_slow))):
         old_far = sides("depth", far, lambda ref: ref[n])
-        new_far = sides("depth", far, lambda ref: ref[2 + n])
         far_old.append(old_far)
-        beyond.append(
-            [
-                jnp.where(inside[end], new_far[end] + reach * old[layer], 0.0)
-                for end, layer in enumerate((0, depth - 1))
-            ]
-        )
+        beyond.append([])
         values, rows_outside = {}, {}
-        for layer in (0, depth - 1):
+        for end, layer in enumerate(ends):
+            at = 2 * n + end
+            above, below = sides("rows", corners, lambda ref: ref[at : at + 1])
+            corner = jnp.where(row == 0, above, 0.0) + jnp.where(row == rows - 1, below, 0.0)
+            beyond[n].append(jnp.where(inside[end], reach * old[layer], 0.0) + (2.0 * reach) * corner)
+        for layer in set(ends):
             near = 0.0
-            if layer == 0:
-                near = near + old_far[0]
-            if layer == depth - 1:
-                near = near + old_far[1]
+            for end in range(2):
+                if layer == ends[end]:
+                    near = near + old_far[end]
             values[layer] = one[layer] + reach * near
             rows_outside[layer] = [
                 outer_ref[(n * 2 + side) * depth + layer : (n * 2 + side) * depth + layer + 1] for side in range(2)
             ]
         fields.append(values)
         outside.append(rows_outside)
-    shading = Shading(palette)
+    shading = Shading(mix_ref)
     for layer in range(depth):
-        if layer in (0, depth - 1):
+        if layer in ends:
             others = []
             for n, one in enumerate((fed_one, auto_one)):
                 others.append(
@@ -268,7 +269,7 @@
                 if layer == beside:
                     fed = fed + (reach_fast * reach_fast) * far_old[0][end]
                     auto = auto + (reach_slow * reach_slow) * far_old[1][end]
-            shading.add(fed, auto, fade_ref[layer])
+            shading.add(fed, auto, e_ref[layer])
         fed_two[layer] = fed
         auto_two[layer] = auto
     if shading.gather is not None:
@@ -276,30 +277,22 @@
             middle_ref[n] = value
 
 
-def shade_kernel(depth_count, fed_two, auto_two, fade_ref, palette, middle_ref, *refs):
-    *corners, fed_out, auto_out, part_ref = refs
+def shade_kernel(depth_count, fed_two, auto_two, e_ref, mix_ref, middle_ref, a_ref, b_ref, fed_out, auto_out, part_ref):
     depth, rows, columns = fed_two.shape
-    row = lax.broadcasted_iota(jnp.int32, (rows, columns), 0)
-    shading = Shading(palette)
+    new_far = [sides("depth", (a_ref, b_ref), lambda ref: ref[n]) for n in range(2)]
+    shading = Shading(mix_ref)
     for layer in range(depth):
-        if layer not in (0, depth - 1):
-            if layer == 1:
-                shading.put([middle_ref[n] for n in range(4)], middle_ref[4])
-            continue
-        values = []
-        for n, (two, out, reach) in enumerate(
-            ((fed_two, fed_out, reach_fast), (auto_two, auto_out, reach_slow))
-        ):
-            value = two[layer]
+        fed, auto = fed_two[layer], auto_two[layer]
+        if layer in (0, depth - 1):
             for end, place in enumerate((0, depth - 1)):
                 if layer == place:
-                    at = 2 * n + end
-                    above, below = sides("rows", corners, lambda ref: ref[at : at + 1])
-                    near = jnp.where(row == 0, above, 0.0) + jnp.where(row == rows - 1, below, 0.0)
-                    value = value + (2.0 * reach * reach) * near
-            out[layer] = value
-            values.append(value)
-        shading.add(values[0], values[1], fade_ref[layer])
+                    fed = fed + reach_fast * new_far[0][end]
+                    auto = auto + reach_slow * new_far[1][end]
+            shading.add(fed, auto, e_ref[layer])
+        elif layer == 1:
+            shading.put([middle_ref[n] for n in range(4)], middle_ref[4])
+        fed_out[layer] = fed
+        auto_out[layer] = auto
     gather = shading.gather
 
     block = columns // depth_count
@@ -332,13 +325,13 @@
     return group if rows % (group * SUBLANES) == 0 else 0
 
 
-def last_kernel(group, part_ref, fed_ref, auto_ref, image_ref, fed_out, auto_out, written):
+def last_kernel(group, part_ref, fed_ref, auto_ref, image_out, fed_out, auto_out, image_ref, written):
     copies = [
         pltpu.make_async_copy(ref, out, written.at[n])
-        for n, (ref, out) in enumerate(((fed_ref, fed_out), (auto_ref, auto_out)))
+        for n, (ref, out) in enumerate(((fed_ref, fed_out), (auto_ref, auto_out), (image_ref, image_out)))
     ]
-    for copy in copies:
-        copy.start()
+    copies[0].start()
+    copies[1].start()
     _, rows, block = image_ref.shape
     high = rows // group
     count = part_ref.shape[0]
@@ -353,6 +346,7 @@
     for channel in range(4):
         for q in range(group):
             image_ref[channel, q * high : (q + 1) * high] = total[channel][:, q * block : (q + 1) * block]
+    copies[2].start()
     for copy in copies:
         copy.wait()
 
@@ -368,81 +362,84 @@
     along_rows = [pairs for pairs in pairings("rows", "depth") if pairs is not None]
 
     cells = (substrate, catalyst, feed_rate, kill_rate)
-    beam = f32((4, rows, columns))
-    layers = lambda count: pltpu.VMEM((count, rows, columns), jnp.float32)
-    held = layers(depth)
-    beams = pl.pallas_call(
-        beam_kernel,
-        out_shape=(beam, beam),
-        in_specs=[HBM] * 4,
+    pair = f32((2, rows, columns))
+    in_hbm = lambda x: pltpu.with_memory_space_constraint(x, pltpu.HBM)
+    old_beams = pl.pallas_call(
+        old_kernel,
+        out_shape=(pair, pair),
+        in_specs=[HBM] * 2,
         out_specs=(VMEM, VMEM),
-        scratch_shapes=[layers(4), layers(4), layers(2), layers(2), pltpu.SemaphoreType.DMA((2, 6))],
-        compiler_params=PARAMS,
-        name="depth_messages",
-    )(*(pltpu.with_memory_space_constraint(x, pltpu.HBM) for x in cells))
-    far = [paired(value, pairs) for value, pairs in zip(beams, along_depth)]
+        scratch_shapes=[pltpu.SemaphoreType.DMA((2, 2))],
+        compiler_params=PARAMS,
+        name="old_layers",
+    )(in_hbm(substrate), in_hbm(catalyst))
+    old_far = [paired(value, pairs) for value, pairs in zip(old_beams, along_depth)]
 
     strip = f32((4 * depth, columns))
-    step_fed, step_auto, *strips = pl.pallas_call(
-        strip_kernel,
-        out_shape=(whole, whole) + (strip,) * len(along_rows),
+    outs = pl.pallas_call(
+        partial_kernel,
+        out_shape=(whole,) * 7 + (pair, pair) + (strip,) * len(along_rows),
+        in_specs=[HBM] * 5 + [ANY],
+        out_specs=(VMEM,) * (9 + len(along_rows)),
+        scratch_shapes=[pltpu.SemaphoreType.DMA((5,))],
         cost_estimate=WORK,
-        in_specs=[VMEM] * 4,
-        out_specs=(VMEM,) * (2 + len(along_rows)),
-        compiler_params=PARAMS,
-        name="row_messages",
-    )(*cells)
-    beside = [paired(value, pairs) for value, pairs in zip(strips, along_rows)]
-    *inner, fade = pl.pallas_call(
+        compiler_params=PARAMS,
+        name="partial_step",
+    )(*(in_hbm(x) for x in cells), in_hbm(extinction), old_beams[0])
+    cells, extinction, partial = outs[:4], outs[4], outs[5:7]
+    new_far = [paired(value, pairs) for value, pairs in zip(outs[7:9], along_depth)]
+    beside = [paired(value, pairs) for value, pairs in zip(outs[9:], along_rows)]
+    *inner, mix = pl.pallas_call(
         inner_kernel,
-        out_shape=(whole,) * 4 + (strip, whole),
+        out_shape=(whole,) * 4 + (strip, f32((9, columns))),
+        in_specs=[VMEM] * 6 + [SMEM] + [VMEM] * len(beside),
+        out_specs=(VMEM,) * 6,
         cost_estimate=WORK,
-        in_specs=[VMEM] * (7 + len(beside)),
-        out_specs=(VMEM,) * 6,
         compiler_params=PARAMS,
         name="inner_cells",
-    )(*cells, extinction, step_fed, step_auto, *beside)
+    )(*cells, *partial, palette, *beside)
 
     corner = f32((4, columns))
     corners = pl.pallas_call(
         corner_kernel,
         out_shape=(corner,) * len(along_rows),
-        in_specs=[VMEM] * 2 + [pl.BlockSpec(memory_space=pl.ANY)],
+        in_specs=[VMEM] * 2 + [ANY],
         out_specs=(VMEM,) * len(along_rows),
         compiler_params=PARAMS,
         name="corner_rows",
-    )(*far, inner[4])
+    )(*old_far, inner[4])
     corners = [paired(value, pairs) for value, pairs in zip(corners, along_rows)]
     fed, auto, middle = pl.pallas_call(
-        second_kernel,
-        out_shape=(held, held, f32((5, rows, columns))),
-        in_specs=[VMEM] * 5 + [SMEM] + [VMEM] * 7,
+        functools.partial(second_kernel, len(corners)),
+        out_shape=(whole, whole, f32((5, rows, columns))),
+        in_specs=[VMEM] * (13 + len(corners)),
         out_specs=(VMEM,) * 3,
+        cost_estimate=WORK,
         compiler_params=PARAMS,
         name="second_step",
-    )(*cells, fade, palette, *inner, *far)
+    )(*cells, extinction, mix, *inner, *old_far, *corners)
 
     block = columns // count
     group = packing(rows, block)
-    part = f32((count, 4 * rows // group, LANES) if group else (4, rows, columns))
+    held = pltpu.VMEM(whole.shape, jnp.float32)
     fed, auto, part = pl.pallas_call(
         functools.partial(shade_kernel, count),
-        out_shape=(held, held, part),
-        in_specs=[VMEM] * 3 + [SMEM] + [VMEM] * (1 + len(corners)),
+        out_shape=(held, held, f32((count, 4 * rows // group, LANES) if group else (4, rows, columns))),
+        in_specs=[VMEM] * 7,
         out_specs=(VMEM,) * 3,
-        input_output_aliases={0: 0, 1: 1},
         compiler_params=PARAMS,
         name="shading",
-    )(fed, auto, fade, palette, middle, *corners)
+    )(fed, auto, extinction, mix, middle, *new_far)
     if not group:
         part = jnp.transpose(part.reshape(4 * rows, count, block), (1, 0, 2))
     part = lax.all_to_all(part, "depth", 0, 0)
+    image = f32((4, rows, block))
     image, fed, auto = pl.pallas_call(
         functools.partial(last_kernel, group or 1),
-        out_shape=(f32((4, rows, block)), whole, whole),
+        out_shape=(image, whole, whole),
         in_specs=[VMEM] * 3,
-        out_specs=(VMEM, HBM, HBM),
-        scratch_shapes=[pltpu.SemaphoreType.DMA((2,))],
+        out_specs=(HBM,) * 3,
+        scratch_shapes=[pltpu.VMEM(image.shape, jnp.float32), pltpu.SemaphoreType.DMA((3,))],
         compiler_params=PARAMS,
         name="front_to_back",
     )(part, fed, auto)

time: 39.1 us -> 34.9 us (0.89)
  waiting for transfers between devices: 9.77 us -> 6.27 us
  blocking collectives: 18.2 us -> 16.4 us
  starting transfers between devices: 3.64 us -> 5.2 us
  Pallas kernels: 5.85 us -> 5.36 us
    ppermute x4 -> x6, waiting for transfers between devices: 9.77 us -> 6.27 us  [paired(): return lax.ppermute(value, ('depth', 'rows'), pairs)]
    all_to_all x1, blocking collectives: 18.2 us -> 16.4 us  [body(): part = lax.all_to_all(part, 'depth', 0, 0)]
    ppermute x4 -> x6, starting transfers between devices: 3.64 us -> 5.2 us  [paired(): return lax.ppermute(value, ('depth', 'rows'), pairs)]
    pallas_call x1, Pallas kernels: 0.96 us -> 0.37 us  [body(): pl.pallas_call(functools.partial(shade_kernel, count), out_shape=(held, h...]
  transfers between devices with their start and end apart: 4 -> 6, of which waited for: 2 -> 4; matrix products, arithmetic and copies ran while one was open for 0% -> 0% of each run, Pallas kernels for 5% -> 9%
where the time goes in v4:
time: 34.9 us; the launch traced here: 34.6 us
  blocking collectives  16.4 us (47%)
  waiting for transfers between devices  6.27 us (18%)
  Pallas kernels  5.36 us (15%)
  starting transfers between devices  5.2 us (15%)
  between operations  0.7 us (2%)
  local copies, waits for them, and re-layouts  0.68 us (2%)
    all_to_all x1, blocking collectives, body(): part = lax.all_to_all(part, 'depth', 0, 0)  16.4 us
    ppermute x6, waiting for transfers between devices, paired(): return lax.ppermute(value, ('depth', 'rows'), pairs)  6.27 us
    ppermute x6, starting transfers between devices, paired(): return lax.ppermute(value, ('depth', 'rows'), pairs)  5.2 us
    pallas_call x1, Pallas kernels, body(): pl.pallas_call(partial_kernel, out_shape=(whole,) * 7 + (pair, pair) + (s...  1.73 us
    pallas_call x1, Pallas kernels, body(): pl.pallas_call(old_kernel, out_shape=(pair, pair), in_specs=[HBM] * 2, ou...  0.98 us
    pallas_call x1, Pallas kernels, body(): pl.pallas_call(inner_kernel, out_shape=(whole,) * 4 + (strip, f32((9, col...  0.89 us
    pallas_call x1, Pallas kernels, body(): pl.pallas_call(functools.partial(last_kernel, group or 1), out_shape=(ima...  0.82 us
  transfers between devices with their start and end apart: 6, of which 4 were waited for; matrix products, arithmetic and copies ran while one was open for 0% of the time, Pallas kernels for 9%

profile of v4, /device:TPU:0, one launch (start us, length us, event | category | flops | bytes accessed | tf_op | source)
XLA Modules:
  0.0 34.6 jit_solution(12133965047316641359)
XLA Ops:
  0.6 1.0 %old_layers.1 = (f32[2,16,1024]{2,1,0:T(8,128)S(1)}, f32[2,16,1024]{2,1,0:T(8,128)S(1)}) custom-call(f32[4,16,1024]{2,1,0:T(8,128)} %refs_0_.1, f32[4,16,1024]{2,1,0:T(8,128)} %refs_1_.1), custom_call_target="tpu_custom_call" | custom-call | tf_op jit(solution)/shard_map/old_layers/pallas_call | solution.py:367
  1.6 0.5 %collective-permute-start.2 = (f32[2,16,1024]{2,1,0:T(8,128)S(1)}, f32[2,16,1024]{2,1,0:T(8,128)S(1)}, u32[]{:S(2)}, u32[]{:S(2)}) collective-permute-start(f32[2,16,1024]{2,1,0:T(8,128)S(1)} %get-tuple-element.45), channel_id=1, source_target_pairs={{0,1},{1,0},{2,4},{3,5},{4,2},{5,3},{6,8},{7,9},{8,6},{9,7},{10,12... | collective-permute-start | bytes 393224 | tf_op jit(solution)/shard_map/ppermute | solution.py:43
  2.1 4.0 %collective-permute-start.1 = (f32[2,16,1024]{2,1,0:T(8,128)S(1)}, f32[2,16,1024]{2,1,0:T(8,128)S(1)}, u32[]{:S(2)}, u32[]{:S(2)}) collective-permute-start(f32[2,16,1024]{2,1,0:T(8,128)S(1)} %get-tuple-element.30.refs_5_), channel_id=1, source_target_pairs={{0,2},{1,3},{2,0},{3,1},{4,6},{5,7},{6,4},{7,5},{8,10},{9,11},{10,... | collective-permute-start | bytes 393224 | tf_op jit(solution)/shard_map/ppermute | solution.py:43
  6.1 1.7 %partial_step.1 = (f32[4,16,1024]{2,1,0:T(8,128)S(1)}, f32[4,16,1024]{2,1,0:T(8,128)S(1)}, f32[4,16,1024]{2,1,0:T(8,128)S(1)}, f32[4,16,1024]{2,1,0:T(8,128)S(1)...) custom-call(f32[4,16,1024]{2,1,0:T(8,128)} %refs_0_.1, ...), custom_call_target="tpu_custom_call" | custom-call | flops 20000000 | bytes 4000000 | tf_op jit(solution)/shard_map/partial_step/pallas_call | solution.py:379
  7.9 0.1 collective-permute-start.4
  7.9 0.1 collective-permute-start.5
  8.0 0.5 %collective-permute-start = (f32[16,1024]{1,0:T(8,128)S(1)}, f32[16,1024]{1,0:T(8,128)S(1)}, u32[]{:S(2)}, u32[]{:S(2)}) collective-permute-start(f32[16,1024]{1,0:T(8,128)S(1)} %get-tuple-element.38), channel_id=1, source_target_pairs={{0,1},{2,3},{4,5},{6,7},{8,9},{10,11},{12,13},{14,15},{16,17},{18,... | collective-permute-start | bytes 196616 | tf_op jit(solution)/shard_map/ppermute | solution.py:43
  8.5 0.9 %collective-permute-done.refs_0_ = f32[16,1024]{1,0:T(8,128)S(1)} collective-permute-done((f32[16,1024]{1,0:T(8,128)S(1)}, f32[16,1024]{1,0:T(8,128)S(1)}, u32[]{:S(2)}, u32[]{:S(2)}) %collective-permute-start) | collective-permute-done | bytes 65568 | tf_op jit(solution)/shard_map/ppermute | solution.py:43
  9.4 0.0 copy-start
  9.4 0.7 %copy-done = f32[3,3]{1,0:T(4,128)S(1)} copy-done((f32[3,3]{1,0:T(4,128)S(1)}, f32[3,3]{1,0:T(4,128)}, u32[]{:S(2)}) %copy-start) | copy-done | bytes 60
  10.1 0.9 %inner_cells.1 = (f32[4,16,1024]{2,1,0:T(8,128)S(1)}, f32[4,16,1024]{2,1,0:T(8,128)S(1)}, f32[4,16,1024]{2,1,0:T(8,128)S(1)}, f32[4,16,1024]{2,1,0:T(8,128)S(1)}...) custom-call(f32[4,16,1024]{2,1,0:T(8,128)S(1)} %get-tuple-element.31.s_ref.refs_0_, ...), custom_call_target="tpu_custom_call" | custom-call | flops 20000000 | bytes 4000000 | tf_op jit(solution)/shard_map/inner_cells/pallas_call | solution.py:392
  11.0 0.0 collective-permute-done.2.b_ref.refs_12_
  11.0 3.8 %collective-permute-done.1.a_ref.refs_11_ = f32[2,16,1024]{2,1,0:T(8,128)S(1)} collective-permute-done((f32[2,16,1024]{2,1,0:T(8,128)S(1)}, f32[2,16,1024]{2,1,0:T(8,128)S(1)}, u32[]{:S(2)}, u32[]{:S(2)}) %collective-permute-start.1) | collective-permute-done | bytes 131104 | tf_op jit(solution)/shard_map/ppermute | solution.py:43
  14.9 0.1 collective-permute-start.3
  15.0 1.2 %collective-permute-done.3.refs_13_ = f32[4,1024]{1,0:T(4,128)S(1)} collective-permute-done((f32[4,1024]{1,0:T(4,128)S(1)}, f32[4,1024]{1,0:T(4,128)S(1)}, u32[]{:S(2)}, u32[]{:S(2)}) %collective-permute-start.3) | collective-permute-done | bytes 16416 | tf_op jit(solution)/shard_map/ppermute | solution.py:43
  16.1 0.6 %second_step.1 = (f32[4,16,1024]{2,1,0:T(8,128)S(1)}, f32[4,16,1024]{2,1,0:T(8,128)S(1)}, f32[5,16,1024]{2,1,0:T(8,128)S(1)}) custom-call(f32[4,16,1024]{2,1,0:T(8,128)S(1)} %get-tuple-element.31.s_ref.refs_0_, f32[4,16,1024]{2,1,0:T(8,128)S(1)} %get-tuple-element.32.c_ref.refs_1_, f32[4,16,1024]{2,1,0:T(8,128)S(1)} %get-tuple-element.33.f_ref.refs_2_, ...), custom_call_target="tpu_custom_call" | custom-call | flops 20000000 | bytes 4000000 | tf_op jit(solution)/shard_map/second_step/pallas_call | solution.py:412
  16.7 0.3 collective-permute-done.4.a_ref
  17.0 0.0 collective-permute-done.5.b_ref
  17.0 0.4 %shading.1 = (f32[4,16,1024]{2,1,0:T(8,128)S(1)}, f32[4,16,1024]{2,1,0:T(8,128)S(1)}, f32[16,32,128]{2,1,0:T(8,128)S(1)}) custom-call(f32[4,16,1024]{2,1,0:T(8,128)S(1)} %get-tuple-element.46.fed_two, f32[4,16,1024]{2,1,0:T(8,128)S(1)} %get-tuple-element.47.auto_two, f32[4,16,1024]{2,1,0:T(8,128)S(1)} %get-tuple-element.35.refs_4_.e_ref, ...), custom_call_target="tpu_custom_call" | custom-call | tf_op jit(solution)/shard_map/shading/pallas_call | solution.py:425
  17.4 16.4 %all_to_all.5.part_ref = f32[16,32,128]{2,1,0:T(8,128)S(1)} all-to-all(f32[16,32,128]{2,1,0:T(8,128)S(1)} %get-tuple-element.51), channel_id=1, replica_groups=mesh['depth'=16,'rows'=2] {'depth'}, dimensions={0} | all-to-all | bytes 524288 | tf_op jit(solution)/shard_map/all_to_all | solution.py:435
  33.8 0.8 %front_to_back.1 = (f32[4,16,64]{2,1,0:T(8,128)}, f32[4,16,1024]{2,1,0:T(8,128)}, f32[4,16,1024]{2,1,0:T(8,128)}) custom-call(f32[16,32,128]{2,1,0:T(8,128)S(1)} %all_to_all.5.part_ref, f32[4,16,1024]{2,1,0:T(8,128)S(1)} %get-tuple-element.52.fed_ref, f32[4,16,1024]{2,1,0:T(8,128)S(1)} %get-tuple-element.53.auto_ref), custom_call_target="tpu_custom_call" | custom-call | tf_op jit(solution)/shard_map/front_to_back/pallas_call | solution.py:437
  (1 shorter events, 0.0 us)
Async XLA Ops:
  1.6 9.4 %collective-permute-start.2 = (f32[2,16,1024]{2,1,0:T(8,128)S(1)}, f32[2,16,1024]{2,1,0:T(8,128)S(1)}, u32[]{:S(2)}, u32[]{:S(2)}) collective-permute-start(f32[2,16,1024]{2,1,0:T(8,128)S(1)} %get-tuple-element.45), channel_id=1, source_target_pairs={{0,1},{1,0},{2,4},{3,5},{4,2},{5,3},{6,8},{7,9},{8,6},{9,7},{10,12... | collective-permute-start | bytes 393224 | tf_op jit(solution)/shard_map/ppermute | solution.py:43
  2.1 12.7 %collective-permute-start.1 = (f32[2,16,1024]{2,1,0:T(8,128)S(1)}, f32[2,16,1024]{2,1,0:T(8,128)S(1)}, u32[]{:S(2)}, u32[]{:S(2)}) collective-permute-start(f32[2,16,1024]{2,1,0:T(8,128)S(1)} %get-tuple-element.30.refs_5_), channel_id=1, source_target_pairs={{0,2},{1,3},{2,0},{3,1},{4,6},{5,7},{6,4},{7,5},{8,10},{9,11},{10,... | collective-permute-start | bytes 393224 | tf_op jit(solution)/shard_map/ppermute | solution.py:43
  7.9 9.2 %collective-permute-start.4 = (f32[2,16,1024]{2,1,0:T(8,128)S(1)}, f32[2,16,1024]{2,1,0:T(8,128)S(1)}, u32[]{:S(2)}, u32[]{:S(2)}) collective-permute-start(f32[2,16,1024]{2,1,0:T(8,128)S(1)} %get-tuple-element.49), channel_id=1, source_target_pairs={{0,2},{1,3},{2,0},{3,1},{4,6},{5,7},{6,4},{7,5},{8,10},{9,11},{10,... | collective-permute-start | bytes 393224 | tf_op jit(solution)/shard_map/ppermute | solution.py:43
  7.9 9.1 %collective-permute-start.5 = (f32[2,16,1024]{2,1,0:T(8,128)S(1)}, f32[2,16,1024]{2,1,0:T(8,128)S(1)}, u32[]{:S(2)}, u32[]{:S(2)}) collective-permute-start(f32[2,16,1024]{2,1,0:T(8,128)S(1)} %get-tuple-element.50), channel_id=1, source_target_pairs={{0,1},{1,0},{2,4},{3,5},{4,2},{5,3},{6,8},{7,9},{8,6},{9,7},{10,12... | collective-permute-start | bytes 393224 | tf_op jit(solution)/shard_map/ppermute | solution.py:43
  8.0 1.4 %collective-permute-start = (f32[16,1024]{1,0:T(8,128)S(1)}, f32[16,1024]{1,0:T(8,128)S(1)}, u32[]{:S(2)}, u32[]{:S(2)}) collective-permute-start(f32[16,1024]{1,0:T(8,128)S(1)} %get-tuple-element.38), channel_id=1, source_target_pairs={{0,1},{2,3},{4,5},{6,7},{8,9},{10,11},{12,13},{14,15},{16,17},{18,... | collective-permute-start | bytes 196616 | tf_op jit(solution)/shard_map/ppermute | solution.py:43
  9.4 0.7 %copy-start = (f32[3,3]{1,0:T(4,128)S(1)}, f32[3,3]{1,0:T(4,128)}, u32[]{:S(2)}) copy-start(f32[3,3]{1,0:T(4,128)} %palette.1) | copy-start | bytes 112
  14.9 1.2 %collective-permute-start.3 = (f32[4,1024]{1,0:T(4,128)S(1)}, f32[4,1024]{1,0:T(4,128)S(1)}, u32[]{:S(2)}, u32[]{:S(2)}) collective-permute-start(f32[4,1024]{1,0:T(4,128)S(1)} %corner_rows.1), channel_id=1, source_target_pairs={{0,1},{2,3},{4,5},{6,7},{8,9},{10,11},{12,13},{14,15},{16,17},{18,... | collective-permute-start | bytes 49160 | tf_op jit(solution)/shard_map/ppermute | solution.py:43

commit v5 on v4

--- a/solution.py
+++ b/solution.py
@@ -81,29 +81,28 @@
     return react(s_ref[layer], c_ref[layer], near[0], near[1], feed, kill)
 
 
-def old_kernel(s_hbm, c_hbm, a_ref, b_ref, arrived):
-    depth = s_hbm.shape[0]
+def old_kernel(s_hbm, c_hbm, palette_hbm, *refs):
+    b_ref, a_ref, mix_ref, palette, arrived = refs[-5:]
+    depth, _, columns = s_hbm.shape
     even = is_even("depth")
     copies = []
     for n, (out, towards_next) in enumerate(((a_ref, even), (b_ref, jnp.logical_not(even)))):
         layer = jnp.where(towards_next, depth - 1, 0)
         for i, hbm in enumerate((s_hbm, c_hbm)):
             copies.append(pltpu.make_async_copy(hbm.at[layer], out.at[i], arrived.at[n, i]))
+    copies.append(pltpu.make_async_copy(palette_hbm, palette, arrived.at[2, 0]))
     for copy in copies:
         copy.start()
-    for copy in copies:
+    copies[-1].wait()
+    for channel in range(3):
+        for n, scale in enumerate((8.0, 8.0, 1.0)):
+            at = 3 * channel + n
+            mix_ref[at : at + 1] = jnp.full((1, columns), scale * palette[channel, n], jnp.float32)
+    for copy in copies[:-1]:
         copy.wait()
 
 
-def partial_kernel(*refs):
-    held = refs[6:11]
-    s_ref, c_ref, f_ref, k_ref, _ = held
-    ps_ref, pc_ref, a_ref, b_ref, *strips, arrived = refs[11:]
-    copies = [pltpu.make_async_copy(refs[n], held[n], arrived.at[n]) for n in range(5)]
-    for copy in copies:
-        copy.start()
-    for copy in copies[:4]:
-        copy.wait()
+def partial_kernel(s_ref, c_ref, f_ref, k_ref, _, ps_ref, pc_ref, a_ref, b_ref, *strips):
     depth, rows, _ = s_ref.shape
     for layer in range(depth):
         inner = [other for other in (layer - 1, layer + 1) if 0 <= other < depth]
@@ -119,7 +118,6 @@
             for layer in range(depth):
                 head, tail = ref[layer, 0:1], ref[layer, rows - 1 : rows]
                 out[n * depth + layer : n * depth + layer + 1] = jnp.where(towards_next, tail, head)
-    copies[4].wait()
 
 
 def sides(axis, refs, read):
@@ -143,8 +141,8 @@
     return react(fields[0][layer], fields[1][layer], near[0], near[1], feed, kill)
 
 
-def inner_kernel(s_ref, c_ref, f_ref, k_ref, ps_ref, pc_ref, palette, *refs):
-    *beside, fed_one, auto_one, fed_two, auto_two, outer_ref, mix_ref = refs
+def inner_kernel(s_ref, c_ref, f_ref, k_ref, ps_ref, pc_ref, *refs):
+    *beside, fed_one, auto_one, fed_two, auto_two, outer_ref = refs
     depth, rows, columns = s_ref.shape
     row = lax.broadcasted_iota(jnp.int32, (rows, columns), 0)
     index, last = lax.axis_index("rows"), lax.axis_size("rows") - 1
@@ -175,13 +173,9 @@
     for layer in range(1, depth - 1):
         others = [(values[layer - 1], values[layer + 1]) for values in fields]
         fed_two[layer], auto_two[layer] = step_two(fields, outside, layer, others, f_ref[layer], k_ref[layer])
-    for channel in range(3):
-        for n, scale in enumerate((8.0, 8.0, 1.0)):
-            at = 3 * channel + n
-            mix_ref[at : at + 1] = jnp.full((1, columns), scale * palette[channel, n], jnp.float32)
-
-
-def corner_kernel(a_ref, b_ref, _, *outs):
+
+
+def corner_kernel(b_ref, a_ref, _, *outs):
     rows = a_ref.shape[1]
     even = is_even("rows")
     for out, towards_next in zip(outs, (even, jnp.logical_not(even))):
@@ -364,40 +358,40 @@
     cells = (substrate, catalyst, feed_rate, kill_rate)
     pair = f32((2, rows, columns))
     in_hbm = lambda x: pltpu.with_memory_space_constraint(x, pltpu.HBM)
-    old_beams = pl.pallas_call(
+    *old_beams, mix = pl.pallas_call(
         old_kernel,
-        out_shape=(pair, pair),
-        in_specs=[HBM] * 2,
-        out_specs=(VMEM, VMEM),
-        scratch_shapes=[pltpu.SemaphoreType.DMA((2, 2))],
+        out_shape=(pair, pair, f32((9, columns))),
+        in_specs=[HBM] * 6,
+        out_specs=(VMEM,) * 3,
+        scratch_shapes=[pltpu.SMEM(palette.shape, jnp.float32), pltpu.SemaphoreType.DMA((3, 2))],
+        cost_estimate=WORK,
         compiler_params=PARAMS,
         name="old_layers",
-    )(in_hbm(substrate), in_hbm(catalyst))
-    old_far = [paired(value, pairs) for value, pairs in zip(old_beams, along_depth)]
+    )(*(in_hbm(x) for x in (substrate, catalyst, palette, feed_rate, kill_rate, extinction)))
+    old_far = [paired(value, pairs) for value, pairs in zip(old_beams[::-1], along_depth)]
 
     strip = f32((4 * depth, columns))
     outs = pl.pallas_call(
         partial_kernel,
-        out_shape=(whole,) * 7 + (pair, pair) + (strip,) * len(along_rows),
-        in_specs=[HBM] * 5 + [ANY],
-        out_specs=(VMEM,) * (9 + len(along_rows)),
-        scratch_shapes=[pltpu.SemaphoreType.DMA((5,))],
+        out_shape=(whole, whole, pair, pair) + (strip,) * len(along_rows),
+        in_specs=[VMEM] * 4 + [ANY],
+        out_specs=(VMEM,) * (4 + len(along_rows)),
         cost_estimate=WORK,
         compiler_params=PARAMS,
         name="partial_step",
-    )(*(in_hbm(x) for x in cells), in_hbm(extinction), old_beams[0])
-    cells, extinction, partial = outs[:4], outs[4], outs[5:7]
-    new_far = [paired(value, pairs) for value, pairs in zip(outs[7:9], along_depth)]
-    beside = [paired(value, pairs) for value, pairs in zip(outs[9:], along_rows)]
-    *inner, mix = pl.pallas_call(
+    )(*cells, old_beams[0])
+    partial = outs[:2]
+    new_far = [paired(value, pairs) for value, pairs in zip(outs[2:4], along_depth)]
+    beside = [paired(value, pairs) for value, pairs in zip(outs[4:], along_rows)]
+    inner = pl.pallas_call(
         inner_kernel,
-        out_shape=(whole,) * 4 + (strip, f32((9, columns))),
-        in_specs=[VMEM] * 6 + [SMEM] + [VMEM] * len(beside),
-        out_specs=(VMEM,) * 6,
+        out_shape=(whole,) * 4 + (strip,),
+        in_specs=[VMEM] * (6 + len(beside)),
+        out_specs=(VMEM,) * 5,
         cost_estimate=WORK,
         compiler_params=PARAMS,
         name="inner_cells",
-    )(*cells, *partial, palette, *beside)
+    )(*cells, *partial, *beside)
 
     corner = f32((4, columns))
     corners = pl.pallas_call(
@@ -407,7 +401,7 @@
         out_specs=(VMEM,) * len(along_rows),
         compiler_params=PARAMS,
         name="corner_rows",
-    )(*old_far, inner[4])
+    )(*old_far[::-1], inner[4])
     corners = [paired(value, pairs) for value, pairs in zip(corners, along_rows)]
     fed, auto, middle = pl.pallas_call(
         functools.partial(second_kernel, len(corners)),

time: 34.9 us -> 34.1 us (0.977)
  Pallas kernels: 5.36 us -> 3.64 us
  starting transfers between devices: 5.2 us -> 6.61 us
  local copies, waits for them, and re-layouts: 0.68 us -> 0.02 us
  blocking collectives: 16.4 us -> 16.8 us
    pallas_call x3, Pallas kernels: 3.61 us -> 1.9 us  [the longest x1 1.08 us: body(): pl.pallas_call(old_kernel, out_shape=(pair, pair, f32((9, columns))), in_...]
    ppermute x6, starting transfers between devices: 5.2 us -> 6.61 us  [paired(): return lax.ppermute(value, ('depth', 'rows'), pairs)]
    unnamed x2 -> x10, local copies, waits for them, and re-layouts: 0.68 us -> 0.02 us
    all_to_all x1, blocking collectives: 16.4 us -> 16.8 us  [body(): part = lax.all_to_all(part, 'depth', 0, 0)]
  transfers between devices with their start and end apart: 6 -> 6, of which waited for: 4 -> 4; matrix products, arithmetic and copies ran while one was open for 0% -> 0% of each run, Pallas kernels for 9% -> 4%
where the time goes in v5:
time: 34.1 us; the launch traced here: 33.9 us
  blocking collectives  16.8 us (49%)
  starting transfers between devices  6.61 us (19%)
  waiting for transfers between devices  6.13 us (18%)
  Pallas kernels  3.64 us (11%)
  between operations  0.73 us (2%)
    all_to_all x1, blocking collectives, body(): part = lax.all_to_all(part, 'depth', 0, 0)  16.8 us
    ppermute x6, starting transfers between devices, paired(): return lax.ppermute(value, ('depth', 'rows'), pairs)  6.61 us
    ppermute x6, waiting for transfers between devices, paired(): return lax.ppermute(value, ('depth', 'rows'), pairs)  6.13 us
    pallas_call x1, Pallas kernels, body(): pl.pallas_call(old_kernel, out_shape=(pair, pair, f32((9, columns))), in_...  1.08 us
    pallas_call x1, Pallas kernels, body(): pl.pallas_call(functools.partial(last_kernel, group or 1), out_shape=(ima...  0.82 us
  transfers between devices with their start and end apart: 6, of which 4 were waited for; matrix products, arithmetic and copies ran while one was open for 0% of the time, Pallas kernels for 4%

profile of v5, /device:TPU:0, one launch (start us, length us, event | category | flops | bytes accessed | tf_op | source)
XLA Modules:
  0.0 33.9 jit_solution(16443594058586919496)
XLA Ops:
  0.6 0.0 copy-start.3
  0.6 0.0 copy-start.2
  0.7 0.0 copy-start.1
  0.7 0.0 copy-start
  0.7 1.1 %old_layers.1 = (f32[2,16,1024]{2,1,0:T(8,128)S(1)}, f32[2,16,1024]{2,1,0:T(8,128)S(1)}, f32[9,1024]{1,0:T(8,128)S(1)}) custom-call(f32[4,16,1024]{2,1,0:T(8,128)} %refs_0_.3, f32[4,16,1024]{2,1,0:T(8,128)} %refs_1_.3, f32[3,3]{1,0:T(4,128)} %palette_hbm.1, f32[4,16,1024]{2,1,0:T(8,128)} %refs_2_.3, f32[4,16,1024]{2,1,0:T(8,128)} %refs_3_.1, ...), custom_call_target="tpu_custom_call" | custom-call | flops 20000000 | bytes 4000000 | tf_op jit(solution)/shard_map/old_layers/pallas_call | solution.py:361
  1.8 3.0 %collective-permute-start.1 = (f32[2,16,1024]{2,1,0:T(8,128)S(1)}, f32[2,16,1024]{2,1,0:T(8,128)S(1)}, u32[]{:S(2)}, u32[]{:S(2)}) collective-permute-start(f32[2,16,1024]{2,1,0:T(8,128)S(1)} %get-tuple-element.35), channel_id=1, source_target_pairs={{0,2},{1,3},{2,0},{3,1},{4,6},{5,7},{6,4},{7,5},{8,10},{9,11},{10,... | collective-permute-start | bytes 393224 | tf_op jit(solution)/shard_map/ppermute | solution.py:43
  4.8 0.0 collective-permute-start.2
  4.8 0.0 copy-done.3
  4.8 0.0 copy-done.2
  4.8 0.0 copy-done.1
  4.8 0.0 copy-done
  4.8 0.5 %partial_step.1 = (f32[4,16,1024]{2,1,0:T(8,128)S(1)}, f32[4,16,1024]{2,1,0:T(8,128)S(1)}, f32[2,16,1024]{2,1,0:T(8,128)S(1)}, f32[2,16,1024]{2,1,0:T(8,128)S(1)}, f32[16,1024]{1,0:T(8,128)S(1)}) custom-call(f32[4,16,1024]{2,1,0:T(8,128)S(1)} %copy-done, f32[4,16,1024]{2,1,0:T(8,128)S(1)} %copy-done.1, f32[4,16,1024]{2,1,0:T(8,128)S(1)} %copy-done.2, ...), custom_call_target="tpu_custom_call" | custom-call | flops 20000000 | bytes 4000000 | tf_op jit(solution)/shard_map/partial_step/pallas_call | solution.py:374
  5.3 3.0 %collective-permute-start.4 = (f32[2,16,1024]{2,1,0:T(8,128)S(1)}, f32[2,16,1024]{2,1,0:T(8,128)S(1)}, u32[]{:S(2)}, u32[]{:S(2)}) collective-permute-start(f32[2,16,1024]{2,1,0:T(8,128)S(1)} %get-tuple-element.39), channel_id=1, source_target_pairs={{0,2},{1,3},{2,0},{3,1},{4,6},{5,7},{6,4},{7,5},{8,10},{9,11},{10,... | collective-permute-start | bytes 393224 | tf_op jit(solution)/shard_map/ppermute | solution.py:43
  8.3 0.0 collective-permute-start.5
  8.3 0.5 %collective-permute-start = (f32[16,1024]{1,0:T(8,128)S(1)}, f32[16,1024]{1,0:T(8,128)S(1)}, u32[]{:S(2)}, u32[]{:S(2)}) collective-permute-start(f32[16,1024]{1,0:T(8,128)S(1)} %get-tuple-element.29), channel_id=1, source_target_pairs={{0,1},{2,3},{4,5},{6,7},{8,9},{10,11},{12,13},{14,15},{16,17},{18,... | collective-permute-start | bytes 196616 | tf_op jit(solution)/shard_map/ppermute | solution.py:43
  8.8 0.9 %collective-permute-done.refs_0_ = f32[16,1024]{1,0:T(8,128)S(1)} collective-permute-done((f32[16,1024]{1,0:T(8,128)S(1)}, f32[16,1024]{1,0:T(8,128)S(1)}, u32[]{:S(2)}, u32[]{:S(2)}) %collective-permute-start) | collective-permute-done | bytes 65568 | tf_op jit(solution)/shard_map/ppermute | solution.py:43
  9.8 0.3 inner_cells.1
  10.1 0.0 copy-start.4
  10.1 3.6 %collective-permute-done.1.a_ref.refs_11_ = f32[2,16,1024]{2,1,0:T(8,128)S(1)} collective-permute-done((f32[2,16,1024]{2,1,0:T(8,128)S(1)}, f32[2,16,1024]{2,1,0:T(8,128)S(1)}, u32[]{:S(2)}, u32[]{:S(2)}) %collective-permute-start.1) | collective-permute-done | bytes 131104 | tf_op jit(solution)/shard_map/ppermute | solution.py:43
  13.7 0.0 collective-permute-done.2.b_ref.refs_12_
  13.7 0.1 collective-permute-start.3
  13.8 1.2 %collective-permute-done.3.refs_13_ = f32[4,1024]{1,0:T(4,128)S(1)} collective-permute-done((f32[4,1024]{1,0:T(4,128)S(1)}, f32[4,1024]{1,0:T(4,128)S(1)}, u32[]{:S(2)}, u32[]{:S(2)}) %collective-permute-start.3) | collective-permute-done | bytes 16416 | tf_op jit(solution)/shard_map/ppermute | solution.py:43
  14.9 0.0 copy-done.4
  14.9 0.5 %second_step.1 = (f32[4,16,1024]{2,1,0:T(8,128)S(1)}, f32[4,16,1024]{2,1,0:T(8,128)S(1)}, f32[5,16,1024]{2,1,0:T(8,128)S(1)}) custom-call(f32[4,16,1024]{2,1,0:T(8,128)S(1)} %copy-done, f32[4,16,1024]{2,1,0:T(8,128)S(1)} %copy-done.1, f32[4,16,1024]{2,1,0:T(8,128)S(1)} %copy-done.2, f32[4,16,1024]{2,1,0:T(8,128)S(1)} %copy-done.3, ...), custom_call_target="tpu_custom_call" | custom-call | flops 20000000 | bytes 4000000 | tf_op jit(solution)/shard_map/second_step/pallas_call | solution.py:406
  15.5 0.5 %collective-permute-done.4.a_ref = f32[2,16,1024]{2,1,0:T(8,128)S(1)} collective-permute-done((f32[2,16,1024]{2,1,0:T(8,128)S(1)}, f32[2,16,1024]{2,1,0:T(8,128)S(1)}, u32[]{:S(2)}, u32[]{:S(2)}) %collective-permute-start.4) | collective-permute-done | bytes 131104 | tf_op jit(solution)/shard_map/ppermute | solution.py:43
  15.9 0.0 collective-permute-done.5.b_ref
  16.0 0.4 %shading.1 = (f32[4,16,1024]{2,1,0:T(8,128)S(1)}, f32[4,16,1024]{2,1,0:T(8,128)S(1)}, f32[16,32,128]{2,1,0:T(8,128)S(1)}) custom-call(f32[4,16,1024]{2,1,0:T(8,128)S(1)} %get-tuple-element.36.fed_two, f32[4,16,1024]{2,1,0:T(8,128)S(1)} %get-tuple-element.37.auto_two, f32[4,16,1024]{2,1,0:T(8,128)S(1)} %copy-done.4, ...), custom_call_target="tpu_custom_call" | custom-call | tf_op jit(solution)/shard_map/shading/pallas_call | solution.py:419
  16.3 16.8 %all_to_all.5.part_ref = f32[16,32,128]{2,1,0:T(8,128)S(1)} all-to-all(f32[16,32,128]{2,1,0:T(8,128)S(1)} %get-tuple-element.41), channel_id=1, replica_groups=mesh['depth'=16,'rows'=2] {'depth'}, dimensions={0} | all-to-all | bytes 524288 | tf_op jit(solution)/shard_map/all_to_all | solution.py:429
  33.1 0.8 %front_to_back.1 = (f32[4,16,64]{2,1,0:T(8,128)}, f32[4,16,1024]{2,1,0:T(8,128)}, f32[4,16,1024]{2,1,0:T(8,128)}) custom-call(f32[16,32,128]{2,1,0:T(8,128)S(1)} %all_to_all.5.part_ref, f32[4,16,1024]{2,1,0:T(8,128)S(1)} %get-tuple-element.42.fed_ref, f32[4,16,1024]{2,1,0:T(8,128)S(1)} %get-tuple-element.43.auto_ref), custom_call_target="tpu_custom_call" | custom-call | tf_op jit(solution)/shard_map/front_to_back/pallas_call | solution.py:431
  (1 shorter events, 0.0 us)
Async XLA Ops:
  0.6 4.1 %copy-start.3 = (f32[4,16,1024]{2,1,0:T(8,128)S(1)}, f32[4,16,1024]{2,1,0:T(8,128)}, u32[]{:S(2)}) copy-start(f32[4,16,1024]{2,1,0:T(8,128)} %refs_3_.1) | copy-start | bytes 786436
  0.6 4.1 %copy-start.2 = (f32[4,16,1024]{2,1,0:T(8,128)S(1)}, f32[4,16,1024]{2,1,0:T(8,128)}, u32[]{:S(2)}) copy-start(f32[4,16,1024]{2,1,0:T(8,128)} %refs_2_.3) | copy-start | bytes 786436
  0.7 4.1 %copy-start.1 = (f32[4,16,1024]{2,1,0:T(8,128)S(1)}, f32[4,16,1024]{2,1,0:T(8,128)}, u32[]{:S(2)}) copy-start(f32[4,16,1024]{2,1,0:T(8,128)} %refs_1_.3) | copy-start | bytes 786436
  0.7 4.1 %copy-start = (f32[4,16,1024]{2,1,0:T(8,128)S(1)}, f32[4,16,1024]{2,1,0:T(8,128)}, u32[]{:S(2)}) copy-start(f32[4,16,1024]{2,1,0:T(8,128)} %refs_0_.3) | copy-start | bytes 786436
  1.8 11.9 %collective-permute-start.1 = (f32[2,16,1024]{2,1,0:T(8,128)S(1)}, f32[2,16,1024]{2,1,0:T(8,128)S(1)}, u32[]{:S(2)}, u32[]{:S(2)}) collective-permute-start(f32[2,16,1024]{2,1,0:T(8,128)S(1)} %get-tuple-element.35), channel_id=1, source_target_pairs={{0,2},{1,3},{2,0},{3,1},{4,6},{5,7},{6,4},{7,5},{8,10},{9,11},{10,... | collective-permute-start | bytes 393224 | tf_op jit(solution)/shard_map/ppermute | solution.py:43
  4.8 8.9 %collective-permute-start.2 = (f32[2,16,1024]{2,1,0:T(8,128)S(1)}, f32[2,16,1024]{2,1,0:T(8,128)S(1)}, u32[]{:S(2)}, u32[]{:S(2)}) collective-permute-start(f32[2,16,1024]{2,1,0:T(8,128)S(1)} %get-tuple-element.26._), channel_id=1, source_target_pairs={{0,1},{1,0},{2,4},{3,5},{4,2},{5,3},{6,8},{7,9},{8,6},{9,7},{10,12... | collective-permute-start | bytes 393224 | tf_op jit(solution)/shard_map/ppermute | solution.py:43
  5.3 10.6 %collective-permute-start.4 = (f32[2,16,1024]{2,1,0:T(8,128)S(1)}, f32[2,16,1024]{2,1,0:T(8,128)S(1)}, u32[]{:S(2)}, u32[]{:S(2)}) collective-permute-start(f32[2,16,1024]{2,1,0:T(8,128)S(1)} %get-tuple-element.39), channel_id=1, source_target_pairs={{0,2},{1,3},{2,0},{3,1},{4,6},{5,7},{6,4},{7,5},{8,10},{9,11},{10,... | collective-permute-start | bytes 393224 | tf_op jit(solution)/shard_map/ppermute | solution.py:43
  8.3 7.6 %collective-permute-start.5 = (f32[2,16,1024]{2,1,0:T(8,128)S(1)}, f32[2,16,1024]{2,1,0:T(8,128)S(1)}, u32[]{:S(2)}, u32[]{:S(2)}) collective-permute-start(f32[2,16,1024]{2,1,0:T(8,128)S(1)} %get-tuple-element.40), channel_id=1, source_target_pairs={{0,1},{1,0},{2,4},{3,5},{4,2},{5,3},{6,8},{7,9},{8,6},{9,7},{10,12... | collective-permute-start | bytes 393224 | tf_op jit(solution)/shard_map/ppermute | solution.py:43
  8.3 1.4 %collective-permute-start = (f32[16,1024]{1,0:T(8,128)S(1)}, f32[16,1024]{1,0:T(8,128)S(1)}, u32[]{:S(2)}, u32[]{:S(2)}) collective-permute-start(f32[16,1024]{1,0:T(8,128)S(1)} %get-tuple-element.29), channel_id=1, source_target_pairs={{0,1},{2,3},{4,5},{6,7},{8,9},{10,11},{12,13},{14,15},{16,17},{18,... | collective-permute-start | bytes 196616 | tf_op jit(solution)/shard_map/ppermute | solution.py:43
  10.1 4.9 %copy-start.4 = (f32[4,16,1024]{2,1,0:T(8,128)S(1)}, f32[4,16,1024]{2,1,0:T(8,128)}, u32[]{:S(2)}) copy-start(f32[4,16,1024]{2,1,0:T(8,128)} %e_ref.1) | copy-start | bytes 786436
  13.7 1.2 %collective-permute-start.3 = (f32[4,1024]{1,0:T(4,128)S(1)}, f32[4,1024]{1,0:T(4,128)S(1)}, u32[]{:S(2)}, u32[]{:S(2)}) collective-permute-start(f32[4,1024]{1,0:T(4,128)S(1)} %corner_rows.1), channel_id=1, source_target_pairs={{0,1},{2,3},{4,5},{6,7},{8,9},{10,11},{12,13},{14,15},{16,17},{18,... | collective-permute-start | bytes 49160 | tf_op jit(solution)/shard_map/ppermute | solution.py:43

commit v6 on v5

--- a/solution.py
+++ b/solution.py
@@ -102,7 +102,7 @@
         copy.wait()
 
 
-def partial_kernel(s_ref, c_ref, f_ref, k_ref, _, ps_ref, pc_ref, a_ref, b_ref, *strips):
+def partial_kernel(s_ref, c_ref, f_ref, k_ref, _, ps_ref, pc_ref, b_ref, a_ref, *strips):
     depth, rows, _ = s_ref.shape
     for layer in range(depth):
         inner = [other for other in (layer - 1, layer + 1) if 0 <= other < depth]
@@ -271,7 +271,7 @@
             middle_ref[n] = value
 
 
-def shade_kernel(depth_count, fed_two, auto_two, e_ref, mix_ref, middle_ref, a_ref, b_ref, fed_out, auto_out, part_ref):
+def shade_kernel(depth_count, fed_two, auto_two, e_ref, mix_ref, middle_ref, b_ref, a_ref, fed_out, auto_out, part_ref):
     depth, rows, columns = fed_two.shape
     new_far = [sides("depth", (a_ref, b_ref), lambda ref: ref[n]) for n in range(2)]
     shading = Shading(mix_ref)
@@ -381,7 +381,7 @@
         name="partial_step",
     )(*cells, old_beams[0])
     partial = outs[:2]
-    new_far = [paired(value, pairs) for value, pairs in zip(outs[2:4], along_depth)]
+    new_far = [paired(value, pairs) for value, pairs in zip((outs[3], outs[2]), along_depth)]
     beside = [paired(value, pairs) for value, pairs in zip(outs[4:], along_rows)]
     inner = pl.pallas_call(
         inner_kernel,
@@ -423,7 +423,7 @@
         out_specs=(VMEM,) * 3,
         compiler_params=PARAMS,
         name="shading",
-    )(fed, auto, extinction, mix, middle, *new_far)
+    )(fed, auto, extinction, mix, middle, *new_far[::-1])
     if not group:
         part = jnp.transpose(part.reshape(4 * rows, count, block), (1, 0, 2))
     part = lax.all_to_all(part, "depth", 0, 0)

time: 34.1 us -> 34 us (level)
  waiting for transfers between devices: 6.13 us -> 7.29 us
  blocking collectives: 16.8 us -> 15.9 us
  starting transfers between devices: 6.61 us -> 6.18 us
    ppermute x6, waiting for transfers between devices: 6.13 us -> 7.29 us  [paired(): return lax.ppermute(value, ('depth', 'rows'), pairs)]
    all_to_all x1, blocking collectives: 16.8 us -> 15.9 us  [body(): part = lax.all_to_all(part, 'depth', 0, 0)]
    ppermute x6, starting transfers between devices: 6.61 us -> 6.18 us  [paired(): return lax.ppermute(value, ('depth', 'rows'), pairs)]
where the time goes in v6:
time: 34 us; the launch traced here: 33.8 us
  blocking collectives  15.9 us (47%)
  waiting for transfers between devices  7.29 us (21%)
  starting transfers between devices  6.18 us (18%)
  Pallas kernels  3.64 us (11%)
  between operations  0.74 us (2%)
    all_to_all x1, blocking collectives, body(): part = lax.all_to_all(part, 'depth', 0, 0)  15.9 us
    ppermute x6, waiting for transfers between devices, paired(): return lax.ppermute(value, ('depth', 'rows'), pairs)  7.29 us
    ppermute x6, starting transfers between devices, paired(): return lax.ppermute(value, ('depth', 'rows'), pairs)  6.18 us
    pallas_call x1, Pallas kernels, body(): pl.pallas_call(old_kernel, out_shape=(pair, pair, f32((9, columns))), in_...  1.08 us
    pallas_call x1, Pallas kernels, body(): pl.pallas_call(functools.partial(last_kernel, group or 1), out_shape=(ima...  0.82 us
  transfers between devices with their start and end apart: 6, of which 4 were waited for; matrix products, arithmetic and copies ran while one was open for 0% of the time, Pallas kernels for 4%

profile of v6, /device:TPU:0, one launch (start us, length us, event | category | flops | bytes accessed | tf_op | source)
XLA Modules:
  0.0 33.8 jit_solution(14369096732060634206)
XLA Ops:
  0.6 0.0 copy-start.3
  0.6 0.0 copy-start.2
  0.7 0.0 copy-start.1
  0.7 0.0 copy-start
  0.7 1.1 %old_layers.1 = (f32[2,16,1024]{2,1,0:T(8,128)S(1)}, f32[2,16,1024]{2,1,0:T(8,128)S(1)}, f32[9,1024]{1,0:T(8,128)S(1)}) custom-call(f32[4,16,1024]{2,1,0:T(8,128)} %refs_0_.3, f32[4,16,1024]{2,1,0:T(8,128)} %refs_1_.3, f32[3,3]{1,0:T(4,128)} %palette_hbm.1, f32[4,16,1024]{2,1,0:T(8,128)} %refs_2_.3, f32[4,16,1024]{2,1,0:T(8,128)} %refs_3_.1, ...), custom_call_target="tpu_custom_call" | custom-call | flops 20000000 | bytes 4000000 | tf_op jit(solution)/shard_map/old_layers/pallas_call | solution.py:361
  1.8 3.0 %collective-permute-start.1 = (f32[2,16,1024]{2,1,0:T(8,128)S(1)}, f32[2,16,1024]{2,1,0:T(8,128)S(1)}, u32[]{:S(2)}, u32[]{:S(2)}) collective-permute-start(f32[2,16,1024]{2,1,0:T(8,128)S(1)} %get-tuple-element.35), channel_id=1, source_target_pairs={{0,2},{1,3},{2,0},{3,1},{4,6},{5,7},{6,4},{7,5},{8,10},{9,11},{10,... | collective-permute-start | bytes 393224 | tf_op jit(solution)/shard_map/ppermute | solution.py:43
  4.8 0.0 collective-permute-start.2
  4.8 0.0 copy-done.3
  4.8 0.0 copy-done.2
  4.8 0.0 copy-done.1
  4.8 0.0 copy-done
  4.8 0.5 %partial_step.1 = (f32[4,16,1024]{2,1,0:T(8,128)S(1)}, f32[4,16,1024]{2,1,0:T(8,128)S(1)}, f32[2,16,1024]{2,1,0:T(8,128)S(1)}, f32[2,16,1024]{2,1,0:T(8,128)S(1)}, f32[16,1024]{1,0:T(8,128)S(1)}) custom-call(f32[4,16,1024]{2,1,0:T(8,128)S(1)} %copy-done, f32[4,16,1024]{2,1,0:T(8,128)S(1)} %copy-done.1, f32[4,16,1024]{2,1,0:T(8,128)S(1)} %copy-done.2, ...), custom_call_target="tpu_custom_call" | custom-call | flops 20000000 | bytes 4000000 | tf_op jit(solution)/shard_map/partial_step/pallas_call | solution.py:374
  5.3 0.6 %collective-permute-start.4 = (f32[2,16,1024]{2,1,0:T(8,128)S(1)}, f32[2,16,1024]{2,1,0:T(8,128)S(1)}, u32[]{:S(2)}, u32[]{:S(2)}) collective-permute-start(f32[2,16,1024]{2,1,0:T(8,128)S(1)} %get-tuple-element.39), channel_id=1, source_target_pairs={{0,1},{1,0},{2,4},{3,5},{4,2},{5,3},{6,8},{7,9},{8,6},{9,7},{10,12... | collective-permute-start | bytes 393224 | tf_op jit(solution)/shard_map/ppermute | solution.py:43
  5.9 2.5 %collective-permute-start.5 = (f32[2,16,1024]{2,1,0:T(8,128)S(1)}, f32[2,16,1024]{2,1,0:T(8,128)S(1)}, u32[]{:S(2)}, u32[]{:S(2)}) collective-permute-start(f32[2,16,1024]{2,1,0:T(8,128)S(1)} %get-tuple-element.40), channel_id=1, source_target_pairs={{0,2},{1,3},{2,0},{3,1},{4,6},{5,7},{6,4},{7,5},{8,10},{9,11},{10,... | collective-permute-start | bytes 393224 | tf_op jit(solution)/shard_map/ppermute | solution.py:43
  8.4 0.0 collective-permute-start
  8.4 1.3 %collective-permute-done.refs_0_ = f32[16,1024]{1,0:T(8,128)S(1)} collective-permute-done((f32[16,1024]{1,0:T(8,128)S(1)}, f32[16,1024]{1,0:T(8,128)S(1)}, u32[]{:S(2)}, u32[]{:S(2)}) %collective-permute-start) | collective-permute-done | bytes 65568 | tf_op jit(solution)/shard_map/ppermute | solution.py:43
  9.7 0.3 inner_cells.1
  10.0 0.0 copy-start.4
  10.0 3.7 %collective-permute-done.1.a_ref.refs_11_ = f32[2,16,1024]{2,1,0:T(8,128)S(1)} collective-permute-done((f32[2,16,1024]{2,1,0:T(8,128)S(1)}, f32[2,16,1024]{2,1,0:T(8,128)S(1)}, u32[]{:S(2)}, u32[]{:S(2)}) %collective-permute-start.1) | collective-permute-done | bytes 131104 | tf_op jit(solution)/shard_map/ppermute | solution.py:43
  13.7 0.0 collective-permute-done.2.b_ref.refs_12_
  13.7 0.1 collective-permute-start.3
  13.8 1.2 %collective-permute-done.3.refs_13_ = f32[4,1024]{1,0:T(4,128)S(1)} collective-permute-done((f32[4,1024]{1,0:T(4,128)S(1)}, f32[4,1024]{1,0:T(4,128)S(1)}, u32[]{:S(2)}, u32[]{:S(2)}) %collective-permute-start.3) | collective-permute-done | bytes 16416 | tf_op jit(solution)/shard_map/ppermute | solution.py:43
  14.9 0.0 copy-done.4
  14.9 0.5 %second_step.1 = (f32[4,16,1024]{2,1,0:T(8,128)S(1)}, f32[4,16,1024]{2,1,0:T(8,128)S(1)}, f32[5,16,1024]{2,1,0:T(8,128)S(1)}) custom-call(f32[4,16,1024]{2,1,0:T(8,128)S(1)} %copy-done, f32[4,16,1024]{2,1,0:T(8,128)S(1)} %copy-done.1, f32[4,16,1024]{2,1,0:T(8,128)S(1)} %copy-done.2, f32[4,16,1024]{2,1,0:T(8,128)S(1)} %copy-done.3, ...), custom_call_target="tpu_custom_call" | custom-call | flops 20000000 | bytes 4000000 | tf_op jit(solution)/shard_map/second_step/pallas_call | solution.py:406
  15.5 0.0 collective-permute-done.4.b_ref
  15.5 1.2 %collective-permute-done.5.a_ref = f32[2,16,1024]{2,1,0:T(8,128)S(1)} collective-permute-done((f32[2,16,1024]{2,1,0:T(8,128)S(1)}, f32[2,16,1024]{2,1,0:T(8,128)S(1)}, u32[]{:S(2)}, u32[]{:S(2)}) %collective-permute-start.5) | collective-permute-done | bytes 131104 | tf_op jit(solution)/shard_map/ppermute | solution.py:43
  16.7 0.4 %shading.1 = (f32[4,16,1024]{2,1,0:T(8,128)S(1)}, f32[4,16,1024]{2,1,0:T(8,128)S(1)}, f32[16,32,128]{2,1,0:T(8,128)S(1)}) custom-call(f32[4,16,1024]{2,1,0:T(8,128)S(1)} %get-tuple-element.36.fed_two, f32[4,16,1024]{2,1,0:T(8,128)S(1)} %get-tuple-element.37.auto_two, f32[4,16,1024]{2,1,0:T(8,128)S(1)} %copy-done.4, ...), custom_call_target="tpu_custom_call" | custom-call | tf_op jit(solution)/shard_map/shading/pallas_call | solution.py:419
  17.1 15.9 %all_to_all.5.part_ref = f32[16,32,128]{2,1,0:T(8,128)S(1)} all-to-all(f32[16,32,128]{2,1,0:T(8,128)S(1)} %get-tuple-element.41), channel_id=1, replica_groups=mesh['depth'=16,'rows'=2] {'depth'}, dimensions={0} | all-to-all | bytes 524288 | tf_op jit(solution)/shard_map/all_to_all | solution.py:429
  33.0 0.8 %front_to_back.1 = (f32[4,16,64]{2,1,0:T(8,128)}, f32[4,16,1024]{2,1,0:T(8,128)}, f32[4,16,1024]{2,1,0:T(8,128)}) custom-call(f32[16,32,128]{2,1,0:T(8,128)S(1)} %all_to_all.5.part_ref, f32[4,16,1024]{2,1,0:T(8,128)S(1)} %get-tuple-element.42.fed_ref, f32[4,16,1024]{2,1,0:T(8,128)S(1)} %get-tuple-element.43.auto_ref), custom_call_target="tpu_custom_call" | custom-call | tf_op jit(solution)/shard_map/front_to_back/pallas_call | solution.py:431
  (1 shorter events, 0.0 us)
Async XLA Ops:
  0.6 4.1 %copy-start.3 = (f32[4,16,1024]{2,1,0:T(8,128)S(1)}, f32[4,16,1024]{2,1,0:T(8,128)}, u32[]{:S(2)}) copy-start(f32[4,16,1024]{2,1,0:T(8,128)} %refs_3_.1) | copy-start | bytes 786436
  0.6 4.1 %copy-start.2 = (f32[4,16,1024]{2,1,0:T(8,128)S(1)}, f32[4,16,1024]{2,1,0:T(8,128)}, u32[]{:S(2)}) copy-start(f32[4,16,1024]{2,1,0:T(8,128)} %refs_2_.3) | copy-start | bytes 786436
  0.7 4.1 %copy-start.1 = (f32[4,16,1024]{2,1,0:T(8,128)S(1)}, f32[4,16,1024]{2,1,0:T(8,128)}, u32[]{:S(2)}) copy-start(f32[4,16,1024]{2,1,0:T(8,128)} %refs_1_.3) | copy-start | bytes 786436
  0.7 4.1 %copy-start = (f32[4,16,1024]{2,1,0:T(8,128)S(1)}, f32[4,16,1024]{2,1,0:T(8,128)}, u32[]{:S(2)}) copy-start(f32[4,16,1024]{2,1,0:T(8,128)} %refs_0_.3) | copy-start | bytes 786436
  1.8 11.9 %collective-permute-start.1 = (f32[2,16,1024]{2,1,0:T(8,128)S(1)}, f32[2,16,1024]{2,1,0:T(8,128)S(1)}, u32[]{:S(2)}, u32[]{:S(2)}) collective-permute-start(f32[2,16,1024]{2,1,0:T(8,128)S(1)} %get-tuple-element.35), channel_id=1, source_target_pairs={{0,2},{1,3},{2,0},{3,1},{4,6},{5,7},{6,4},{7,5},{8,10},{9,11},{10,... | collective-permute-start | bytes 393224 | tf_op jit(solution)/shard_map/ppermute | solution.py:43
  4.8 8.9 %collective-permute-start.2 = (f32[2,16,1024]{2,1,0:T(8,128)S(1)}, f32[2,16,1024]{2,1,0:T(8,128)S(1)}, u32[]{:S(2)}, u32[]{:S(2)}) collective-permute-start(f32[2,16,1024]{2,1,0:T(8,128)S(1)} %get-tuple-element.26._), channel_id=1, source_target_pairs={{0,1},{1,0},{2,4},{3,5},{4,2},{5,3},{6,8},{7,9},{8,6},{9,7},{10,12... | collective-permute-start | bytes 393224 | tf_op jit(solution)/shard_map/ppermute | solution.py:43
  5.3 10.2 %collective-permute-start.4 = (f32[2,16,1024]{2,1,0:T(8,128)S(1)}, f32[2,16,1024]{2,1,0:T(8,128)S(1)}, u32[]{:S(2)}, u32[]{:S(2)}) collective-permute-start(f32[2,16,1024]{2,1,0:T(8,128)S(1)} %get-tuple-element.39), channel_id=1, source_target_pairs={{0,1},{1,0},{2,4},{3,5},{4,2},{5,3},{6,8},{7,9},{8,6},{9,7},{10,12... | collective-permute-start | bytes 393224 | tf_op jit(solution)/shard_map/ppermute | solution.py:43
  5.9 10.8 %collective-permute-start.5 = (f32[2,16,1024]{2,1,0:T(8,128)S(1)}, f32[2,16,1024]{2,1,0:T(8,128)S(1)}, u32[]{:S(2)}, u32[]{:S(2)}) collective-permute-start(f32[2,16,1024]{2,1,0:T(8,128)S(1)} %get-tuple-element.40), channel_id=1, source_target_pairs={{0,2},{1,3},{2,0},{3,1},{4,6},{5,7},{6,4},{7,5},{8,10},{9,11},{10,... | collective-permute-start | bytes 393224 | tf_op jit(solution)/shard_map/ppermute | solution.py:43
  8.4 1.3 %collective-permute-start = (f32[16,1024]{1,0:T(8,128)S(1)}, f32[16,1024]{1,0:T(8,128)S(1)}, u32[]{:S(2)}, u32[]{:S(2)}) collective-permute-start(f32[16,1024]{1,0:T(8,128)S(1)} %get-tuple-element.29), channel_id=1, source_target_pairs={{0,1},{2,3},{4,5},{6,7},{8,9},{10,11},{12,13},{14,15},{16,17},{18,... | collective-permute-start | bytes 196616 | tf_op jit(solution)/shard_map/ppermute | solution.py:43
  10.0 5.0 %copy-start.4 = (f32[4,16,1024]{2,1,0:T(8,128)S(1)}, f32[4,16,1024]{2,1,0:T(8,128)}, u32[]{:S(2)}) copy-start(f32[4,16,1024]{2,1,0:T(8,128)} %e_ref.1) | copy-start | bytes 786436
  13.7 1.2 %collective-permute-start.3 = (f32[4,1024]{1,0:T(4,128)S(1)}, f32[4,1024]{1,0:T(4,128)S(1)}, u32[]{:S(2)}, u32[]{:S(2)}) collective-permute-start(f32[4,1024]{1,0:T(4,128)S(1)} %corner_rows.1), channel_id=1, source_target_pairs={{0,1},{2,3},{4,5},{6,7},{8,9},{10,11},{12,13},{14,15},{16,17},{18,... | collective-permute-start | bytes 49160 | tf_op jit(solution)/shard_map/ppermute | solution.py:43

commit v7 on v6

--- a/solution.py
+++ b/solution.py
@@ -45,6 +45,12 @@
 
 def is_even(axis):
     return lax.rem(lax.axis_index(axis), 2) == 0
+
+
+def partners(axis):
+    index, last = lax.axis_index(axis), lax.axis_size(axis) - 1
+    odd = lax.rem(index, 2)
+    return [jnp.clip(index + 1 - 2 * odd, 0, last), jnp.clip(index - 1 + 2 * odd, 0, last)]
 
 
 def shifted_columns(value):
@@ -102,16 +108,14 @@
         copy.wait()
 
 
-def partial_kernel(s_ref, c_ref, f_ref, k_ref, _, ps_ref, pc_ref, b_ref, a_ref, *strips):
+def partial_kernel(s_ref, c_ref, f_ref, k_ref, _, ps_ref, pc_ref, a_ref, *strips):
     depth, rows, _ = s_ref.shape
     for layer in range(depth):
         inner = [other for other in (layer - 1, layer + 1) if 0 <= other < depth]
         ps_ref[layer], pc_ref[layer] = partial_step(s_ref, c_ref, f_ref[layer], k_ref[layer], layer, inner)
-    even = is_even("depth")
-    for out, towards_next in ((a_ref, even), (b_ref, jnp.logical_not(even))):
-        layer = jnp.where(towards_next, depth - 1, 0)
-        out[0] = ps_ref[layer]
-        out[1] = pc_ref[layer]
+    layer = jnp.where(is_even("depth"), depth - 1, 0)
+    a_ref[0] = ps_ref[layer]
+    a_ref[1] = pc_ref[layer]
     even = is_even("rows")
     for out, towards_next in zip(strips, (even, jnp.logical_not(even))):
         for n, ref in enumerate((s_ref, c_ref, ps_ref, pc_ref)):
@@ -142,7 +146,8 @@
 
 
 def inner_kernel(s_ref, c_ref, f_ref, k_ref, ps_ref, pc_ref, *refs):
-    *beside, fed_one, auto_one, fed_two, auto_two, outer_ref = refs
+    *strips, fed_one, auto_one, fed_two, auto_two, outer_ref, b_ref = refs
+    beside = [ref.at[place] for ref, place in zip(strips, partners("rows"))]
     depth, rows, columns = s_ref.shape
     row = lax.broadcasted_iota(jnp.int32, (rows, columns), 0)
     index, last = lax.axis_index("rows"), lax.axis_size("rows") - 1
@@ -173,20 +178,22 @@
     for layer in range(1, depth - 1):
         others = [(values[layer - 1], values[layer + 1]) for values in fields]
         fed_two[layer], auto_two[layer] = step_two(fields, outside, layer, others, f_ref[layer], k_ref[layer])
-
-
-def corner_kernel(b_ref, a_ref, _, *outs):
-    rows = a_ref.shape[1]
-    even = is_even("rows")
-    for out, towards_next in zip(outs, (even, jnp.logical_not(even))):
-        for n in range(2):
-            pair = sides(
-                "depth",
-                (a_ref, b_ref),
-                lambda ref: jnp.where(towards_next, ref[n, rows - 1 : rows], ref[n, 0:1]),
-            )
-            for end in range(2):
-                out[2 * n + end : 2 * n + end + 1] = pair[end]
+    end = jnp.where(is_even("depth"), 0, depth - 1)
+    for n, (one, partial) in enumerate(((fed_one, ps_ref), (auto_one, pc_ref))):
+        b_ref[n] = one[end] + (one[end] - partial[end])
+
+
+def corner_kernel(depth, *refs):
+    *strips, out = refs
+    beside = [ref.at[place] for ref, place in zip(strips, partners("rows"))]
+    even = is_even("depth")
+    for n in range(2):
+        first, final = [
+            sides("rows", beside, lambda ref: ref[n * depth + layer : n * depth + layer + 1])
+            for layer in (0, depth - 1)
+        ]
+        for side in range(2):
+            out[2 * n + side : 2 * n + side + 1] = jnp.where(even, final[side], first[side])
 
 
 class Shading:
@@ -212,14 +219,12 @@
         self.put(pieces + [opacity], passing)
 
 
-def second_kernel(row_pairings, *refs):
+def second_kernel(*refs):
     s_ref, c_ref, f_ref, k_ref, e_ref, mix_ref = refs[:6]
     fed_one, auto_one, fed_mid, auto_mid, outer_ref = refs[6:11]
     far = refs[11:13]
-    corners = refs[13 : 13 + row_pairings]
-    fed_two, auto_two, middle_ref = refs[13 + row_pairings :]
-    depth, rows, columns = s_ref.shape
-    row = lax.broadcasted_iota(jnp.int32, (rows, columns), 0)
+    fed_two, auto_two, middle_ref = refs[13:]
+    depth = s_ref.shape[0]
     index, last = lax.axis_index("depth"), lax.axis_size("depth") - 1
     inside = (index > 0, index < last)
     ends = (0, depth - 1)
@@ -230,10 +235,7 @@
         beyond.append([])
         values, rows_outside = {}, {}
         for end, layer in enumerate(ends):
-            at = 2 * n + end
-            above, below = sides("rows", corners, lambda ref: ref[at : at + 1])
-            corner = jnp.where(row == 0, above, 0.0) + jnp.where(row == rows - 1, below, 0.0)
-            beyond[n].append(jnp.where(inside[end], reach * old[layer], 0.0) + (2.0 * reach) * corner)
+            beyond[n].append(jnp.where(inside[end], reach * old[layer], 0.0))
         for layer in set(ends):
             near = 0.0
             for end in range(2):
@@ -271,17 +273,32 @@
             middle_ref[n] = value
 
 
-def shade_kernel(depth_count, fed_two, auto_two, e_ref, mix_ref, middle_ref, b_ref, a_ref, fed_out, auto_out, part_ref):
+def shade_kernel(depth_count, *refs):
+    fed_two, auto_two, e_ref, mix_ref, middle_ref, a_ref, b_ref, corner_ref, fed_out, auto_out, part_ref = refs
     depth, rows, columns = fed_two.shape
-    new_far = [sides("depth", (a_ref, b_ref), lambda ref: ref[n]) for n in range(2)]
+    row = lax.broadcasted_iota(jnp.int32, (rows, columns), 0)
+    index = lax.axis_index("depth")
+    even = is_even("depth")
+    there = (
+        jnp.logical_and(jnp.logical_not(even), index > 0),
+        jnp.logical_and(even, index < depth_count - 1),
+    )
+    more = []
+    for n, reach in enumerate((reach_fast, reach_slow)):
+        new_far = sides("depth", (a_ref, b_ref), lambda ref: ref[n])
+        above, below = corner_ref[2 * n : 2 * n + 1], corner_ref[2 * n + 1 : 2 * n + 2]
+        corner = jnp.where(row == 0, above, 0.0) + jnp.where(row == rows - 1, below, 0.0)
+        more.append(
+            [reach * new_far[end] + jnp.where(there[end], (2.0 * reach * reach) * corner, 0.0) for end in range(2)]
+        )
     shading = Shading(mix_ref)
     for layer in range(depth):
         fed, auto = fed_two[layer], auto_two[layer]
         if layer in (0, depth - 1):
             for end, place in enumerate((0, depth - 1)):
                 if layer == place:
-                    fed = fed + reach_fast * new_far[0][end]
-                    auto = auto + reach_slow * new_far[1][end]
+                    fed = fed + more[0][end]
+                    auto = auto + more[1][end]
             shading.add(fed, auto, e_ref[layer])
         elif layer == 1:
             shading.put([middle_ref[n] for n in range(4)], middle_ref[4])
@@ -373,45 +390,43 @@
     strip = f32((4 * depth, columns))
     outs = pl.pallas_call(
         partial_kernel,
-        out_shape=(whole, whole, pair, pair) + (strip,) * len(along_rows),
+        out_shape=(whole, whole, pair) + (strip,) * len(along_rows),
         in_specs=[VMEM] * 4 + [ANY],
-        out_specs=(VMEM,) * (4 + len(along_rows)),
-        cost_estimate=WORK,
+        out_specs=(VMEM,) * (3 + len(along_rows)),
         compiler_params=PARAMS,
         name="partial_step",
     )(*cells, old_beams[0])
     partial = outs[:2]
-    new_far = [paired(value, pairs) for value, pairs in zip((outs[3], outs[2]), along_depth)]
-    beside = [paired(value, pairs) for value, pairs in zip(outs[4:], along_rows)]
-    inner = pl.pallas_call(
+    new_a = paired(outs[2], along_depth[0])
+    beside = [lax.all_gather(value, "rows") for value in outs[3:]]
+    *inner, new_b = pl.pallas_call(
         inner_kernel,
-        out_shape=(whole,) * 4 + (strip,),
+        out_shape=(whole,) * 4 + (strip, pair),
         in_specs=[VMEM] * (6 + len(beside)),
-        out_specs=(VMEM,) * 5,
-        cost_estimate=WORK,
+        out_specs=(VMEM,) * 6,
         compiler_params=PARAMS,
         name="inner_cells",
     )(*cells, *partial, *beside)
-
-    corner = f32((4, columns))
-    corners = pl.pallas_call(
-        corner_kernel,
-        out_shape=(corner,) * len(along_rows),
-        in_specs=[VMEM] * 2 + [ANY],
-        out_specs=(VMEM,) * len(along_rows),
+    new_far = [new_a, paired(new_b, along_depth[1])]
+
+    corner = pl.pallas_call(
+        functools.partial(corner_kernel, depth),
+        out_shape=f32((4, columns)),
+        in_specs=[VMEM] * len(beside),
+        out_specs=VMEM,
         compiler_params=PARAMS,
         name="corner_rows",
-    )(*old_far[::-1], inner[4])
-    corners = [paired(value, pairs) for value, pairs in zip(corners, along_rows)]
+    )(*beside)
+    corner = paired(corner, along_depth[0])
     fed, auto, middle = pl.pallas_call(
-        functools.partial(second_kernel, len(corners)),
+        second_kernel,
         out_shape=(whole, whole, f32((5, rows, columns))),
-        in_specs=[VMEM] * (13 + len(corners)),
+        in_specs=[VMEM] * 13,
         out_specs=(VMEM,) * 3,
         cost_estimate=WORK,
         compiler_params=PARAMS,
         name="second_step",
-    )(*cells, extinction, mix, *inner, *old_far, *corners)
+    )(*cells, extinction, mix, *inner, *old_far)
 
     block = columns // count
     group = packing(rows, block)
@@ -419,11 +434,11 @@
     fed, auto, part = pl.pallas_call(
         functools.partial(shade_kernel, count),
         out_shape=(held, held, f32((count, 4 * rows // group, LANES) if group else (4, rows, columns))),
-        in_specs=[VMEM] * 7,
+        in_specs=[VMEM] * 8,
         out_specs=(VMEM,) * 3,
         compiler_params=PARAMS,
         name="shading",
-    )(fed, auto, extinction, mix, middle, *new_far[::-1])
+    )(fed, auto, extinction, mix, middle, *new_far, corner)
     if not group:
         part = jnp.transpose(part.reshape(4 * rows, count, block), (1, 0, 2))
     part = lax.all_to_all(part, "depth", 0, 0)

time: 34 us -> 33.9 us (level)
  waiting for transfers between devices: 7.29 us -> 3.29 us
  starting transfers between devices: 6.18 us -> 9.13 us
  blocking collectives: 15.9 us -> 16.9 us
    ppermute x6 -> x5, waiting for transfers between devices: 7.29 us -> 3.29 us  [paired(): return lax.ppermute(value, ('depth', 'rows'), pairs)]
    ppermute x6 -> x5, starting transfers between devices: 6.18 us -> 9.13 us  [paired(): return lax.ppermute(value, ('depth', 'rows'), pairs)]
    all_gather x0 -> x1, blocking collectives: none -> 1.89 us  [body(): beside = [lax.all_gather(value, 'rows') for value in outs[3:]]]
    all_to_all x1, blocking collectives: 15.9 us -> 15 us  [body(): part = lax.all_to_all(part, 'depth', 0, 0)]
  transfers between devices with their start and end apart: 6 -> 5, of which waited for: 4 -> 1; matrix products, arithmetic and copies ran while one was open for 0% -> 0% of each run, Pallas kernels for 4% -> 4%
where the time goes in v7:
time: 33.9 us; the launch traced here: 33.7 us
  blocking collectives  16.9 us (50%)
  starting transfers between devices  9.13 us (27%)
  Pallas kernels  3.64 us (11%)
  waiting for transfers between devices  3.29 us (10%)
  between operations  0.72 us (2%)
    all_to_all x1, blocking collectives, body(): part = lax.all_to_all(part, 'depth', 0, 0)  15 us
    ppermute x5, starting transfers between devices, paired(): return lax.ppermute(value, ('depth', 'rows'), pairs)  9.13 us
    ppermute x5, waiting for transfers between devices, paired(): return lax.ppermute(value, ('depth', 'rows'), pairs)  3.29 us
    all_gather x1, blocking collectives, body(): beside = [lax.all_gather(value, 'rows') for value in outs[3:]]  1.89 us
    pallas_call x1, Pallas kernels, body(): pl.pallas_call(old_kernel, out_shape=(pair, pair, f32((9, columns))), in_...  1.08 us
    pallas_call x1, Pallas kernels, body(): pl.pallas_call(functools.partial(last_kernel, group or 1), out_shape=(ima...  0.82 us
  transfers between devices with their start and end apart: 5, of which 1 were waited for; matrix products, arithmetic and copies ran while one was open for 0% of the time, Pallas kernels for 4%

profile of v7, /device:TPU:0, one launch (start us, length us, event | category | flops | bytes accessed | tf_op | source)
XLA Modules:
  0.0 33.7 jit_solution(16325747172979643017)
XLA Ops:
  0.6 0.0 copy-start.3
  0.6 0.0 copy-start.2
  0.7 0.0 copy-start.1
  0.7 0.0 copy-start
  0.7 1.1 %old_layers.1 = (f32[2,16,1024]{2,1,0:T(8,128)S(1)}, f32[2,16,1024]{2,1,0:T(8,128)S(1)}, f32[9,1024]{1,0:T(8,128)S(1)}) custom-call(f32[4,16,1024]{2,1,0:T(8,128)} %refs_0_.3, f32[4,16,1024]{2,1,0:T(8,128)} %refs_1_.3, f32[3,3]{1,0:T(4,128)} %palette_hbm.1, f32[4,16,1024]{2,1,0:T(8,128)} %refs_2_.4, f32[4,16,1024]{2,1,0:T(8,128)} %refs_3_.1, ...), custom_call_target="tpu_custom_call" | custom-call | flops 20000000 | bytes 4000000 | tf_op jit(solution)/shard_map/old_layers/pallas_call | solution.py:378
  1.8 3.0 %collective-permute-start = (f32[2,16,1024]{2,1,0:T(8,128)S(1)}, f32[2,16,1024]{2,1,0:T(8,128)S(1)}, u32[]{:S(2)}, u32[]{:S(2)}) collective-permute-start(f32[2,16,1024]{2,1,0:T(8,128)S(1)} %get-tuple-element.35), channel_id=1, source_target_pairs={{0,2},{1,3},{2,0},{3,1},{4,6},{5,7},{6,4},{7,5},{8,10},{9,11},{10,... | collective-permute-start | bytes 393224 | tf_op jit(solution)/shard_map/ppermute | solution.py:43
  4.8 0.0 collective-permute-start.1
  4.8 0.0 copy-done.3
  4.8 0.0 copy-done.2
  4.8 0.0 copy-done.1
  4.8 0.0 copy-done
  4.8 0.5 %partial_step.1 = (f32[4,16,1024]{2,1,0:T(8,128)S(1)}, f32[4,16,1024]{2,1,0:T(8,128)S(1)}, f32[2,16,1024]{2,1,0:T(8,128)S(1)}, f32[16,1024]{1,0:T(8,128)S(1)}) custom-call(f32[4,16,1024]{2,1,0:T(8,128)S(1)} %copy-done, f32[4,16,1024]{2,1,0:T(8,128)S(1)} %copy-done.1, f32[4,16,1024]{2,1,0:T(8,128)S(1)} %copy-done.2, f32[4,16,1024]{2,1,0:T(8,128)S(1)} %copy-done.3, ...), custom_call_target="tpu_custom_call" | custom-call | tf_op jit(solution)/shard_map/partial_step/pallas_call | solution.py:391
  5.3 3.0 %collective-permute-start.2 = (f32[2,16,1024]{2,1,0:T(8,128)S(1)}, f32[2,16,1024]{2,1,0:T(8,128)S(1)}, u32[]{:S(2)}, u32[]{:S(2)}) collective-permute-start(f32[2,16,1024]{2,1,0:T(8,128)S(1)} %get-tuple-element.39), channel_id=1, source_target_pairs={{0,2},{1,3},{2,0},{3,1},{4,6},{5,7},{6,4},{7,5},{8,10},{9,11},{10,... | collective-permute-start | bytes 393224 | tf_op jit(solution)/shard_map/ppermute | solution.py:43
  8.3 1.9 %all-gather = f32[32,1024]{1,0:T(8,128)S(1)} all-gather(f32[16,1024]{1,0:T(8,128)S(1)} %get-tuple-element.29), channel_id=2, replica_groups=mesh['depth'=16,'rows'=2] {'rows'}, dimensions={0}, use_global_device_ids=true | all-gather | bytes 196608 | tf_op jit(solution)/shard_map/all_gather | solution.py:401
  10.2 0.0 copy-start.4
  10.2 0.3 inner_cells.1
  10.5 0.2 collective-permute-start.3
  10.8 2.9 %collective-permute-start.4 = (f32[4,1024]{1,0:T(4,128)S(1)}, f32[4,1024]{1,0:T(4,128)S(1)}, u32[]{:S(2)}, u32[]{:S(2)}) collective-permute-start(f32[4,1024]{1,0:T(4,128)S(1)} %corner_rows.1), channel_id=1, source_target_pairs={{0,2},{1,3},{2,0},{3,1},{4,6},{5,7},{6,4},{7,5},{8,10},{9,11},{10,... | collective-permute-start | bytes 49160 | tf_op jit(solution)/shard_map/ppermute | solution.py:43
  13.7 0.0 collective-permute-done.refs_11_
  13.7 0.0 collective-permute-done.1.refs_12_
  13.7 0.0 copy-done.4
  13.7 0.5 %second_step.1 = (f32[4,16,1024]{2,1,0:T(8,128)S(1)}, f32[4,16,1024]{2,1,0:T(8,128)S(1)}, f32[5,16,1024]{2,1,0:T(8,128)S(1)}) custom-call(f32[4,16,1024]{2,1,0:T(8,128)S(1)} %copy-done, f32[4,16,1024]{2,1,0:T(8,128)S(1)} %copy-done.1, f32[4,16,1024]{2,1,0:T(8,128)S(1)} %copy-done.2, f32[4,16,1024]{2,1,0:T(8,128)S(1)} %copy-done.3, ...), custom_call_target="tpu_custom_call" | custom-call | flops 20000000 | bytes 4000000 | tf_op jit(solution)/shard_map/second_step/pallas_call | solution.py:421
  14.2 3.3 %collective-permute-done.4.refs_7_ = f32[4,1024]{1,0:T(4,128)S(1)} collective-permute-done((f32[4,1024]{1,0:T(4,128)S(1)}, f32[4,1024]{1,0:T(4,128)S(1)}, u32[]{:S(2)}, u32[]{:S(2)}) %collective-permute-start.4) | collective-permute-done | bytes 16416 | tf_op jit(solution)/shard_map/ppermute | solution.py:43
  17.5 0.0 collective-permute-done.2.refs_5_
  17.5 0.0 collective-permute-done.3.refs_6_
  17.5 0.4 %shading.1 = (f32[4,16,1024]{2,1,0:T(8,128)S(1)}, f32[4,16,1024]{2,1,0:T(8,128)S(1)}, f32[16,32,128]{2,1,0:T(8,128)S(1)}) custom-call(f32[4,16,1024]{2,1,0:T(8,128)S(1)} %get-tuple-element.36.refs_0_, f32[4,16,1024]{2,1,0:T(8,128)S(1)} %get-tuple-element.37.refs_1_, f32[4,16,1024]{2,1,0:T(8,128)S(1)} %copy-done.4, ...), custom_call_target="tpu_custom_call" | custom-call | tf_op jit(solution)/shard_map/shading/pallas_call | solution.py:434
  17.9 15.0 %all_to_all.5.part_ref = f32[16,32,128]{2,1,0:T(8,128)S(1)} all-to-all(f32[16,32,128]{2,1,0:T(8,128)S(1)} %get-tuple-element.41), channel_id=1, replica_groups=mesh['depth'=16,'rows'=2] {'depth'}, dimensions={0} | all-to-all | bytes 524288 | tf_op jit(solution)/shard_map/all_to_all | solution.py:444
  32.9 0.8 %front_to_back.1 = (f32[4,16,64]{2,1,0:T(8,128)}, f32[4,16,1024]{2,1,0:T(8,128)}, f32[4,16,1024]{2,1,0:T(8,128)}) custom-call(f32[16,32,128]{2,1,0:T(8,128)S(1)} %all_to_all.5.part_ref, f32[4,16,1024]{2,1,0:T(8,128)S(1)} %get-tuple-element.42.fed_ref, f32[4,16,1024]{2,1,0:T(8,128)S(1)} %get-tuple-element.43.auto_ref), custom_call_target="tpu_custom_call" | custom-call | tf_op jit(solution)/shard_map/front_to_back/pallas_call | solution.py:446
  (1 shorter events, 0.0 us)
Async XLA Ops:
  0.6 4.1 %copy-start.3 = (f32[4,16,1024]{2,1,0:T(8,128)S(1)}, f32[4,16,1024]{2,1,0:T(8,128)}, u32[]{:S(2)}) copy-start(f32[4,16,1024]{2,1,0:T(8,128)} %refs_3_.1) | copy-start | bytes 786436
  0.6 4.1 %copy-start.2 = (f32[4,16,1024]{2,1,0:T(8,128)S(1)}, f32[4,16,1024]{2,1,0:T(8,128)}, u32[]{:S(2)}) copy-start(f32[4,16,1024]{2,1,0:T(8,128)} %refs_2_.4) | copy-start | bytes 786436
  0.7 4.1 %copy-start.1 = (f32[4,16,1024]{2,1,0:T(8,128)S(1)}, f32[4,16,1024]{2,1,0:T(8,128)}, u32[]{:S(2)}) copy-start(f32[4,16,1024]{2,1,0:T(8,128)} %refs_1_.3) | copy-start | bytes 786436
  0.7 4.1 %copy-start = (f32[4,16,1024]{2,1,0:T(8,128)S(1)}, f32[4,16,1024]{2,1,0:T(8,128)}, u32[]{:S(2)}) copy-start(f32[4,16,1024]{2,1,0:T(8,128)} %refs_0_.3) | copy-start | bytes 786436
  1.8 11.9 %collective-permute-start = (f32[2,16,1024]{2,1,0:T(8,128)S(1)}, f32[2,16,1024]{2,1,0:T(8,128)S(1)}, u32[]{:S(2)}, u32[]{:S(2)}) collective-permute-start(f32[2,16,1024]{2,1,0:T(8,128)S(1)} %get-tuple-element.35), channel_id=1, source_target_pairs={{0,2},{1,3},{2,0},{3,1},{4,6},{5,7},{6,4},{7,5},{8,10},{9,11},{10,... | collective-permute-start | bytes 393224 | tf_op jit(solution)/shard_map/ppermute | solution.py:43
  4.8 8.9 %collective-permute-start.1 = (f32[2,16,1024]{2,1,0:T(8,128)S(1)}, f32[2,16,1024]{2,1,0:T(8,128)S(1)}, u32[]{:S(2)}, u32[]{:S(2)}) collective-permute-start(f32[2,16,1024]{2,1,0:T(8,128)S(1)} %get-tuple-element.26._), channel_id=1, source_target_pairs={{0,1},{1,0},{2,4},{3,5},{4,2},{5,3},{6,8},{7,9},{8,6},{9,7},{10,12... | collective-permute-start | bytes 393224 | tf_op jit(solution)/shard_map/ppermute | solution.py:43
  5.3 12.2 %collective-permute-start.2 = (f32[2,16,1024]{2,1,0:T(8,128)S(1)}, f32[2,16,1024]{2,1,0:T(8,128)S(1)}, u32[]{:S(2)}, u32[]{:S(2)}) collective-permute-start(f32[2,16,1024]{2,1,0:T(8,128)S(1)} %get-tuple-element.39), channel_id=1, source_target_pairs={{0,2},{1,3},{2,0},{3,1},{4,6},{5,7},{6,4},{7,5},{8,10},{9,11},{10,... | collective-permute-start | bytes 393224 | tf_op jit(solution)/shard_map/ppermute | solution.py:43
  10.2 3.5 %copy-start.4 = (f32[4,16,1024]{2,1,0:T(8,128)S(1)}, f32[4,16,1024]{2,1,0:T(8,128)}, u32[]{:S(2)}) copy-start(f32[4,16,1024]{2,1,0:T(8,128)} %refs_2_.5) | copy-start | bytes 786436
  10.5 6.9 %collective-permute-start.3 = (f32[2,16,1024]{2,1,0:T(8,128)S(1)}, f32[2,16,1024]{2,1,0:T(8,128)S(1)}, u32[]{:S(2)}, u32[]{:S(2)}) collective-permute-start(f32[2,16,1024]{2,1,0:T(8,128)S(1)} %get-tuple-element.40), channel_id=1, source_target_pairs={{0,1},{1,0},{2,4},{3,5},{4,2},{5,3},{6,8},{7,9},{8,6},{9,7},{10,12... | collective-permute-start | bytes 393224 | tf_op jit(solution)/shard_map/ppermute | solution.py:43
  10.8 6.7 %collective-permute-start.4 = (f32[4,1024]{1,0:T(4,128)S(1)}, f32[4,1024]{1,0:T(4,128)S(1)}, u32[]{:S(2)}, u32[]{:S(2)}) collective-permute-start(f32[4,1024]{1,0:T(4,128)S(1)} %corner_rows.1), channel_id=1, source_target_pairs={{0,2},{1,3},{2,0},{3,1},{4,6},{5,7},{6,4},{7,5},{8,10},{9,11},{10,... | collective-permute-start | bytes 49160 | tf_op jit(solution)/shard_map/ppermute | solution.py:43

commit v8 on v7

--- a/solution.py
+++ b/solution.py
@@ -87,24 +87,18 @@
     return react(s_ref[layer], c_ref[layer], near[0], near[1], feed, kill)
 
 
-def old_kernel(s_hbm, c_hbm, palette_hbm, *refs):
-    b_ref, a_ref, mix_ref, palette, arrived = refs[-5:]
-    depth, _, columns = s_hbm.shape
+def old_kernel(s_hbm, c_hbm, *refs):
+    b_ref, a_ref, arrived = refs[-3:]
+    depth = s_hbm.shape[0]
     even = is_even("depth")
     copies = []
     for n, (out, towards_next) in enumerate(((a_ref, even), (b_ref, jnp.logical_not(even)))):
         layer = jnp.where(towards_next, depth - 1, 0)
         for i, hbm in enumerate((s_hbm, c_hbm)):
             copies.append(pltpu.make_async_copy(hbm.at[layer], out.at[i], arrived.at[n, i]))
-    copies.append(pltpu.make_async_copy(palette_hbm, palette, arrived.at[2, 0]))
     for copy in copies:
         copy.start()
-    copies[-1].wait()
-    for channel in range(3):
-        for n, scale in enumerate((8.0, 8.0, 1.0)):
-            at = 3 * channel + n
-            mix_ref[at : at + 1] = jnp.full((1, columns), scale * palette[channel, n], jnp.float32)
-    for copy in copies[:-1]:
+    for copy in copies:
         copy.wait()
 
 
@@ -220,10 +214,14 @@
 
 
 def second_kernel(*refs):
-    s_ref, c_ref, f_ref, k_ref, e_ref, mix_ref = refs[:6]
+    s_ref, c_ref, f_ref, k_ref, e_ref, palette = refs[:6]
     fed_one, auto_one, fed_mid, auto_mid, outer_ref = refs[6:11]
     far = refs[11:13]
-    fed_two, auto_two, middle_ref = refs[13:]
+    fed_two, auto_two, middle_ref, mix_ref = refs[13:]
+    for channel in range(3):
+        for n, scale in enumerate((8.0, 8.0, 1.0)):
+            at = 3 * channel + n
+            mix_ref[at : at + 1] = jnp.full((1, s_ref.shape[2]), scale * palette[channel, n], jnp.float32)
     depth = s_ref.shape[0]
     index, last = lax.axis_index("depth"), lax.axis_size("depth") - 1
     inside = (index > 0, index < last)
@@ -375,16 +373,16 @@
     cells = (substrate, catalyst, feed_rate, kill_rate)
     pair = f32((2, rows, columns))
     in_hbm = lambda x: pltpu.with_memory_space_constraint(x, pltpu.HBM)
-    *old_beams, mix = pl.pallas_call(
+    old_beams = pl.pallas_call(
         old_kernel,
-        out_shape=(pair, pair, f32((9, columns))),
-        in_specs=[HBM] * 6,
-        out_specs=(VMEM,) * 3,
-        scratch_shapes=[pltpu.SMEM(palette.shape, jnp.float32), pltpu.SemaphoreType.DMA((3, 2))],
+        out_shape=(pair, pair),
+        in_specs=[HBM] * 5,
+        out_specs=(VMEM,) * 2,
+        scratch_shapes=[pltpu.SemaphoreType.DMA((2, 2))],
         cost_estimate=WORK,
         compiler_params=PARAMS,
         name="old_layers",
-    )(*(in_hbm(x) for x in (substrate, catalyst, palette, feed_rate, kill_rate, extinction)))
+    )(*(in_hbm(x) for x in (substrate, catalyst, feed_rate, kill_rate, extinction)))
     old_far = [paired(value, pairs) for value, pairs in zip(old_beams[::-1], along_depth)]
 
     strip = f32((4 * depth, columns))
@@ -418,15 +416,15 @@
         name="corner_rows",
     )(*beside)
     corner = paired(corner, along_depth[0])
-    fed, auto, middle = pl.pallas_call(
+    fed, auto, middle, mix = pl.pallas_call(
         second_kernel,
-        out_shape=(whole, whole, f32((5, rows, columns))),
-        in_specs=[VMEM] * 13,
-        out_specs=(VMEM,) * 3,
+        out_shape=(whole, whole, f32((5, rows, columns)), f32((9, columns))),
+        in_specs=[VMEM] * 5 + [SMEM] + [VMEM] * 7,
+        out_specs=(VMEM,) * 4,
         cost_estimate=WORK,
         compiler_params=PARAMS,
         name="second_step",
-    )(*cells, extinction, mix, *inner, *old_far)
+    )(*cells, extinction, palette, *inner, *old_far)
 
     block = columns // count
     group = packing(rows, block)

time: 33.9 us -> 33.9 us (level)
  waiting for transfers between devices: 3.29 us -> 2.03 us
  local copies, waits for them, and re-layouts: 0.02 us -> 0.69 us
  Pallas kernels: 3.64 us -> 4.26 us
    ppermute x5, waiting for transfers between devices: 3.29 us -> 2.03 us  [paired(): return lax.ppermute(value, ('depth', 'rows'), pairs)]
    unnamed x10 -> x12, local copies, waits for them, and re-layouts: 0.02 us -> 0.69 us
    pallas_call x1, Pallas kernels: 0.51 us -> 1.1 us  [body(): pl.pallas_call(second_kernel, out_shape=(whole, whole, f32((5, rows, colu...]
  transfers between devices with their start and end apart: 5 -> 5, of which waited for: 1 -> 1; matrix products, arithmetic and copies ran while one was open for 0% -> 0% of each run, Pallas kernels for 4% -> 6%
where the time goes in v8:
time: 33.9 us; the launch traced here: 33.7 us
  blocking collectives  16.8 us (50%)
  starting transfers between devices  9.13 us (27%)
  Pallas kernels  4.26 us (13%)
  waiting for transfers between devices  2.03 us (6%)
  between operations  0.72 us (2%)
  local copies, waits for them, and re-layouts  0.69 us (2%)
    all_to_all x1, blocking collectives, body(): part = lax.all_to_all(part, 'depth', 0, 0)  15 us
    ppermute x5, starting transfers between devices, paired(): return lax.ppermute(value, ('depth', 'rows'), pairs)  9.13 us
    ppermute x5, waiting for transfers between devices, paired(): return lax.ppermute(value, ('depth', 'rows'), pairs)  2.03 us
    all_gather x1, blocking collectives, body(): beside = [lax.all_gather(value, 'rows') for value in outs[3:]]  1.89 us
    pallas_call x1, Pallas kernels, body(): pl.pallas_call(second_kernel, out_shape=(whole, whole, f32((5, rows, colu...  1.1 us
    pallas_call x1, Pallas kernels, body(): pl.pallas_call(old_kernel, out_shape=(pair, pair), in_specs=[HBM] * 5, ou...  1.06 us
    pallas_call x1, Pallas kernels, body(): pl.pallas_call(functools.partial(last_kernel, group or 1), out_shape=(ima...  0.82 us
    unnamed x12, local copies, waits for them, and re-layouts  0.69 us
  transfers between devices with their start and end apart: 5, of which 1 were waited for; matrix products, arithmetic and copies ran while one was open for 0% of the time, Pallas kernels for 6%

profile of v8, /device:TPU:0, one launch (start us, length us, event | category | flops | bytes accessed | tf_op | source)
XLA Modules:
  0.0 33.7 jit_solution(3832224403318212864)
XLA Ops:
  0.6 0.0 copy-start.3
  0.6 0.0 copy-start.2
  0.7 0.0 copy-start.1
  0.7 0.0 copy-start
  0.7 1.1 %old_layers.1 = (f32[2,16,1024]{2,1,0:T(8,128)S(1)}, f32[2,16,1024]{2,1,0:T(8,128)S(1)}) custom-call(f32[4,16,1024]{2,1,0:T(8,128)} %refs_0_.3, f32[4,16,1024]{2,1,0:T(8,128)} %refs_1_.3, f32[4,16,1024]{2,1,0:T(8,128)} %refs_2_.4, f32[4,16,1024]{2,1,0:T(8,128)} %refs_3_.1, f32[4,16,1024]{2,1,0:T(8,128)} %refs_2_.5), custom_call_target="tpu_custom_call" | custom-call | flops 20000000 | bytes 4000000 | tf_op jit(solution)/shard_map/old_layers/pallas_call | solution.py:376
  1.7 3.0 %collective-permute-start = (f32[2,16,1024]{2,1,0:T(8,128)S(1)}, f32[2,16,1024]{2,1,0:T(8,128)S(1)}, u32[]{:S(2)}, u32[]{:S(2)}) collective-permute-start(f32[2,16,1024]{2,1,0:T(8,128)S(1)} %get-tuple-element.34), channel_id=1, source_target_pairs={{0,2},{1,3},{2,0},{3,1},{4,6},{5,7},{6,4},{7,5},{8,10},{9,11},{10,... | collective-permute-start | bytes 393224 | tf_op jit(solution)/shard_map/ppermute | solution.py:43
  4.7 0.0 collective-permute-start.1
  4.7 0.0 copy-done.3
  4.8 0.0 copy-done.2
  4.8 0.0 copy-done.1
  4.8 0.0 copy-done
  4.8 0.5 %partial_step.1 = (f32[4,16,1024]{2,1,0:T(8,128)S(1)}, f32[4,16,1024]{2,1,0:T(8,128)S(1)}, f32[2,16,1024]{2,1,0:T(8,128)S(1)}, f32[16,1024]{1,0:T(8,128)S(1)}) custom-call(f32[4,16,1024]{2,1,0:T(8,128)S(1)} %copy-done, f32[4,16,1024]{2,1,0:T(8,128)S(1)} %copy-done.1, f32[4,16,1024]{2,1,0:T(8,128)S(1)} %copy-done.2, f32[4,16,1024]{2,1,0:T(8,128)S(1)} %copy-done.3, ...), custom_call_target="tpu_custom_call" | custom-call | tf_op jit(solution)/shard_map/partial_step/pallas_call | solution.py:389
  5.3 3.0 %collective-permute-start.2 = (f32[2,16,1024]{2,1,0:T(8,128)S(1)}, f32[2,16,1024]{2,1,0:T(8,128)S(1)}, u32[]{:S(2)}, u32[]{:S(2)}) collective-permute-start(f32[2,16,1024]{2,1,0:T(8,128)S(1)} %get-tuple-element.39), channel_id=1, source_target_pairs={{0,2},{1,3},{2,0},{3,1},{4,6},{5,7},{6,4},{7,5},{8,10},{9,11},{10,... | collective-permute-start | bytes 393224 | tf_op jit(solution)/shard_map/ppermute | solution.py:43
  8.3 1.9 %all-gather = f32[32,1024]{1,0:T(8,128)S(1)} all-gather(f32[16,1024]{1,0:T(8,128)S(1)} %get-tuple-element.28), channel_id=2, replica_groups=mesh['depth'=16,'rows'=2] {'rows'}, dimensions={0}, use_global_device_ids=true | all-gather | bytes 196608 | tf_op jit(solution)/shard_map/all_gather | solution.py:399
  10.2 0.0 copy-start.4
  10.2 0.4 %inner_cells.1 = (f32[4,16,1024]{2,1,0:T(8,128)S(1)}, f32[4,16,1024]{2,1,0:T(8,128)S(1)}, f32[4,16,1024]{2,1,0:T(8,128)S(1)}, f32[4,16,1024]{2,1,0:T(8,128)S(1)}...) custom-call(f32[4,16,1024]{2,1,0:T(8,128)S(1)} %copy-done, f32[4,16,1024]{2,1,0:T(8,128)S(1)} %copy-done.1, ...), custom_call_target="tpu_custom_call" | custom-call | tf_op jit(solution)/shard_map/inner_cells/pallas_call | solution.py:400
  10.5 0.2 collective-permute-start.3
  10.8 2.9 %collective-permute-start.4 = (f32[4,1024]{1,0:T(4,128)S(1)}, f32[4,1024]{1,0:T(4,128)S(1)}, u32[]{:S(2)}, u32[]{:S(2)}) collective-permute-start(f32[4,1024]{1,0:T(4,128)S(1)} %corner_rows.1), channel_id=1, source_target_pairs={{0,2},{1,3},{2,0},{3,1},{4,6},{5,7},{6,4},{7,5},{8,10},{9,11},{10,... | collective-permute-start | bytes 49160 | tf_op jit(solution)/shard_map/ppermute | solution.py:43
  13.7 0.0 collective-permute-done.refs_11_
  13.7 0.0 collective-permute-done.1.refs_12_
  13.7 0.0 copy-start.5
  13.7 0.0 copy-done.4
  13.7 0.7 %copy-done.5 = f32[3,3]{1,0:T(4,128)S(1)} copy-done((f32[3,3]{1,0:T(4,128)S(1)}, f32[3,3]{1,0:T(4,128)}, u32[]{:S(2)}) %copy-start.5) | copy-done | bytes 60
  14.4 1.1 %second_step.1 = (f32[4,16,1024]{2,1,0:T(8,128)S(1)}, f32[4,16,1024]{2,1,0:T(8,128)S(1)}, f32[5,16,1024]{2,1,0:T(8,128)S(1)}, f32[9,1024]{1,0:T(8,128)S(1)}) custom-call(f32[4,16,1024]{2,1,0:T(8,128)S(1)} %copy-done, f32[4,16,1024]{2,1,0:T(8,128)S(1)} %copy-done.1, f32[4,16,1024]{2,1,0:T(8,128)S(1)} %copy-done.2, f32[4,16,1024]{2,1,0:T(8,128)S(1)} %copy-done.3, ...), custom_call_target="tpu_custom_call" | custom-call | flops 20000000 | bytes 4000000 | tf_op jit(solution)/shard_map/second_step/pallas_call | solution.py:419
  15.5 2.0 %collective-permute-done.4.refs_7_ = f32[4,1024]{1,0:T(4,128)S(1)} collective-permute-done((f32[4,1024]{1,0:T(4,128)S(1)}, f32[4,1024]{1,0:T(4,128)S(1)}, u32[]{:S(2)}, u32[]{:S(2)}) %collective-permute-start.4) | collective-permute-done | bytes 16416 | tf_op jit(solution)/shard_map/ppermute | solution.py:43
  17.5 0.0 collective-permute-done.2.refs_5_
  17.5 0.0 collective-permute-done.3.refs_6_
  17.5 0.4 %shading.1 = (f32[4,16,1024]{2,1,0:T(8,128)S(1)}, f32[4,16,1024]{2,1,0:T(8,128)S(1)}, f32[16,32,128]{2,1,0:T(8,128)S(1)}) custom-call(f32[4,16,1024]{2,1,0:T(8,128)S(1)} %get-tuple-element.35.refs_0_, f32[4,16,1024]{2,1,0:T(8,128)S(1)} %get-tuple-element.36.refs_1_, f32[4,16,1024]{2,1,0:T(8,128)S(1)} %copy-done.4, f32[9,1024]{1,0:T(8,128)S(1)} %get-tuple-element.37.refs_3_, ...), custom_call_target="tpu_custom_call" | custom-call | tf_op jit(solution)/shard_map/shading/pallas_call | solution.py:432
  17.9 15.0 %all_to_all.5.part_ref = f32[16,32,128]{2,1,0:T(8,128)S(1)} all-to-all(f32[16,32,128]{2,1,0:T(8,128)S(1)} %get-tuple-element.41), channel_id=1, replica_groups=mesh['depth'=16,'rows'=2] {'depth'}, dimensions={0} | all-to-all | bytes 524288 | tf_op jit(solution)/shard_map/all_to_all | solution.py:442
  32.9 0.8 %front_to_back.1 = (f32[4,16,64]{2,1,0:T(8,128)}, f32[4,16,1024]{2,1,0:T(8,128)}, f32[4,16,1024]{2,1,0:T(8,128)}) custom-call(f32[16,32,128]{2,1,0:T(8,128)S(1)} %all_to_all.5.part_ref, f32[4,16,1024]{2,1,0:T(8,128)S(1)} %get-tuple-element.42.fed_ref, f32[4,16,1024]{2,1,0:T(8,128)S(1)} %get-tuple-element.43.auto_ref), custom_call_target="tpu_custom_call" | custom-call | tf_op jit(solution)/shard_map/front_to_back/pallas_call | solution.py:444
  (1 shorter events, 0.0 us)
Async XLA Ops:
  0.6 4.1 %copy-start.3 = (f32[4,16,1024]{2,1,0:T(8,128)S(1)}, f32[4,16,1024]{2,1,0:T(8,128)}, u32[]{:S(2)}) copy-start(f32[4,16,1024]{2,1,0:T(8,128)} %refs_3_.1) | copy-start | bytes 786436
  0.6 4.1 %copy-start.2 = (f32[4,16,1024]{2,1,0:T(8,128)S(1)}, f32[4,16,1024]{2,1,0:T(8,128)}, u32[]{:S(2)}) copy-start(f32[4,16,1024]{2,1,0:T(8,128)} %refs_2_.4) | copy-start | bytes 786436
  0.7 4.1 %copy-start.1 = (f32[4,16,1024]{2,1,0:T(8,128)S(1)}, f32[4,16,1024]{2,1,0:T(8,128)}, u32[]{:S(2)}) copy-start(f32[4,16,1024]{2,1,0:T(8,128)} %refs_1_.3) | copy-start | bytes 786436
  0.7 4.1 %copy-start = (f32[4,16,1024]{2,1,0:T(8,128)S(1)}, f32[4,16,1024]{2,1,0:T(8,128)}, u32[]{:S(2)}) copy-start(f32[4,16,1024]{2,1,0:T(8,128)} %refs_0_.3) | copy-start | bytes 786436
  1.7 11.9 %collective-permute-start = (f32[2,16,1024]{2,1,0:T(8,128)S(1)}, f32[2,16,1024]{2,1,0:T(8,128)S(1)}, u32[]{:S(2)}, u32[]{:S(2)}) collective-permute-start(f32[2,16,1024]{2,1,0:T(8,128)S(1)} %get-tuple-element.34), channel_id=1, source_target_pairs={{0,2},{1,3},{2,0},{3,1},{4,6},{5,7},{6,4},{7,5},{8,10},{9,11},{10,... | collective-permute-start | bytes 393224 | tf_op jit(solution)/shard_map/ppermute | solution.py:43
  4.7 8.9 %collective-permute-start.1 = (f32[2,16,1024]{2,1,0:T(8,128)S(1)}, f32[2,16,1024]{2,1,0:T(8,128)S(1)}, u32[]{:S(2)}, u32[]{:S(2)}) collective-permute-start(f32[2,16,1024]{2,1,0:T(8,128)S(1)} %get-tuple-element.25._), channel_id=1, source_target_pairs={{0,1},{1,0},{2,4},{3,5},{4,2},{5,3},{6,8},{7,9},{8,6},{9,7},{10,12... | collective-permute-start | bytes 393224 | tf_op jit(solution)/shard_map/ppermute | solution.py:43
  5.3 12.2 %collective-permute-start.2 = (f32[2,16,1024]{2,1,0:T(8,128)S(1)}, f32[2,16,1024]{2,1,0:T(8,128)S(1)}, u32[]{:S(2)}, u32[]{:S(2)}) collective-permute-start(f32[2,16,1024]{2,1,0:T(8,128)S(1)} %get-tuple-element.39), channel_id=1, source_target_pairs={{0,2},{1,3},{2,0},{3,1},{4,6},{5,7},{6,4},{7,5},{8,10},{9,11},{10,... | collective-permute-start | bytes 393224 | tf_op jit(solution)/shard_map/ppermute | solution.py:43
  10.2 3.5 %copy-start.4 = (f32[4,16,1024]{2,1,0:T(8,128)S(1)}, f32[4,16,1024]{2,1,0:T(8,128)}, u32[]{:S(2)}) copy-start(f32[4,16,1024]{2,1,0:T(8,128)} %refs_2_.5) | copy-start | bytes 786436
  10.5 6.9 %collective-permute-start.3 = (f32[2,16,1024]{2,1,0:T(8,128)S(1)}, f32[2,16,1024]{2,1,0:T(8,128)S(1)}, u32[]{:S(2)}, u32[]{:S(2)}) collective-permute-start(f32[2,16,1024]{2,1,0:T(8,128)S(1)} %get-tuple-element.40), channel_id=1, source_target_pairs={{0,1},{1,0},{2,4},{3,5},{4,2},{5,3},{6,8},{7,9},{8,6},{9,7},{10,12... | collective-permute-start | bytes 393224 | tf_op jit(solution)/shard_map/ppermute | solution.py:43
  10.8 6.7 %collective-permute-start.4 = (f32[4,1024]{1,0:T(4,128)S(1)}, f32[4,1024]{1,0:T(4,128)S(1)}, u32[]{:S(2)}, u32[]{:S(2)}) collective-permute-start(f32[4,1024]{1,0:T(4,128)S(1)} %corner_rows.1), channel_id=1, source_target_pairs={{0,2},{1,3},{2,0},{3,1},{4,6},{5,7},{6,4},{7,5},{8,10},{9,11},{10,... | collective-permute-start | bytes 49160 | tf_op jit(solution)/shard_map/ppermute | solution.py:43
  13.7 0.7 %copy-start.5 = (f32[3,3]{1,0:T(4,128)S(1)}, f32[3,3]{1,0:T(4,128)}, u32[]{:S(2)}) copy-start(f32[3,3]{1,0:T(4,128)} %refs_5_.1) | copy-start | bytes 112

commit v9 on v8

--- a/solution.py
+++ b/solution.py
@@ -206,10 +206,11 @@
     def add(self, fed, auto, extinction):
         passing = jnp.exp(-extinction * (0.25 + 4.0 * auto * auto))
         opacity = 1.0 - passing
+        half = 0.5 * opacity
         pieces = []
         for fed_mix, auto_mix, offset in self.mix:
             level = fed_mix * (fed - 0.65) + auto_mix * (auto - 0.25) + offset
-            pieces.append(opacity / (1.0 + jnp.exp(-level)))
+            pieces.append(half + half * jnp.tanh(level))
         self.put(pieces + [opacity], passing)
 
 
@@ -219,7 +220,7 @@
     far = refs[11:13]
     fed_two, auto_two, middle_ref, mix_ref = refs[13:]
     for channel in range(3):
-        for n, scale in enumerate((8.0, 8.0, 1.0)):
+        for n, scale in enumerate((4.0, 4.0, 0.5)):
             at = 3 * channel + n
             mix_ref[at : at + 1] = jnp.full((1, s_ref.shape[2]), scale * palette[channel, n], jnp.float32)
     depth = s_ref.shape[0]

time: 33.9 us -> 33.8 us (level)
  no operation moved by 1% of the time
where the time goes in v9:
time: 33.8 us; the launch traced here: 33.6 us
  blocking collectives  16.8 us (50%)
  starting transfers between devices  9.13 us (27%)
  Pallas kernels  4.19 us (12%)
  waiting for transfers between devices  2.06 us (6%)
  between operations  0.72 us (2%)
  local copies, waits for them, and re-layouts  0.69 us (2%)
    all_to_all x1, blocking collectives, body(): part = lax.all_to_all(part, 'depth', 0, 0)  15 us
    ppermute x5, starting transfers between devices, paired(): return lax.ppermute(value, ('depth', 'rows'), pairs)  9.13 us
    ppermute x5, waiting for transfers between devices, paired(): return lax.ppermute(value, ('depth', 'rows'), pairs)  2.06 us
    all_gather x1, blocking collectives, body(): beside = [lax.all_gather(value, 'rows') for value in outs[3:]]  1.89 us
    pallas_call x1, Pallas kernels, body(): pl.pallas_call(second_kernel, out_shape=(whole, whole, f32((5, rows, colu...  1.07 us
    pallas_call x1, Pallas kernels, body(): pl.pallas_call(old_kernel, out_shape=(pair, pair), in_specs=[HBM] * 5, ou...  1.06 us
    pallas_call x1, Pallas kernels, body(): pl.pallas_call(functools.partial(last_kernel, group or 1), out_shape=(ima...  0.82 us
    unnamed x12, local copies, waits for them, and re-layouts  0.69 us
  transfers between devices with their start and end apart: 5, of which 1 were waited for; matrix products, arithmetic and copies ran while one was open for 0% of the time, Pallas kernels for 6%

profile of v9, /device:TPU:0, one launch (start us, length us, event | category | flops | bytes accessed | tf_op | source)
XLA Modules:
  0.0 33.6 jit_solution(12433881273254364775)
XLA Ops:
  0.6 0.0 copy-start.3
  0.6 0.0 copy-start.2
  0.7 0.0 copy-start.1
  0.7 0.0 copy-start
  0.7 1.1 %old_layers.1 = (f32[2,16,1024]{2,1,0:T(8,128)S(1)}, f32[2,16,1024]{2,1,0:T(8,128)S(1)}) custom-call(f32[4,16,1024]{2,1,0:T(8,128)} %refs_0_.3, f32[4,16,1024]{2,1,0:T(8,128)} %refs_1_.3, f32[4,16,1024]{2,1,0:T(8,128)} %refs_2_.4, f32[4,16,1024]{2,1,0:T(8,128)} %refs_3_.1, f32[4,16,1024]{2,1,0:T(8,128)} %refs_2_.5), custom_call_target="tpu_custom_call" | custom-call | flops 20000000 | bytes 4000000 | tf_op jit(solution)/shard_map/old_layers/pallas_call | solution.py:377
  1.7 3.0 %collective-permute-start = (f32[2,16,1024]{2,1,0:T(8,128)S(1)}, f32[2,16,1024]{2,1,0:T(8,128)S(1)}, u32[]{:S(2)}, u32[]{:S(2)}) collective-permute-start(f32[2,16,1024]{2,1,0:T(8,128)S(1)} %get-tuple-element.34), channel_id=1, source_target_pairs={{0,2},{1,3},{2,0},{3,1},{4,6},{5,7},{6,4},{7,5},{8,10},{9,11},{10,... | collective-permute-start | bytes 393224 | tf_op jit(solution)/shard_map/ppermute | solution.py:43
  4.7 0.0 collective-permute-start.1
  4.7 0.0 copy-done.3
  4.8 0.0 copy-done.2
  4.8 0.0 copy-done.1
  4.8 0.0 copy-done
  4.8 0.5 %partial_step.1 = (f32[4,16,1024]{2,1,0:T(8,128)S(1)}, f32[4,16,1024]{2,1,0:T(8,128)S(1)}, f32[2,16,1024]{2,1,0:T(8,128)S(1)}, f32[16,1024]{1,0:T(8,128)S(1)}) custom-call(f32[4,16,1024]{2,1,0:T(8,128)S(1)} %copy-done, f32[4,16,1024]{2,1,0:T(8,128)S(1)} %copy-done.1, f32[4,16,1024]{2,1,0:T(8,128)S(1)} %copy-done.2, f32[4,16,1024]{2,1,0:T(8,128)S(1)} %copy-done.3, ...), custom_call_target="tpu_custom_call" | custom-call | tf_op jit(solution)/shard_map/partial_step/pallas_call | solution.py:390
  5.3 3.0 %collective-permute-start.2 = (f32[2,16,1024]{2,1,0:T(8,128)S(1)}, f32[2,16,1024]{2,1,0:T(8,128)S(1)}, u32[]{:S(2)}, u32[]{:S(2)}) collective-permute-start(f32[2,16,1024]{2,1,0:T(8,128)S(1)} %get-tuple-element.39), channel_id=1, source_target_pairs={{0,2},{1,3},{2,0},{3,1},{4,6},{5,7},{6,4},{7,5},{8,10},{9,11},{10,... | collective-permute-start | bytes 393224 | tf_op jit(solution)/shard_map/ppermute | solution.py:43
  8.3 1.9 %all-gather = f32[32,1024]{1,0:T(8,128)S(1)} all-gather(f32[16,1024]{1,0:T(8,128)S(1)} %get-tuple-element.28), channel_id=2, replica_groups=mesh['depth'=16,'rows'=2] {'rows'}, dimensions={0}, use_global_device_ids=true | all-gather | bytes 196608 | tf_op jit(solution)/shard_map/all_gather | solution.py:400
  10.2 0.0 copy-start.4
  10.2 0.4 %inner_cells.1 = (f32[4,16,1024]{2,1,0:T(8,128)S(1)}, f32[4,16,1024]{2,1,0:T(8,128)S(1)}, f32[4,16,1024]{2,1,0:T(8,128)S(1)}, f32[4,16,1024]{2,1,0:T(8,128)S(1)}...) custom-call(f32[4,16,1024]{2,1,0:T(8,128)S(1)} %copy-done, f32[4,16,1024]{2,1,0:T(8,128)S(1)} %copy-done.1, ...), custom_call_target="tpu_custom_call" | custom-call | tf_op jit(solution)/shard_map/inner_cells/pallas_call | solution.py:401
  10.5 0.2 collective-permute-start.3
  10.8 2.9 %collective-permute-start.4 = (f32[4,1024]{1,0:T(4,128)S(1)}, f32[4,1024]{1,0:T(4,128)S(1)}, u32[]{:S(2)}, u32[]{:S(2)}) collective-permute-start(f32[4,1024]{1,0:T(4,128)S(1)} %corner_rows.1), channel_id=1, source_target_pairs={{0,2},{1,3},{2,0},{3,1},{4,6},{5,7},{6,4},{7,5},{8,10},{9,11},{10,... | collective-permute-start | bytes 49160 | tf_op jit(solution)/shard_map/ppermute | solution.py:43
  13.7 0.0 collective-permute-done.refs_11_
  13.7 0.0 collective-permute-done.1.refs_12_
  13.7 0.0 copy-start.5
  13.7 0.0 copy-done.4
  13.7 0.7 %copy-done.5 = f32[3,3]{1,0:T(4,128)S(1)} copy-done((f32[3,3]{1,0:T(4,128)S(1)}, f32[3,3]{1,0:T(4,128)}, u32[]{:S(2)}) %copy-start.5) | copy-done | bytes 60
  14.4 1.1 %second_step.1 = (f32[4,16,1024]{2,1,0:T(8,128)S(1)}, f32[4,16,1024]{2,1,0:T(8,128)S(1)}, f32[5,16,1024]{2,1,0:T(8,128)S(1)}, f32[9,1024]{1,0:T(8,128)S(1)}) custom-call(f32[4,16,1024]{2,1,0:T(8,128)S(1)} %copy-done, f32[4,16,1024]{2,1,0:T(8,128)S(1)} %copy-done.1, f32[4,16,1024]{2,1,0:T(8,128)S(1)} %copy-done.2, f32[4,16,1024]{2,1,0:T(8,128)S(1)} %copy-done.3, ...), custom_call_target="tpu_custom_call" | custom-call | flops 20000000 | bytes 4000000 | tf_op jit(solution)/shard_map/second_step/pallas_call | solution.py:420
  15.4 2.0 %collective-permute-done.4.refs_7_ = f32[4,1024]{1,0:T(4,128)S(1)} collective-permute-done((f32[4,1024]{1,0:T(4,128)S(1)}, f32[4,1024]{1,0:T(4,128)S(1)}, u32[]{:S(2)}, u32[]{:S(2)}) %collective-permute-start.4) | collective-permute-done | bytes 16416 | tf_op jit(solution)/shard_map/ppermute | solution.py:43
  17.5 0.0 collective-permute-done.2.refs_5_
  17.5 0.0 collective-permute-done.3.refs_6_
  17.5 0.4 %shading.1 = (f32[4,16,1024]{2,1,0:T(8,128)S(1)}, f32[4,16,1024]{2,1,0:T(8,128)S(1)}, f32[16,32,128]{2,1,0:T(8,128)S(1)}) custom-call(f32[4,16,1024]{2,1,0:T(8,128)S(1)} %get-tuple-element.35.refs_0_, f32[4,16,1024]{2,1,0:T(8,128)S(1)} %get-tuple-element.36.refs_1_, f32[4,16,1024]{2,1,0:T(8,128)S(1)} %copy-done.4, f32[9,1024]{1,0:T(8,128)S(1)} %get-tuple-element.37.refs_3_, ...), custom_call_target="tpu_custom_call" | custom-call | tf_op jit(solution)/shard_map/shading/pallas_call | solution.py:433
  17.9 15.0 %all_to_all.5.part_ref = f32[16,32,128]{2,1,0:T(8,128)S(1)} all-to-all(f32[16,32,128]{2,1,0:T(8,128)S(1)} %get-tuple-element.41), channel_id=1, replica_groups=mesh['depth'=16,'rows'=2] {'depth'}, dimensions={0} | all-to-all | bytes 524288 | tf_op jit(solution)/shard_map/all_to_all | solution.py:443
  32.8 0.8 %front_to_back.1 = (f32[4,16,64]{2,1,0:T(8,128)}, f32[4,16,1024]{2,1,0:T(8,128)}, f32[4,16,1024]{2,1,0:T(8,128)}) custom-call(f32[16,32,128]{2,1,0:T(8,128)S(1)} %all_to_all.5.part_ref, f32[4,16,1024]{2,1,0:T(8,128)S(1)} %get-tuple-element.42.fed_ref, f32[4,16,1024]{2,1,0:T(8,128)S(1)} %get-tuple-element.43.auto_ref), custom_call_target="tpu_custom_call" | custom-call | tf_op jit(solution)/shard_map/front_to_back/pallas_call | solution.py:445
  (1 shorter events, 0.0 us)
Async XLA Ops:
  0.6 4.1 %copy-start.3 = (f32[4,16,1024]{2,1,0:T(8,128)S(1)}, f32[4,16,1024]{2,1,0:T(8,128)}, u32[]{:S(2)}) copy-start(f32[4,16,1024]{2,1,0:T(8,128)} %refs_3_.1) | copy-start | bytes 786436
  0.6 4.1 %copy-start.2 = (f32[4,16,1024]{2,1,0:T(8,128)S(1)}, f32[4,16,1024]{2,1,0:T(8,128)}, u32[]{:S(2)}) copy-start(f32[4,16,1024]{2,1,0:T(8,128)} %refs_2_.4) | copy-start | bytes 786436
  0.7 4.1 %copy-start.1 = (f32[4,16,1024]{2,1,0:T(8,128)S(1)}, f32[4,16,1024]{2,1,0:T(8,128)}, u32[]{:S(2)}) copy-start(f32[4,16,1024]{2,1,0:T(8,128)} %refs_1_.3) | copy-start | bytes 786436
  0.7 4.1 %copy-start = (f32[4,16,1024]{2,1,0:T(8,128)S(1)}, f32[4,16,1024]{2,1,0:T(8,128)}, u32[]{:S(2)}) copy-start(f32[4,16,1024]{2,1,0:T(8,128)} %refs_0_.3) | copy-start | bytes 786436
  1.7 11.9 %collective-permute-start = (f32[2,16,1024]{2,1,0:T(8,128)S(1)}, f32[2,16,1024]{2,1,0:T(8,128)S(1)}, u32[]{:S(2)}, u32[]{:S(2)}) collective-permute-start(f32[2,16,1024]{2,1,0:T(8,128)S(1)} %get-tuple-element.34), channel_id=1, source_target_pairs={{0,2},{1,3},{2,0},{3,1},{4,6},{5,7},{6,4},{7,5},{8,10},{9,11},{10,... | collective-permute-start | bytes 393224 | tf_op jit(solution)/shard_map/ppermute | solution.py:43
  4.7 8.9 %collective-permute-start.1 = (f32[2,16,1024]{2,1,0:T(8,128)S(1)}, f32[2,16,1024]{2,1,0:T(8,128)S(1)}, u32[]{:S(2)}, u32[]{:S(2)}) collective-permute-start(f32[2,16,1024]{2,1,0:T(8,128)S(1)} %get-tuple-element.25._), channel_id=1, source_target_pairs={{0,1},{1,0},{2,4},{3,5},{4,2},{5,3},{6,8},{7,9},{8,6},{9,7},{10,12... | collective-permute-start | bytes 393224 | tf_op jit(solution)/shard_map/ppermute | solution.py:43
  5.3 12.2 %collective-permute-start.2 = (f32[2,16,1024]{2,1,0:T(8,128)S(1)}, f32[2,16,1024]{2,1,0:T(8,128)S(1)}, u32[]{:S(2)}, u32[]{:S(2)}) collective-permute-start(f32[2,16,1024]{2,1,0:T(8,128)S(1)} %get-tuple-element.39), channel_id=1, source_target_pairs={{0,2},{1,3},{2,0},{3,1},{4,6},{5,7},{6,4},{7,5},{8,10},{9,11},{10,... | collective-permute-start | bytes 393224 | tf_op jit(solution)/shard_map/ppermute | solution.py:43
  10.2 3.5 %copy-start.4 = (f32[4,16,1024]{2,1,0:T(8,128)S(1)}, f32[4,16,1024]{2,1,0:T(8,128)}, u32[]{:S(2)}) copy-start(f32[4,16,1024]{2,1,0:T(8,128)} %refs_2_.5) | copy-start | bytes 786436
  10.5 6.9 %collective-permute-start.3 = (f32[2,16,1024]{2,1,0:T(8,128)S(1)}, f32[2,16,1024]{2,1,0:T(8,128)S(1)}, u32[]{:S(2)}, u32[]{:S(2)}) collective-permute-start(f32[2,16,1024]{2,1,0:T(8,128)S(1)} %get-tuple-element.40), channel_id=1, source_target_pairs={{0,1},{1,0},{2,4},{3,5},{4,2},{5,3},{6,8},{7,9},{8,6},{9,7},{10,12... | collective-permute-start | bytes 393224 | tf_op jit(solution)/shard_map/ppermute | solution.py:43
  10.8 6.7 %collective-permute-start.4 = (f32[4,1024]{1,0:T(4,128)S(1)}, f32[4,1024]{1,0:T(4,128)S(1)}, u32[]{:S(2)}, u32[]{:S(2)}) collective-permute-start(f32[4,1024]{1,0:T(4,128)S(1)} %corner_rows.1), channel_id=1, source_target_pairs={{0,2},{1,3},{2,0},{3,1},{4,6},{5,7},{6,4},{7,5},{8,10},{9,11},{10,... | collective-permute-start | bytes 49160 | tf_op jit(solution)/shard_map/ppermute | solution.py:43
  13.7 0.7 %copy-start.5 = (f32[3,3]{1,0:T(4,128)S(1)}, f32[3,3]{1,0:T(4,128)}, u32[]{:S(2)}) copy-start(f32[3,3]{1,0:T(4,128)} %refs_5_.1) | copy-start | bytes 112

commit v10 on v8

--- a/solution.py
+++ b/solution.py
@@ -89,13 +89,16 @@
 
 def old_kernel(s_hbm, c_hbm, *refs):
     b_ref, a_ref, arrived = refs[-3:]
-    depth = s_hbm.shape[0]
+    depth, rows, _ = s_hbm.shape
+    cuts = 2 if rows % (2 * SUBLANES) == 0 else 1
     even = is_even("depth")
     copies = []
     for n, (out, towards_next) in enumerate(((a_ref, even), (b_ref, jnp.logical_not(even)))):
         layer = jnp.where(towards_next, depth - 1, 0)
         for i, hbm in enumerate((s_hbm, c_hbm)):
-            copies.append(pltpu.make_async_copy(hbm.at[layer], out.at[i], arrived.at[n, i]))
+            for k in range(cuts):
+                part = pl.ds(k * (rows // cuts), rows // cuts)
+                copies.append(pltpu.make_async_copy(hbm.at[layer, part], out.at[i, part], arrived.at[n, cuts * i + k]))
     for copy in copies:
         copy.start()
     for copy in copies:
@@ -378,7 +381,7 @@
         out_shape=(pair, pair),
         in_specs=[HBM] * 5,
         out_specs=(VMEM,) * 2,
-        scratch_shapes=[pltpu.SemaphoreType.DMA((2, 2))],
+        scratch_shapes=[pltpu.SemaphoreType.DMA((2, 4))],
         cost_estimate=WORK,
         compiler_params=PARAMS,
         name="old_layers",

time: 33.9 us -> 33.9 us (level)
  no operation moved by 1% of the time
where the time goes in v10:
time: 33.9 us; the launch traced here: 33.6 us
  blocking collectives  16.8 us (50%)
  starting transfers between devices  9.13 us (27%)
  Pallas kernels  4.23 us (12%)
  waiting for transfers between devices  2.03 us (6%)
  between operations  0.72 us (2%)
  local copies, waits for them, and re-layouts  0.69 us (2%)
    all_to_all x1, blocking collectives, body(): part = lax.all_to_all(part, 'depth', 0, 0)  15 us
    ppermute x5, starting transfers between devices, paired(): return lax.ppermute(value, ('depth', 'rows'), pairs)  9.13 us
    ppermute x5, waiting for transfers between devices, paired(): return lax.ppermute(value, ('depth', 'rows'), pairs)  2.03 us
    all_gather x1, blocking collectives, body(): beside = [lax.all_gather(value, 'rows') for value in outs[3:]]  1.89 us
    pallas_call x1, Pallas kernels, body(): pl.pallas_call(second_kernel, out_shape=(whole, whole, f32((5, rows, colu...  1.1 us
    pallas_call x1, Pallas kernels, body(): pl.pallas_call(old_kernel, out_shape=(pair, pair), in_specs=[HBM] * 5, ou...  1.03 us
    pallas_call x1, Pallas kernels, body(): pl.pallas_call(functools.partial(last_kernel, group or 1), out_shape=(ima...  0.82 us
    unnamed x12, local copies, waits for them, and re-layouts  0.69 us
  transfers between devices with their start and end apart: 5, of which 1 were waited for; matrix products, arithmetic and copies ran while one was open for 0% of the time, Pallas kernels for 6%

profile of v10, /device:TPU:0, one launch (start us, length us, event | category | flops | bytes accessed | tf_op | source)
XLA Modules:
  0.0 33.6 jit_solution(10442813384150339722)
XLA Ops:
  0.6 0.0 copy-start.3
  0.6 0.0 copy-start.2
  0.7 0.0 copy-start.1
  0.7 0.0 copy-start
  0.7 1.0 %old_layers.1 = (f32[2,16,1024]{2,1,0:T(8,128)S(1)}, f32[2,16,1024]{2,1,0:T(8,128)S(1)}) custom-call(f32[4,16,1024]{2,1,0:T(8,128)} %refs_0_.3, f32[4,16,1024]{2,1,0:T(8,128)} %refs_1_.3, f32[4,16,1024]{2,1,0:T(8,128)} %refs_2_.4, f32[4,16,1024]{2,1,0:T(8,128)} %refs_3_.1, f32[4,16,1024]{2,1,0:T(8,128)} %refs_2_.5), custom_call_target="tpu_custom_call" | custom-call | flops 20000000 | bytes 4000000 | tf_op jit(solution)/shard_map/old_layers/pallas_call | solution.py:379
  1.7 3.0 %collective-permute-start = (f32[2,16,1024]{2,1,0:T(8,128)S(1)}, f32[2,16,1024]{2,1,0:T(8,128)S(1)}, u32[]{:S(2)}, u32[]{:S(2)}) collective-permute-start(f32[2,16,1024]{2,1,0:T(8,128)S(1)} %get-tuple-element.34), channel_id=1, source_target_pairs={{0,2},{1,3},{2,0},{3,1},{4,6},{5,7},{6,4},{7,5},{8,10},{9,11},{10,... | collective-permute-start | bytes 393224 | tf_op jit(solution)/shard_map/ppermute | solution.py:43
  4.7 0.0 collective-permute-start.1
  4.7 0.0 copy-done.3
  4.7 0.0 copy-done.2
  4.7 0.0 copy-done.1
  4.7 0.0 copy-done
  4.7 0.5 %partial_step.1 = (f32[4,16,1024]{2,1,0:T(8,128)S(1)}, f32[4,16,1024]{2,1,0:T(8,128)S(1)}, f32[2,16,1024]{2,1,0:T(8,128)S(1)}, f32[16,1024]{1,0:T(8,128)S(1)}) custom-call(f32[4,16,1024]{2,1,0:T(8,128)S(1)} %copy-done, f32[4,16,1024]{2,1,0:T(8,128)S(1)} %copy-done.1, f32[4,16,1024]{2,1,0:T(8,128)S(1)} %copy-done.2, f32[4,16,1024]{2,1,0:T(8,128)S(1)} %copy-done.3, ...), custom_call_target="tpu_custom_call" | custom-call | tf_op jit(solution)/shard_map/partial_step/pallas_call | solution.py:392
  5.3 3.0 %collective-permute-start.2 = (f32[2,16,1024]{2,1,0:T(8,128)S(1)}, f32[2,16,1024]{2,1,0:T(8,128)S(1)}, u32[]{:S(2)}, u32[]{:S(2)}) collective-permute-start(f32[2,16,1024]{2,1,0:T(8,128)S(1)} %get-tuple-element.39), channel_id=1, source_target_pairs={{0,2},{1,3},{2,0},{3,1},{4,6},{5,7},{6,4},{7,5},{8,10},{9,11},{10,... | collective-permute-start | bytes 393224 | tf_op jit(solution)/shard_map/ppermute | solution.py:43
  8.3 1.9 %all-gather = f32[32,1024]{1,0:T(8,128)S(1)} all-gather(f32[16,1024]{1,0:T(8,128)S(1)} %get-tuple-element.28), channel_id=2, replica_groups=mesh['depth'=16,'rows'=2] {'rows'}, dimensions={0}, use_global_device_ids=true | all-gather | bytes 196608 | tf_op jit(solution)/shard_map/all_gather | solution.py:402
  10.2 0.0 copy-start.4
  10.2 0.4 %inner_cells.1 = (f32[4,16,1024]{2,1,0:T(8,128)S(1)}, f32[4,16,1024]{2,1,0:T(8,128)S(1)}, f32[4,16,1024]{2,1,0:T(8,128)S(1)}, f32[4,16,1024]{2,1,0:T(8,128)S(1)}...) custom-call(f32[4,16,1024]{2,1,0:T(8,128)S(1)} %copy-done, f32[4,16,1024]{2,1,0:T(8,128)S(1)} %copy-done.1, ...), custom_call_target="tpu_custom_call" | custom-call | tf_op jit(solution)/shard_map/inner_cells/pallas_call | solution.py:403
  10.5 0.2 collective-permute-start.3
  10.8 2.9 %collective-permute-start.4 = (f32[4,1024]{1,0:T(4,128)S(1)}, f32[4,1024]{1,0:T(4,128)S(1)}, u32[]{:S(2)}, u32[]{:S(2)}) collective-permute-start(f32[4,1024]{1,0:T(4,128)S(1)} %corner_rows.1), channel_id=1, source_target_pairs={{0,2},{1,3},{2,0},{3,1},{4,6},{5,7},{6,4},{7,5},{8,10},{9,11},{10,... | collective-permute-start | bytes 49160 | tf_op jit(solution)/shard_map/ppermute | solution.py:43
  13.6 0.0 collective-permute-done.refs_11_
  13.6 0.0 collective-permute-done.1.refs_12_
  13.6 0.0 copy-start.5
  13.7 0.0 copy-done.4
  13.7 0.7 %copy-done.5 = f32[3,3]{1,0:T(4,128)S(1)} copy-done((f32[3,3]{1,0:T(4,128)S(1)}, f32[3,3]{1,0:T(4,128)}, u32[]{:S(2)}) %copy-start.5) | copy-done | bytes 60
  14.3 1.1 %second_step.1 = (f32[4,16,1024]{2,1,0:T(8,128)S(1)}, f32[4,16,1024]{2,1,0:T(8,128)S(1)}, f32[5,16,1024]{2,1,0:T(8,128)S(1)}, f32[9,1024]{1,0:T(8,128)S(1)}) custom-call(f32[4,16,1024]{2,1,0:T(8,128)S(1)} %copy-done, f32[4,16,1024]{2,1,0:T(8,128)S(1)} %copy-done.1, f32[4,16,1024]{2,1,0:T(8,128)S(1)} %copy-done.2, f32[4,16,1024]{2,1,0:T(8,128)S(1)} %copy-done.3, ...), custom_call_target="tpu_custom_call" | custom-call | flops 20000000 | bytes 4000000 | tf_op jit(solution)/shard_map/second_step/pallas_call | solution.py:422
  15.4 2.0 %collective-permute-done.4.refs_7_ = f32[4,1024]{1,0:T(4,128)S(1)} collective-permute-done((f32[4,1024]{1,0:T(4,128)S(1)}, f32[4,1024]{1,0:T(4,128)S(1)}, u32[]{:S(2)}, u32[]{:S(2)}) %collective-permute-start.4) | collective-permute-done | bytes 16416 | tf_op jit(solution)/shard_map/ppermute | solution.py:43
  17.5 0.0 collective-permute-done.2.refs_5_
  17.5 0.0 collective-permute-done.3.refs_6_
  17.5 0.4 %shading.1 = (f32[4,16,1024]{2,1,0:T(8,128)S(1)}, f32[4,16,1024]{2,1,0:T(8,128)S(1)}, f32[16,32,128]{2,1,0:T(8,128)S(1)}) custom-call(f32[4,16,1024]{2,1,0:T(8,128)S(1)} %get-tuple-element.35.refs_0_, f32[4,16,1024]{2,1,0:T(8,128)S(1)} %get-tuple-element.36.refs_1_, f32[4,16,1024]{2,1,0:T(8,128)S(1)} %copy-done.4, f32[9,1024]{1,0:T(8,128)S(1)} %get-tuple-element.37.refs_3_, ...), custom_call_target="tpu_custom_call" | custom-call | tf_op jit(solution)/shard_map/shading/pallas_call | solution.py:435
  17.9 15.0 %all_to_all.5.part_ref = f32[16,32,128]{2,1,0:T(8,128)S(1)} all-to-all(f32[16,32,128]{2,1,0:T(8,128)S(1)} %get-tuple-element.41), channel_id=1, replica_groups=mesh['depth'=16,'rows'=2] {'depth'}, dimensions={0} | all-to-all | bytes 524288 | tf_op jit(solution)/shard_map/all_to_all | solution.py:445
  32.8 0.8 %front_to_back.1 = (f32[4,16,64]{2,1,0:T(8,128)}, f32[4,16,1024]{2,1,0:T(8,128)}, f32[4,16,1024]{2,1,0:T(8,128)}) custom-call(f32[16,32,128]{2,1,0:T(8,128)S(1)} %all_to_all.5.part_ref, f32[4,16,1024]{2,1,0:T(8,128)S(1)} %get-tuple-element.42.fed_ref, f32[4,16,1024]{2,1,0:T(8,128)S(1)} %get-tuple-element.43.auto_ref), custom_call_target="tpu_custom_call" | custom-call | tf_op jit(solution)/shard_map/front_to_back/pallas_call | solution.py:447
  (1 shorter events, 0.0 us)
Async XLA Ops:
  0.6 4.1 %copy-start.3 = (f32[4,16,1024]{2,1,0:T(8,128)S(1)}, f32[4,16,1024]{2,1,0:T(8,128)}, u32[]{:S(2)}) copy-start(f32[4,16,1024]{2,1,0:T(8,128)} %refs_3_.1) | copy-start | bytes 786436
  0.6 4.1 %copy-start.2 = (f32[4,16,1024]{2,1,0:T(8,128)S(1)}, f32[4,16,1024]{2,1,0:T(8,128)}, u32[]{:S(2)}) copy-start(f32[4,16,1024]{2,1,0:T(8,128)} %refs_2_.4) | copy-start | bytes 786436
  0.7 4.1 %copy-start.1 = (f32[4,16,1024]{2,1,0:T(8,128)S(1)}, f32[4,16,1024]{2,1,0:T(8,128)}, u32[]{:S(2)}) copy-start(f32[4,16,1024]{2,1,0:T(8,128)} %refs_1_.3) | copy-start | bytes 786436
  0.7 4.1 %copy-start = (f32[4,16,1024]{2,1,0:T(8,128)S(1)}, f32[4,16,1024]{2,1,0:T(8,128)}, u32[]{:S(2)}) copy-start(f32[4,16,1024]{2,1,0:T(8,128)} %refs_0_.3) | copy-start | bytes 786436
  1.7 11.9 %collective-permute-start = (f32[2,16,1024]{2,1,0:T(8,128)S(1)}, f32[2,16,1024]{2,1,0:T(8,128)S(1)}, u32[]{:S(2)}, u32[]{:S(2)}) collective-permute-start(f32[2,16,1024]{2,1,0:T(8,128)S(1)} %get-tuple-element.34), channel_id=1, source_target_pairs={{0,2},{1,3},{2,0},{3,1},{4,6},{5,7},{6,4},{7,5},{8,10},{9,11},{10,... | collective-permute-start | bytes 393224 | tf_op jit(solution)/shard_map/ppermute | solution.py:43
  4.7 8.9 %collective-permute-start.1 = (f32[2,16,1024]{2,1,0:T(8,128)S(1)}, f32[2,16,1024]{2,1,0:T(8,128)S(1)}, u32[]{:S(2)}, u32[]{:S(2)}) collective-permute-start(f32[2,16,1024]{2,1,0:T(8,128)S(1)} %get-tuple-element.25._), channel_id=1, source_target_pairs={{0,1},{1,0},{2,4},{3,5},{4,2},{5,3},{6,8},{7,9},{8,6},{9,7},{10,12... | collective-permute-start | bytes 393224 | tf_op jit(solution)/shard_map/ppermute | solution.py:43
  5.3 12.2 %collective-permute-start.2 = (f32[2,16,1024]{2,1,0:T(8,128)S(1)}, f32[2,16,1024]{2,1,0:T(8,128)S(1)}, u32[]{:S(2)}, u32[]{:S(2)}) collective-permute-start(f32[2,16,1024]{2,1,0:T(8,128)S(1)} %get-tuple-element.39), channel_id=1, source_target_pairs={{0,2},{1,3},{2,0},{3,1},{4,6},{5,7},{6,4},{7,5},{8,10},{9,11},{10,... | collective-permute-start | bytes 393224 | tf_op jit(solution)/shard_map/ppermute | solution.py:43
  10.2 3.5 %copy-start.4 = (f32[4,16,1024]{2,1,0:T(8,128)S(1)}, f32[4,16,1024]{2,1,0:T(8,128)}, u32[]{:S(2)}) copy-start(f32[4,16,1024]{2,1,0:T(8,128)} %refs_2_.5) | copy-start | bytes 786436
  10.5 6.9 %collective-permute-start.3 = (f32[2,16,1024]{2,1,0:T(8,128)S(1)}, f32[2,16,1024]{2,1,0:T(8,128)S(1)}, u32[]{:S(2)}, u32[]{:S(2)}) collective-permute-start(f32[2,16,1024]{2,1,0:T(8,128)S(1)} %get-tuple-element.40), channel_id=1, source_target_pairs={{0,1},{1,0},{2,4},{3,5},{4,2},{5,3},{6,8},{7,9},{8,6},{9,7},{10,12... | collective-permute-start | bytes 393224 | tf_op jit(solution)/shard_map/ppermute | solution.py:43
  10.8 6.7 %collective-permute-start.4 = (f32[4,1024]{1,0:T(4,128)S(1)}, f32[4,1024]{1,0:T(4,128)S(1)}, u32[]{:S(2)}, u32[]{:S(2)}) collective-permute-start(f32[4,1024]{1,0:T(4,128)S(1)} %corner_rows.1), channel_id=1, source_target_pairs={{0,2},{1,3},{2,0},{3,1},{4,6},{5,7},{6,4},{7,5},{8,10},{9,11},{10,... | collective-permute-start | bytes 49160 | tf_op jit(solution)/shard_map/ppermute | solution.py:43
  13.6 0.7 %copy-start.5 = (f32[3,3]{1,0:T(4,128)S(1)}, f32[3,3]{1,0:T(4,128)}, u32[]{:S(2)}) copy-start(f32[3,3]{1,0:T(4,128)} %refs_5_.1) | copy-start | bytes 112
